TPU v7x, 32 devices: a whole 2x2x4 slice. The times are simulated.
32 devices in a mesh: query: 4 (over y, x), corpus: 8 (over z, core).
Axes of the slice: x: 2, y: 2, z: 4, core: 2. Of those that a mesh axis runs over, the one named last changes fastest.
Arguments:
- queries: float32 [1536, 768], P('query'), may hold values from -20 to 20
- codes: int32 [8192, 96], P('corpus'), may hold values from 0 to 255
- positive: int32 [1536], P('query'), may hold values from 0 to 8191
- codebook: float32 [256, 768], replicated, may hold values from -0.6 to 0.6
Outputs:
- grad_queries: float32 [1536, 768], P('query')
- grad_codebook: float32 [256, 768], replicated
- loss: float32 [1536], P('query')
All inputs are finite; a program needn't handle non-finite values.
Results may differ from a plain program's by a relative error of at most 0.0003.
Values sent between devices are 32-bit elements; how exact they have to be, the bound alone decides.
No kernel may reach another device: no remote copies, remote signals or barrier semaphores. Data moves between devices by JAX's collectives and lax.ppermute only.
A program may use at most 64 MiB of HBM per device.

v0:
```python
import jax
import jax.numpy as jnp
from jax import lax
from jax.sharding import PartitionSpec as P

precise = lax.Precision.HIGHEST


def one_hot_block(codes, first, count, words):
    picked = lax.slice_in_dim(codes, first, first + count, axis=1)
    return (picked[:, :, None] == jnp.arange(words, dtype=jnp.int32)[None, None, :]).astype(
        jnp.float32
    )


def local(queries, codes, positive, codebook):
    doc_rows = codes.shape[0]
    subspaces = codes.shape[1]
    words = codebook.shape[0]
    width = codebook.shape[1]
    sub_width = width // subspaces
    group = 8
    book_split = codebook.reshape(words, subspaces, sub_width)
    pieces = []
    for first in range(0, subspaces, group):
        table = one_hot_block(codes, first, group, words)
        book_part = lax.slice_in_dim(book_split, first, first + group, axis=1)
        pieces.append(
            jnp.einsum(
                "jmk,kmc->jmc",
                table,
                book_part,
                precision=precise,
                preferred_element_type=jnp.float32,
            )
        )
    rebuilt = jnp.concatenate(pieces, axis=1).reshape(doc_rows, width)
    scores = lax.dot_general(
        queries,
        rebuilt,
        (((1,), (1,)), ((), ())),
        precision=precise,
        preferred_element_type=jnp.float32,
    )
    doc_start = lax.axis_index("corpus") * doc_rows
    doc_ids = doc_start + jnp.arange(doc_rows, dtype=jnp.int32)
    positive_hits = (positive[:, None] == doc_ids[None, :]).astype(jnp.float32)
    own_score = jnp.sum(scores * positive_hits, axis=1)
    local_top = jnp.max(scores, axis=1)
    row_top = lax.pmax(local_top, "corpus")
    row_total, pos_score = lax.psum(
        (jnp.sum(jnp.exp(scores - row_top[:, None]), axis=1), own_score), "corpus"
    )
    log_total = row_top + jnp.log(row_total)
    loss = log_total - pos_score
    weights = jnp.exp(scores - log_total[:, None]) - positive_hits
    query_terms = jnp.dot(weights, rebuilt, precision=precise, preferred_element_type=jnp.float32)
    grad_queries = lax.psum(query_terms, "corpus")
    doc_grad = lax.dot_general(
        weights,
        queries,
        (((0,), (0,)), ((), ())),
        precision=precise,
        preferred_element_type=jnp.float32,
    )
    grad_split = doc_grad.reshape(doc_rows, subspaces, sub_width)
    book_pieces = []
    for first in range(0, subspaces, group):
        table = one_hot_block(codes, first, group, words)
        grad_part = lax.slice_in_dim(grad_split, first, first + group, axis=1)
        book_pieces.append(
            jnp.einsum(
                "jmk,jmc->kmc",
                table,
                grad_part,
                precision=precise,
                preferred_element_type=jnp.float32,
            )
        )
    local_codebook = jnp.concatenate(book_pieces, axis=1).reshape(words, width)
    codebook_part = lax.psum_scatter(local_codebook, "corpus", scatter_dimension=0, tiled=True)
    codebook_part = lax.psum(codebook_part, "query")
    grad_codebook = lax.all_gather(codebook_part, "corpus", axis=0, tiled=True)
    return (grad_queries, grad_codebook, loss)


def solution(mesh):
    placed = (P("query", None), P("corpus", None), P("query"), P())
    return jax.shard_map(
        local,
        mesh=mesh,
        in_specs=placed,
        out_specs=(P("query", None), P(), P("query")),
        check_vma=False,
    )
```

profile of v0, /device:TPU:0, one launch (start us, length us, event | category | flops | bytes accessed | tf_op | source)
XLA Modules:
  0.0 301.9 jit_solution(3842349768565503291)
XLA Ops:
  7.2 0.0 copy-start
  7.2 0.0 reduce-scatter.2.cloned.1.call-start
  7.2 1.0 fusion.187
  8.3 0.0 copy-start.22
  8.3 0.0 copy-start.24
  8.3 0.0 copy-start.20
  8.3 0.0 copy-start.18
  8.3 0.0 copy-start.16
  8.3 0.0 copy-start.14
  8.3 0.0 copy-start.12
  8.4 0.0 copy-start.10
  8.4 0.0 copy-start.8
  8.4 0.0 copy-start.6
  8.4 0.0 copy-start.4
  8.4 0.0 copy-start.2
  8.4 1.4 copy.7
  9.9 5.0 %fusion.73 = f32[1024,96,8]{0,2,1:T(8,128)S(1)} fusion(s32[1024,8]{0,1:T(8,128)S(1)} %get-tuple-element.19, f32[256,96,8]{0,2,1:T(8,128)S(1)} %bitcast.194), kind=kOutput, calls=%fused_computation.87 | convolution fusion | flops 203423744 | bytes 360448 | tf_op jit(solution)/shard_map/jmk,kmc->jmc/dot_general | solution.py:29
  14.9 5.0 %fusion.75 = f32[1024,96,8]{0,2,1:T(8,128)S(1)} fusion(f32[1024,96,8]{0,2,1:T(8,128)S(1)} %fusion.73, s32[1024,8]{0,1:T(8,128)S(1)} %get-tuple-element.18, f32[256,96,8]{0,2,1:T(8,128)S(1)} %bitcast.195), kind=kOutput, calls=%fused_computation.89 | convolution fusion | flops 203423744 | bytes 360448 | tf_op jit(solution)/shard_map/jmk,kmc->jmc/dot_general | solution.py:29
  19.9 0.0 copy-done.24
  19.9 0.0 copy-done.20
  19.9 5.0 %fusion.77 = f32[1024,96,8]{0,2,1:T(8,128)S(1)} fusion(f32[1024,96,8]{0,2,1:T(8,128)S(1)} %fusion.75, s32[1024,8]{0,1:T(8,128)S(1)} %get-tuple-element.17, f32[256,96,8]{0,2,1:T(8,128)S(1)} %bitcast.196), kind=kOutput, calls=%fused_computation.91 | convolution fusion | flops 203423744 | bytes 360448 | tf_op jit(solution)/shard_map/jmk,kmc->jmc/dot_general | solution.py:29
  25.0 5.0 %fusion.79 = f32[1024,96,8]{0,2,1:T(8,128)S(1)} fusion(f32[1024,96,8]{0,2,1:T(8,128)S(1)} %fusion.77, s32[1024,8]{0,1:T(8,128)S(1)} %get-tuple-element.16, f32[256,96,8]{0,2,1:T(8,128)S(1)} %bitcast.197), kind=kOutput, calls=%fused_computation.93 | convolution fusion | flops 203423744 | bytes 360448 | tf_op jit(solution)/shard_map/jmk,kmc->jmc/dot_general | solution.py:29
  30.0 5.0 %fusion.81 = f32[1024,96,8]{0,2,1:T(8,128)S(1)} fusion(f32[1024,96,8]{0,2,1:T(8,128)S(1)} %fusion.79, s32[1024,8]{0,1:T(8,128)S(1)} %get-tuple-element.15, f32[256,96,8]{0,2,1:T(8,128)S(1)} %bitcast.198), kind=kOutput, calls=%fused_computation.95 | convolution fusion | flops 203423744 | bytes 360448 | tf_op jit(solution)/shard_map/jmk,kmc->jmc/dot_general | solution.py:29
  35.0 5.0 %fusion.83 = f32[1024,96,8]{0,2,1:T(8,128)S(1)} fusion(f32[1024,96,8]{0,2,1:T(8,128)S(1)} %fusion.81, s32[1024,8]{0,1:T(8,128)S(1)} %get-tuple-element.14, f32[256,96,8]{0,2,1:T(8,128)S(1)} %bitcast.199), kind=kOutput, calls=%fused_computation.97 | convolution fusion | flops 203423744 | bytes 360448 | tf_op jit(solution)/shard_map/jmk,kmc->jmc/dot_general | solution.py:29
  40.0 5.0 %fusion.85 = f32[1024,96,8]{0,2,1:T(8,128)S(1)} fusion(f32[1024,96,8]{0,2,1:T(8,128)S(1)} %fusion.83, s32[1024,8]{0,1:T(8,128)S(1)} %get-tuple-element.13, f32[256,96,8]{0,2,1:T(8,128)S(1)} %bitcast.200), kind=kOutput, calls=%fused_computation.99 | convolution fusion | flops 203423744 | bytes 360448 | tf_op jit(solution)/shard_map/jmk,kmc->jmc/dot_general | solution.py:29
  45.0 5.0 %fusion.87 = f32[1024,96,8]{0,2,1:T(8,128)S(1)} fusion(f32[1024,96,8]{0,2,1:T(8,128)S(1)} %fusion.85, s32[1024,8]{0,1:T(8,128)S(1)} %get-tuple-element.12, f32[256,96,8]{0,2,1:T(8,128)S(1)} %bitcast.201), kind=kOutput, calls=%fused_computation.101 | convolution fusion | flops 203423744 | bytes 360448 | tf_op jit(solution)/shard_map/jmk,kmc->jmc/dot_general | solution.py:29
  50.1 5.0 %fusion.89 = f32[1024,96,8]{0,2,1:T(8,128)S(1)} fusion(f32[1024,96,8]{0,2,1:T(8,128)S(1)} %fusion.87, s32[1024,8]{0,1:T(8,128)S(1)} %get-tuple-element.11, f32[256,96,8]{0,2,1:T(8,128)S(1)} %bitcast.202), kind=kOutput, calls=%fused_computation.103 | convolution fusion | flops 203423744 | bytes 360448 | tf_op jit(solution)/shard_map/jmk,kmc->jmc/dot_general | solution.py:29
  55.1 5.0 %fusion.91 = f32[1024,96,8]{0,2,1:T(8,128)S(1)} fusion(f32[1024,96,8]{0,2,1:T(8,128)S(1)} %fusion.89, s32[1024,8]{0,1:T(8,128)S(1)} %get-tuple-element.10, f32[256,96,8]{0,2,1:T(8,128)S(1)} %bitcast.203), kind=kOutput, calls=%fused_computation.105 | convolution fusion | flops 203423744 | bytes 360448 | tf_op jit(solution)/shard_map/jmk,kmc->jmc/dot_general | solution.py:29
  60.1 0.0 copy-done.4
  60.1 5.0 %fusion.93 = f32[1024,96,8]{0,2,1:T(8,128)S(1)} fusion(f32[1024,96,8]{0,2,1:T(8,128)S(1)} %fusion.91, s32[1024,8]{0,1:T(8,128)S(1)} %get-tuple-element.20, f32[256,96,8]{0,2,1:T(8,128)S(1)} %bitcast.204), kind=kOutput, calls=%fused_computation.107 | convolution fusion | flops 203423744 | bytes 360448 | tf_op jit(solution)/shard_map/jmk,kmc->jmc/dot_general | solution.py:29
  65.1 0.0 copy-done.2
  65.1 5.5 %fusion.95 = f32[1024,96,8]{0,2,1:T(8,128)S(1)} fusion(f32[1024,96,8]{0,2,1:T(8,128)S(1)} %fusion.93, s32[1024,8]{0,1:T(8,128)S(1)} %get-tuple-element.9, f32[256,96,8]{0,2,1:T(8,128)S(1)} %bitcast.205), kind=kOutput, calls=%fused_computation.109 | convolution fusion | flops 203423744 | bytes 360448 | tf_op jit(solution)/shard_map/jmk,kmc->jmc/dot_general | solution.py:29
  70.7 1.6 copy-done.1
  72.3 9.9 %fusion.188 = (f32[384]{0:T(512)S(1)}, f32[1024,384]{1,0:T(8,128)S(1)}) fusion(f32[384,768]{1,0:T(8,128)S(1)} %copy-done, f32[1024,96,8]{0,2,1:T(8,128)S(1)} %fusion.95), kind=kOutput, calls=%fused_computation.156 | convolution fusion | flops 3624271360 | bytes 5899776 | tf_op jit(solution)/shard_map/dot_general | solution.py:38
  82.3 18.1 %pmax.7 = f32[384]{0:T(512)S(1)} all-reduce(f32[384]{0:T(512)S(1)} %get-tuple-element.21), channel_id=1, replica_groups=mesh['query'=4,'corpus'=8] {'corpus'}, use_global_device_ids=true, to_apply=%region_1.0 | all-reduce | flops 384 | bytes 3072 | tf_op jit(solution)/shard_map/pmax | solution.py:50
  100.3 0.4 fusion.65
  100.7 13.7 %all-reduce = (f32[384]{0:T(512)S(1)}, f32[384]{0:T(512)S(1)}) all-reduce(f32[384]{0:T(512)S(1)} %get-tuple-element.4, f32[384]{0:T(512)S(1)} %get-tuple-element.3), channel_id=1, replica_groups=mesh['query'=4,'corpus'=8] {'corpus'}, use_global_device_ids=true, to_apply=%region_3.0 | all-reduce | flops 768 | bytes 6144 | tf_op jit(solution)/shard_map/psum | solution.py:51
  114.5 0.6 fusion.186
  115.1 5.7 %fusion.69 = f32[1024,768]{0,1:T(8,128)S(1)} fusion(f32[384,768]{1,0:T(8,128)S(1)} %copy-done, f32[1024,384]{1,0:T(8,128)S(1)} %get-tuple-element.22, s32[384]{0:T(512)S(1)} %copy-done.25, f32[384]{0:T(512)S(1)} %get-tuple-element.8, s32[1024]{0:T(1024)S(1)} %iota_add_fusion), kind=kOutput, calls=%fused_computation.85 | convolution fusion | flops 3625451520 | bytes 5905408 | tf_op jit(solution)/shard_map/dot_general | solution.py:59
  120.8 3.4 %fusion.99 = f32[256,96,8]{0,2,1:T(8,128)S(1)} fusion(s32[1024,8]{0,1:T(8,128)} %copy-done.24, f32[1024,768]{0,1:T(8,128)S(1)} %fusion.69), kind=kOutput, calls=%fused_computation.111 | convolution fusion | flops 203423744 | bytes 3244032 | tf_op jit(solution)/shard_map/jmk,jmc->kmc/dot_general | solution.py:72
  124.2 2.6 fusion.105
  126.9 2.8 fusion.111
  129.7 2.6 fusion.117
  132.4 2.6 fusion.123
  135.0 2.6 fusion.129
  137.7 2.6 fusion.135
  140.3 2.6 fusion.141
  143.0 3.0 %fusion.147 = f32[256,96,8]{0,2,1:T(8,128)S(1)} fusion(f32[256,96,8]{0,2,1:T(8,128)S(1)} %fusion.141, s32[1024,8]{0,1:T(8,128)S(1)} %copy-done.9, f32[1024,768]{0,1:T(8,128)S(1)} %fusion.69), kind=kOutput, calls=%fused_computation.127 | convolution fusion | flops 203423744 | bytes 3244032 | tf_op jit(solution)/shard_map/jmk,jmc->kmc/dot_general | solution.py:72
  146.0 2.6 fusion.153
  148.7 2.6 fusion.159
  151.3 2.6 fusion.165
  154.0 1.2 copy.8
  155.1 0.0 reduce-scatter.2.cloned.1.call-update
  155.2 0.0 all-reduce.6.cloned.1.call-start
  155.2 29.9 %reduce-scatter.2.cloned.1.call-done = f32[32,768]{1,0:T(8,128)} async-done(((f32[256,768]{1,0:T(8,128)}), f32[32,768]{1,0:T(8,128)}) %reduce-scatter.2.cloned.1.call-update) | async-done | bytes 98320 | tf_op jit(solution)/shard_map/reduce_scatter | solution.py:81
  185.1 0.0 all-reduce.6.cloned.1.call-update
  185.2 0.2 all-reduce.4.cloned.1.call-start
  185.4 10.7 %fusion.60 = f32[384,768]{1,0:T(8,128)} fusion(f32[1024,96,8]{0,2,1:T(8,128)} %copy-done.1, f32[1024,384]{1,0:T(8,128)S(1)} %get-tuple-element.22, s32[384]{0:T(512)S(1)} %copy-done.25, f32[384]{0:T(512)S(1)} %get-tuple-element.8, s32[1024]{0:T(1024)S(1)} %iota_add_fusion), kind=kOutput, calls=%fused_computation.72 | convolution fusion | flops 3625451520 | bytes 5905408 | tf_op jit(solution)/shard_map/dot_general | solution.py:57
  196.0 0.0 all-reduce.4.cloned.1.call-update
  196.1 32.3 %all-reduce.6.cloned.1.call-done = f32[32,768]{1,0:T(8,128)} async-done(((f32[32,768]{1,0:T(8,128)}), f32[32,768]{1,0:T(8,128)}) %all-reduce.6.cloned.1.call-update) | async-done | bytes 98320 | tf_op jit(solution)/shard_map/psum | solution.py:82
  228.4 18.2 %all_gather.3 = f32[256,768]{1,0:T(8,128)S(1)} all-gather(f32[32,768]{1,0:T(8,128)} %all-reduce.6.cloned.1.call-done), channel_id=1, replica_groups=mesh['query'=4,'corpus'=8] {'corpus'}, dimensions={0}, use_global_device_ids=true | all-gather | bytes 884736 | tf_op jit(solution)/shard_map/all_gather | solution.py:83
  246.6 45.4 %all-reduce.4.cloned.1.call-done = f32[384,768]{1,0:T(8,128)} async-done(((f32[384,768]{1,0:T(8,128)}), f32[384,768]{1,0:T(8,128)}) %all-reduce.4.cloned.1.call-update) | async-done | bytes 1179664 | tf_op jit(solution)/shard_map/psum | solution.py:58
  291.9 2.4 copy.34
  294.3 0.9 copy.35
  (35 shorter events, 0.1 us)
Async XLA Ops:
  7.2 65.2 %copy-start = (f32[384,768]{1,0:T(8,128)S(1)}, f32[384,768]{1,0:T(8,128)}, u32[]{:S(2)}) copy-start(f32[384,768]{1,0:T(8,128)} %param.4) | copy-start | bytes 3538948
  7.2 178.0 %reduce-scatter.2.cloned.1.call-start = ((), (), s32[]{:S(2)}) async-start(), calls=%async_computation.2 | async-start | bytes 884736 | tf_op jit(solution)/shard_map/reduce_scatter | solution.py:81
  8.3 11.6 %copy-start.22 = (s32[1024,8]{0,1:T(8,128)}, s32[1024,8]{0,1:T(8,128)S(1)}, u32[]{:S(2)}) copy-start(s32[1024,8]{0,1:T(8,128)S(1)} %get-tuple-element.18) | copy-start | bytes 98308
  8.3 11.6 %copy-start.24 = (s32[1024,8]{0,1:T(8,128)}, s32[1024,8]{0,1:T(8,128)S(1)}, u32[]{:S(2)}) copy-start(s32[1024,8]{0,1:T(8,128)S(1)} %get-tuple-element.19) | copy-start | bytes 98308
  8.3 11.6 %copy-start.20 = (s32[1024,8]{0,1:T(8,128)}, s32[1024,8]{0,1:T(8,128)S(1)}, u32[]{:S(2)}) copy-start(s32[1024,8]{0,1:T(8,128)S(1)} %get-tuple-element.17) | copy-start | bytes 98308
  8.3 16.6 %copy-start.18 = (s32[1024,8]{0,1:T(8,128)}, s32[1024,8]{0,1:T(8,128)S(1)}, u32[]{:S(2)}) copy-start(s32[1024,8]{0,1:T(8,128)S(1)} %get-tuple-element.16) | copy-start | bytes 98308
  8.3 21.6 %copy-start.16 = (s32[1024,8]{0,1:T(8,128)}, s32[1024,8]{0,1:T(8,128)S(1)}, u32[]{:S(2)}) copy-start(s32[1024,8]{0,1:T(8,128)S(1)} %get-tuple-element.15) | copy-start | bytes 98308
  8.3 26.7 %copy-start.14 = (s32[1024,8]{0,1:T(8,128)}, s32[1024,8]{0,1:T(8,128)S(1)}, u32[]{:S(2)}) copy-start(s32[1024,8]{0,1:T(8,128)S(1)} %get-tuple-element.14) | copy-start | bytes 98308
  8.3 31.7 %copy-start.12 = (s32[1024,8]{0,1:T(8,128)}, s32[1024,8]{0,1:T(8,128)S(1)}, u32[]{:S(2)}) copy-start(s32[1024,8]{0,1:T(8,128)S(1)} %get-tuple-element.13) | copy-start | bytes 98308
  8.4 36.7 %copy-start.10 = (s32[1024,8]{0,1:T(8,128)}, s32[1024,8]{0,1:T(8,128)S(1)}, u32[]{:S(2)}) copy-start(s32[1024,8]{0,1:T(8,128)S(1)} %get-tuple-element.12) | copy-start | bytes 98308
  8.4 41.7 %copy-start.8 = (s32[1024,8]{0,1:T(8,128)}, s32[1024,8]{0,1:T(8,128)S(1)}, u32[]{:S(2)}) copy-start(s32[1024,8]{0,1:T(8,128)S(1)} %get-tuple-element.11) | copy-start | bytes 98308
  8.4 46.7 %copy-start.6 = (s32[1024,8]{0,1:T(8,128)}, s32[1024,8]{0,1:T(8,128)S(1)}, u32[]{:S(2)}) copy-start(s32[1024,8]{0,1:T(8,128)S(1)} %get-tuple-element.10) | copy-start | bytes 98308
  8.4 51.7 %copy-start.4 = (s32[1024,8]{0,1:T(8,128)}, s32[1024,8]{0,1:T(8,128)S(1)}, u32[]{:S(2)}) copy-start(s32[1024,8]{0,1:T(8,128)S(1)} %get-tuple-element.20) | copy-start | bytes 98308
  8.4 56.7 %copy-start.2 = (s32[1024,8]{0,1:T(8,128)}, s32[1024,8]{0,1:T(8,128)S(1)}, u32[]{:S(2)}) copy-start(s32[1024,8]{0,1:T(8,128)S(1)} %get-tuple-element.9) | copy-start | bytes 98308
  70.7 1.7 copy-start.1
  72.3 28.0 %copy-start.25 = (s32[384]{0:T(512)S(1)}, s32[384]{0:T(512)}, u32[]{:S(2)}) copy-start(s32[384]{0:T(512)} %param.6) | copy-start | bytes 4612
  115.1 9.1 %copy-start.23 = (s32[1024,8]{0,1:T(8,128)S(1)}, s32[1024,8]{0,1:T(8,128)}, u32[]{:S(2)}) copy-start(s32[1024,8]{0,1:T(8,128)} %copy-done.22) | copy-start | bytes 98308
  120.8 6.1 %copy-start.21 = (s32[1024,8]{0,1:T(8,128)S(1)}, s32[1024,8]{0,1:T(8,128)}, u32[]{:S(2)}) copy-start(s32[1024,8]{0,1:T(8,128)} %copy-done.20) | copy-start | bytes 98308
  124.2 5.5 %copy-start.19 = (s32[1024,8]{0,1:T(8,128)S(1)}, s32[1024,8]{0,1:T(8,128)}, u32[]{:S(2)}) copy-start(s32[1024,8]{0,1:T(8,128)} %copy-done.18) | copy-start | bytes 98308
  126.9 5.5 %copy-start.17 = (s32[1024,8]{0,1:T(8,128)S(1)}, s32[1024,8]{0,1:T(8,128)}, u32[]{:S(2)}) copy-start(s32[1024,8]{0,1:T(8,128)} %copy-done.16) | copy-start | bytes 98308
  129.7 5.3 %copy-start.15 = (s32[1024,8]{0,1:T(8,128)S(1)}, s32[1024,8]{0,1:T(8,128)}, u32[]{:S(2)}) copy-start(s32[1024,8]{0,1:T(8,128)} %copy-done.14) | copy-start | bytes 98308
  132.4 5.3 %copy-start.13 = (s32[1024,8]{0,1:T(8,128)S(1)}, s32[1024,8]{0,1:T(8,128)}, u32[]{:S(2)}) copy-start(s32[1024,8]{0,1:T(8,128)} %copy-done.12) | copy-start | bytes 98308
  135.0 5.3 %copy-start.11 = (s32[1024,8]{0,1:T(8,128)S(1)}, s32[1024,8]{0,1:T(8,128)}, u32[]{:S(2)}) copy-start(s32[1024,8]{0,1:T(8,128)} %copy-done.10) | copy-start | bytes 98308
  137.7 5.3 %copy-start.9 = (s32[1024,8]{0,1:T(8,128)S(1)}, s32[1024,8]{0,1:T(8,128)}, u32[]{:S(2)}) copy-start(s32[1024,8]{0,1:T(8,128)} %copy-done.8) | copy-start | bytes 98308
  140.3 5.7 %copy-start.7 = (s32[1024,8]{0,1:T(8,128)S(1)}, s32[1024,8]{0,1:T(8,128)}, u32[]{:S(2)}) copy-start(s32[1024,8]{0,1:T(8,128)} %copy-done.6) | copy-start | bytes 98308
  143.0 5.7 %copy-start.5 = (s32[1024,8]{0,1:T(8,128)S(1)}, s32[1024,8]{0,1:T(8,128)}, u32[]{:S(2)}) copy-start(s32[1024,8]{0,1:T(8,128)} %copy-done.4) | copy-start | bytes 98308
  146.0 5.3 %copy-start.3 = (s32[1024,8]{0,1:T(8,128)S(1)}, s32[1024,8]{0,1:T(8,128)}, u32[]{:S(2)}) copy-start(s32[1024,8]{0,1:T(8,128)} %copy-done.2) | copy-start | bytes 98308
  155.2 73.3 %all-reduce.6.cloned.1.call-start = ((), (), s32[]{:S(2)}) async-start(), calls=%async_computation.3 | async-start | bytes 196608 | tf_op jit(solution)/shard_map/psum | solution.py:82
  185.2 106.8 %all-reduce.4.cloned.1.call-start = ((), (), s32[]{:S(2)}) async-start(), calls=%async_computation.1 | async-start | bytes 2359296 | tf_op jit(solution)/shard_map/psum | solution.py:58
Sparse Core Ops, SparseCore 0:
  155.3 29.8 reduce-scatter.1
  188.3 40.0 all-reduce.5
  231.3 60.5 all-reduce.3
where the time goes:
time: 306 us; the launch traced here: 302 us
  matrix products  120 us (39%)
  waiting for transfers between devices  108 us (35%)
  blocking collectives  50 us (16%)
  between operations  14.1 us (5%)
  local copies, waits for them, and re-layouts  8.65 us (3%)
    dot_general x12, matrix products, local(): jnp.einsum('jmk,kmc->jmc', table, book_part, precision=precise, preferred...  60.8 us
    psum x1, waiting for transfers between devices, local(): grad_queries = lax.psum(query_terms, 'corpus')  45.4 us
    dot_general x12, matrix products, local(): jnp.einsum('jmk,jmc->kmc', table, grad_part, precision=precise, preferred...  33.1 us
    psum x1, waiting for transfers between devices, local(): codebook_part = lax.psum(codebook_part, 'query')  32.3 us
    reduce_scatter x1, waiting for transfers between devices, local(): lax.psum_scatter(local_codebook, 'corpus', scatter_dimension=0, tiled=True)  29.9 us
    all_gather x1, blocking collectives, local(): grad_codebook = lax.all_gather(codebook_part, 'corpus', axis=0, tiled=True)  18.2 us
    pmax x1, blocking collectives, local(): row_top = lax.pmax(local_top, 'corpus')  18.1 us
    psum x1, blocking collectives, local(): lax.psum((jnp.sum(jnp.exp(scores - row_top[:, None]), axis=1), own_score)...  13.7 us
  transfers between devices with their start and end apart: 3, of which 3 were waited for; matrix products, arithmetic and copies ran while one was open for 4% of the time, Pallas kernels for 0%

commit v1 on v0

v1 whole, which is shorter than its diff:
```python
import functools

import jax
import jax.numpy as jnp
from jax import lax
from jax.experimental import pallas as pl
from jax.experimental.pallas import tpu as pltpu
from jax.sharding import PartitionSpec as P

F32, BF16, I32 = jnp.float32, jnp.bfloat16, jnp.int32
LANES = 128


def split2(x):
    high = x.astype(BF16)
    return high, (x - high.astype(F32)).astype(BF16)


def split3(x):
    high = x.astype(BF16)
    rest = x - high.astype(F32)
    mid = rest.astype(BF16)
    return high, mid, (rest - mid.astype(F32)).astype(BF16)


def dot(a, b):
    return jnp.dot(a, b, preferred_element_type=F32)


def dot_nt(a, b):
    return lax.dot_general(a, b, (((1,), (1,)), ((), ())), preferred_element_type=F32)


def score_kernel(q_ref, codes_t_ref, book_t_ref, pos_ref, e_ref, r_ref, stats_ref, qs_ref, s_ref, low_ref):
    rows, width = q_ref.shape
    subs, docs = codes_t_ref.shape
    words = book_t_ref.shape[1]
    sub_width = width // subs
    high, mid, low = split3(q_ref[...])
    qs_ref[:, 0:width] = low
    qs_ref[:, width : 2 * width] = mid
    qs_ref[:, 2 * width : 3 * width] = high

    def rebuild(g, _):
        first = pl.multiple_of(g * 8, 8)
        block = codes_t_ref[pl.ds(first, 8), :]
        for pair in range(4):
            out_row = pl.multiple_of(g * 8 * sub_width + pair * 16, 16)
            tables = [book_t_ref[pl.ds(out_row + 8 * k, 8), :] for k in range(2)]
            for d in range(docs // LANES):
                lanes = slice(d * LANES, (d + 1) * LANES)
                halves = []
                for k in range(2):
                    code = jnp.broadcast_to(block[2 * pair + k : 2 * pair + k + 1, lanes], (8, LANES))
                    inner = code & (LANES - 1)
                    value = jnp.take_along_axis(tables[k][:, :LANES], inner, axis=1)
                    for w in range(1, words // LANES):
                        other = jnp.take_along_axis(tables[k][:, w * LANES : (w + 1) * LANES], inner, axis=1)
                        value = jnp.where(code >= w * LANES, other, value)
                    halves.append(value)
                high, mid, low = split3(jnp.concatenate(halves, axis=0))
                r_ref[pl.ds(out_row, 16), lanes] = high
                r_ref[pl.ds(out_row + width, 16), lanes] = mid
                low_ref[pl.ds(out_row, 16), lanes] = low
        return 0

    lax.fori_loop(0, subs // 8, rebuild, 0)

    tile = 256

    def score(t, _):
        lanes = pl.ds(pl.multiple_of(t * tile, tile), tile)
        small = dot(qs_ref[:, 0 : 2 * width], r_ref[:, lanes]) + dot(qs_ref[:, 2 * width :], low_ref[:, lanes])
        middle = dot(qs_ref[:, width:], r_ref[:, lanes])
        s_ref[:, lanes] = (small + middle) + dot(qs_ref[:, 2 * width :], r_ref[0:width, lanes])
        return 0

    lax.fori_loop(0, docs // tile, score, 0)
    s = s_ref[...]
    top = jnp.max(s, axis=1, keepdims=True)
    e = jnp.exp(s - top)
    e_ref[...] = e
    total = jnp.sum(e, axis=1, keepdims=True)
    hits = pos_ref[...] == lax.broadcasted_iota(I32, s.shape, 1)
    own = jnp.sum(jnp.where(hits, s, 0.0), axis=1, keepdims=True)
    lane = lax.broadcasted_iota(I32, (rows, LANES), 1)
    packed = jnp.where(lane == 0, top, jnp.where(lane == 1, total, jnp.where(lane == 2, own, 0.0)))
    stats_ref[...] = packed.T[0:8, :]


def query_kernel(e_ref, pos_ref, r_ref, u_ref, p_ref):
    rows, docs = e_ref.shape
    width = u_ref.shape[1]
    eh, em = split2(e_ref[...])
    hits = (pos_ref[...] == lax.broadcasted_iota(I32, (rows, docs), 1)).astype(F32).astype(BF16)
    tile = 256

    def step(t, _):
        first = pl.multiple_of(t * tile, tile)
        rh = r_ref[pl.ds(first, tile), :]
        rm = r_ref[pl.ds(first + width, tile), :]
        u_ref[:, pl.ds(first, tile)] = (dot_nt(em, rh) + dot_nt(eh, rm)) + dot_nt(eh, rh)
        p_ref[:, pl.ds(first, tile)] = dot_nt(hits, rm) + dot_nt(hits, rh)
        return 0

    lax.fori_loop(0, width // tile, step, 0)


def book_kernel(e_ref, pos_ref, scale_ref, q_ref, codes_t_ref, out_ref, ws_ref, qt_ref, dg_ref, gt_ref):
    rows, docs = e_ref.shape
    width = q_ref.shape[1]
    subs = codes_t_ref.shape[0]
    sub_width = width // subs
    words = out_ref.shape[0]
    hits = pos_ref[...] == lax.broadcasted_iota(I32, (rows, docs), 1)
    w = e_ref[...] * scale_ref[...] - jnp.where(hits, 1.0, 0.0)
    wh, wm = split2(w)
    ws_ref[0:rows, :] = wh
    ws_ref[rows : 2 * rows, :] = wm
    qh, qm = split2(q_ref[...].T)
    qt_ref[:, 0:rows] = qm
    qt_ref[:, rows : 2 * rows] = qh
    tile = 256

    def grad(t, _):
        lanes = pl.ds(pl.multiple_of(t * tile, tile), tile)
        dg_ref[:, lanes] = dot(qt_ref[...], ws_ref[:, lanes]) + dot(qt_ref[:, rows:], ws_ref[0:rows, lanes])
        return 0

    lax.fori_loop(0, docs // tile, grad, 0)

    fine = 64
    coarse = words // fine

    def scatter(g, _):
        first = pl.multiple_of(g * 8, 8)
        block = codes_t_ref[pl.ds(first, 8), :]
        for half in range(2):
            lhs, rhs = [], []
            for s in range(4):
                sub = half * 4 + s
                code = block[sub : sub + 1, :]
                row = pl.multiple_of(g * 8 * sub_width + sub * 8, 8)
                value = dg_ref[pl.ds(row, 8), :]
                high = value.astype(BF16).astype(F32)
                rest = value - high
                outer = jnp.broadcast_to(code // fine, value.shape)
                for piece in (high, rest):
                    for b in range(coarse):
                        lhs.append(jnp.where(outer == b, piece, 0.0))
                inner = jnp.broadcast_to(code & (fine - 1), (fine, docs))
                rhs.append(jnp.where(inner == lax.broadcasted_iota(I32, (fine, docs), 0), 1.0, 0.0))
            lhs = jnp.concatenate(lhs, axis=0).astype(BF16)
            rhs = jnp.concatenate(rhs, axis=0).astype(BF16)
            out = dot_nt(lhs, rhs)
            span = coarse * 8
            for s in range(4):
                both = out[2 * span * s : 2 * span * s + span, :] + out[2 * span * s + span : 2 * span * (s + 1), :]
                mine = both[:, s * fine : (s + 1) * fine]
                parts = [mine[8 * b : 8 * b + 8, :] for b in range(coarse)]
                row = pl.multiple_of(g * 8 * sub_width + (half * 4 + s) * 8, 8)
                gt_ref[pl.ds(row, 8), :] = jnp.concatenate(parts, axis=1)
        return 0

    lax.fori_loop(0, subs // 8, scatter, 0)
    out_ref[...] = gt_ref[...].T


def pairs(axis, bits):
    return [(i, i ^ bits) for i in range(lax.axis_size(axis))]


def swap(x, axis, bits):
    return lax.ppermute(x, axis, pairs(axis, bits))


def pick(parts, index):
    return lax.dynamic_index_in_dim(parts, index, 0, keepdims=False)


def scatter_sum(x, axis, place, count, unit):
    parts = x.reshape((count, x.shape[0] // count) + x.shape[1:])
    got = [swap(pick(parts, place ^ k), axis, k * unit) for k in range(1, count)]
    mine = pick(parts, place)
    for piece in got:
        mine = mine + piece
    return mine


def gather(x, axis, place, count, unit):
    got = [x] + [swap(x, axis, k * unit) for k in range(1, count)]
    out = jnp.zeros((count,) + x.shape, x.dtype)
    for k, piece in enumerate(got):
        out = lax.dynamic_update_index_in_dim(out, piece, place ^ k, 0)
    return out.reshape((count * x.shape[0],) + x.shape[1:])


def join_stats(a, b):
    top = jnp.maximum(a[0], b[0])
    total = a[1] * jnp.exp(a[0] - top) + b[1] * jnp.exp(b[0] - top)
    return jnp.stack([top, total, a[2] + b[2]])


VMEM = pl.BlockSpec(memory_space=pltpu.VMEM)


def local(queries, codes, positive, codebook):
    rows, width = queries.shape
    docs, subs = codes.shape
    words = codebook.shape[0]
    codes_t = codes.T
    book_t = codebook.T
    rel = (positive - lax.axis_index("corpus") * docs)[:, None]
    e, r, stats = pl.pallas_call(
        score_kernel,
        out_shape=(
            jax.ShapeDtypeStruct((rows, docs), F32),
            jax.ShapeDtypeStruct((2 * width, docs), BF16),
            jax.ShapeDtypeStruct((8, rows), F32),
        ),
        in_specs=[VMEM] * 4,
        out_specs=[VMEM] * 3,
        scratch_shapes=[pltpu.VMEM((rows, 3 * width), BF16), pltpu.VMEM((rows, docs), F32), pltpu.VMEM((width, docs), BF16)],
        compiler_params=pltpu.CompilerParams(vmem_limit_bytes=32 * 2**20),
        name="scores",
    )(queries, codes_t, book_t, rel)
    corpus, query = lax.axis_size("corpus"), lax.axis_size("query")
    me = lax.axis_index("corpus")
    core, chip, chips = me % 2, me // 2, corpus // 2
    plane = lax.axis_index("query")
    top = stats[0]
    joined = stats[0:3]
    bits = 1
    while bits < corpus:
        joined = join_stats(joined, swap(joined, "corpus", bits))
        bits *= 2
    log_total = joined[0] + jnp.log(joined[1])
    loss = log_total - joined[2]
    scale = jnp.exp(top - log_total)[:, None]
    u, p = pl.pallas_call(
        query_kernel,
        out_shape=(jax.ShapeDtypeStruct((rows, width), F32), jax.ShapeDtypeStruct((rows, width), F32)),
        in_specs=[VMEM] * 3,
        out_specs=[VMEM] * 2,
        compiler_params=pltpu.CompilerParams(vmem_limit_bytes=32 * 2**20),
        name="query_terms",
    )(e, rel, r)
    terms = u * scale - p
    book = pl.pallas_call(
        book_kernel,
        out_shape=jax.ShapeDtypeStruct((words, width), F32),
        in_specs=[VMEM] * 5,
        out_specs=VMEM,
        scratch_shapes=[
            pltpu.VMEM((2 * rows, docs), BF16),
            pltpu.VMEM((width, 2 * rows), BF16),
            pltpu.VMEM((width, docs), F32),
            pltpu.VMEM((width, words), F32),
        ],
        compiler_params=pltpu.CompilerParams(vmem_limit_bytes=32 * 2**20),
        name="book_terms",
    )(e, rel, scale, queries, codes_t)
    part = scatter_sum(terms, "corpus", core, 2, 1)
    part = scatter_sum(part, "corpus", chip, chips, 2)
    part = gather(part, "corpus", chip, chips, 2)
    grad_queries = gather(part, "corpus", core, 2, 1)
    part = scatter_sum(book, "corpus", core, 2, 1)
    part = scatter_sum(part, "query", plane, query, 1)
    part = scatter_sum(part, "corpus", chip, chips, 2)
    part = gather(part, "corpus", chip, chips, 2)
    part = gather(part, "query", plane, query, 1)
    grad_codebook = gather(part, "corpus", core, 2, 1)
    return grad_queries, grad_codebook, loss


def solution(mesh):
    placed = (P("query", None), P("corpus", None), P("query"), P())
    return jax.shard_map(
        local,
        mesh=mesh,
        in_specs=placed,
        out_specs=(P("query", None), P(), P("query")),
        check_vma=False,
    )
```

time: 306 us -> 128 us (0.42)
  matrix products: 120 us -> 0 us
  waiting for transfers between devices: 108 us -> 35.8 us
  blocking collectives: 50 us -> 0 us
  starting transfers between devices: 0.29 us -> 31.8 us
  Pallas kernels: 0 us -> 24.5 us
  local copies, waits for them, and re-layouts: 8.65 us -> 24.4 us
  between operations: 14.1 us -> 1.13 us
  other arithmetic: 0.97 us -> 9.04 us
    dot_general x27 -> x0, matrix products: 120 us -> none  [the longest x12 60.8 us: local(): jnp.einsum('jmk,kmc->jmc', table, book_part, precision=precise, preferred...]
    psum x2 -> x0, waiting for transfers between devices: 77.7 us -> none  [the longest x1 45.4 us: local(): grad_queries = lax.psum(query_terms, 'corpus')]
    ppermute x0 -> x25, waiting for transfers between devices: none -> 35.8 us  [swap(): return lax.ppermute(x, axis, pairs(axis, bits))]
    ppermute x0 -> x25, starting transfers between devices: none -> 31.8 us  [swap(): return lax.ppermute(x, axis, pairs(axis, bits))]
    reduce_scatter x1 -> x0, waiting for transfers between devices: 29.9 us -> none  [local(): lax.psum_scatter(local_codebook, 'corpus', scatter_dimension=0, tiled=True)]
    pallas_call x0 -> x3, Pallas kernels: none -> 24.5 us  [the longest x1 10.3 us: local(): pl.pallas_call(book_kernel, out_shape=jax.ShapeDtypeStruct((words, width)...]
    all_gather x1 -> x0, blocking collectives: 18.2 us -> none  [local(): grad_codebook = lax.all_gather(codebook_part, 'corpus', axis=0, tiled=True)]
    pmax x1 -> x0, blocking collectives: 18.1 us -> none  [local(): row_top = lax.pmax(local_top, 'corpus')]
  transfers between devices with their start and end apart: 3 -> 25, of which waited for: 3 -> 14; matrix products, arithmetic and copies ran while one was open for 4% -> 9% of each run, Pallas kernels for 0% -> 3%
where the time goes in v1:
time: 128 us; the launch traced here: 127 us
  waiting for transfers between devices  35.8 us (28%)
  starting transfers between devices  31.8 us (25%)
  Pallas kernels  24.5 us (19%)
  local copies, waits for them, and re-layouts  24.4 us (19%)
  other arithmetic  9.04 us (7%)
    ppermute x25, waiting for transfers between devices, swap(): return lax.ppermute(x, axis, pairs(axis, bits))  35.8 us
    ppermute x25, starting transfers between devices, swap(): return lax.ppermute(x, axis, pairs(axis, bits))  31.8 us
    unnamed x39, local copies, waits for them, and re-layouts  10.9 us
    pallas_call x1, Pallas kernels, local(): pl.pallas_call(book_kernel, out_shape=jax.ShapeDtypeStruct((words, width)...  10.3 us
    pallas_call x1, Pallas kernels, local(): pl.pallas_call(score_kernel, out_shape=(jax.ShapeDtypeStruct((rows, docs)...  10.1 us
    squeeze x4, local copies, waits for them, and re-layouts, join_stats(): total = a[1] * jnp.exp(a[0] - top) + b[1] * jnp.exp(b[0] - top)  5.26 us
    squeeze x3, local copies, waits for them, and re-layouts, join_stats(): top = jnp.maximum(a[0], b[0])  4.48 us
    pallas_call x1, Pallas kernels, local(): pl.pallas_call(query_kernel, out_shape=(jax.ShapeDtypeStruct((rows, width...  4.16 us
  transfers between devices with their start and end apart: 25, of which 14 were waited for; matrix products, arithmetic and copies ran while one was open for 9% of the time, Pallas kernels for 3%

profile of v1, /device:TPU:0, one launch (start us, length us, event | category | flops | bytes accessed | tf_op | source)
XLA Modules:
  0.0 126.8 jit_solution(11944983789584661947)
XLA Ops:
  0.7 0.8 broadcast_subtract_fusion
  1.5 0.1 broadcast_in_dim.94.pos_ref
  1.6 2.3 %copy.25 = f32[256,768]{0,1:T(8,128)} copy(f32[256,768]{1,0:T(8,128)} %param.7) | data formatting | bytes 1572864 | tf_op args[3]
  3.9 1.1 copy-done.3
  5.0 10.1 %scores.1 = (f32[384,1024]{1,0:T(8,128)S(1)}, bf16[1536,1024]{1,0:T(8,128)(2,1)S(1)}, f32[8,384]{1,0:T(8,128)S(1)}) custom-call(f32[384,768]{1,0:T(8,128)S(1)} %copy-done, s32[96,1024]{1,0:T(8,128)S(1)} %bitcast.116, f32[768,256]{1,0:T(8,128)S(1)} %bitcast.113, s32[384,1]{1,0:T(8,128)S(1)} %broadcast_in_dim.94.pos_ref), custom_call_target="tpu_custom_call" | custom-call | tf_op jit(solution)/shard_map/scores/pallas_call | solution.py:214
  15.1 1.6 %copy-done.1 = bf16[1536,1024]{1,0:T(8,128)(2,1)} copy-done((bf16[1536,1024]{1,0:T(8,128)(2,1)}, bf16[1536,1024]{1,0:T(8,128)(2,1)S(1)}, u32[]{:S(2)}) %copy-start.1) | copy-done | bytes 3145752
  16.8 0.5 collective-permute-start
  17.2 0.8 collective-permute-done
  18.0 1.2 slice_bitcast_fusion.6
  19.2 3.0 %collective-permute-start.1 = (f32[3,384]{1,0:T(4,128)S(1)}, f32[3,384]{1,0:T(4,128)S(1)}, u32[]{:S(2)}, u32[]{:S(2)}) collective-permute-start(f32[3,384]{1,0:T(4,128)S(1)} %pad_maximum_fusion), channel_id=1, source_target_pairs={{0,2},{1,3},{2,0},{3,1},{4,6},{5,7},{6,4},{7,5},{8,10},{9,11},{10,... | collective-permute-start | bytes 13832 | tf_op jit(solution)/shard_map/ppermute | solution.py:174
  22.2 1.6 %collective-permute-done.1 = f32[3,384]{1,0:T(4,128)S(1)} collective-permute-done((f32[3,384]{1,0:T(4,128)S(1)}, f32[3,384]{1,0:T(4,128)S(1)}, u32[]{:S(2)}, u32[]{:S(2)}) %collective-permute-start.1) | collective-permute-done | bytes 4640 | tf_op jit(solution)/shard_map/ppermute | solution.py:174
  23.8 1.2 slice_reduce_fusion.5
  25.0 0.6 pad_maximum_fusion.1
  25.6 3.0 %collective-permute-start.2 = (f32[3,384]{1,0:T(4,128)}, f32[3,384]{1,0:T(4,128)}, u32[]{:S(2)}, u32[]{:S(2)}) collective-permute-start(f32[3,384]{1,0:T(4,128)} %pad_maximum_fusion.1), channel_id=1, source_target_pairs={{0,4},{1,5},{2,6},{3,7},{4,0},{5,1},{6,2},{7,3},{8,12},{9,13},{10,... | collective-permute-start | bytes 13832 | tf_op jit(solution)/shard_map/ppermute | solution.py:174
  28.6 0.6 bitcast_maximum_fusion
  29.2 0.8 copy.33
  30.0 1.5 %copy.34 = f32[384,1]{1,0:T(8,128)} copy(f32[384,1]{0,1:T(1,128)} %get-tuple-element.48) | data formatting | bytes 3072 | tf_op jit(solution)/shard_map/squeeze | solution.py:199
  31.5 1.5 %copy.36 = f32[384,1]{1,0:T(8,128)} copy(f32[384,1]{0,1:T(1,128)} %get-tuple-element.49) | data formatting | bytes 3072 | tf_op jit(solution)/shard_map/squeeze | solution.py:200
  33.0 1.5 %copy.42 = f32[384,1]{1,0:T(8,128)} copy(f32[384,1]{0,1:T(1,128)} %get-tuple-element.53) | data formatting | bytes 3072 | tf_op jit(solution)/shard_map/squeeze | solution.py:231
  34.5 1.5 %copy.28 = f32[384,1]{1,0:T(8,128)} copy(f32[384,1]{0,1:T(1,128)} %bitcast_maximum_fusion) | data formatting | bytes 3072 | tf_op jit(solution)/shard_map/max | solution.py:199
  36.0 1.5 %copy.29 = f32[384,1]{1,0:T(8,128)} copy(f32[384,1]{0,1:T(1,128)} %get-tuple-element.64) | data formatting | bytes 3072 | tf_op jit(solution)/shard_map/squeeze | solution.py:199
  37.4 1.5 %copy.39 = f32[384,1]{1,0:T(8,128)} copy(f32[384,1]{0,1:T(1,128)} %get-tuple-element.63) | data formatting | bytes 3072 | tf_op jit(solution)/shard_map/squeeze | solution.py:200
  38.9 2.0 %fusion.17 = (f32[384]{0:T(512)}, f32[384]{0:T(512)}, f32[384]{0:T(512)}, f32[384,1]{0,1:T(1,128)}, f32[384,1]{0,1:T(1,128)}) fusion(f32[1,384]{1,0:T(1,128)S(1)} %get-tuple-element.67, f32[3,384]{1,0:T(4,128)} %collective-permute-done.2), kind=kLoop, calls=%fused_computation.61 | loop fusion | flops 384 | bytes 13824 | tf_op jit(solution)/shard_map/add | solution.py:201
  40.9 1.5 %copy.30 = f32[384,1]{1,0:T(8,128)} copy(f32[384,1]{0,1:T(1,128)} %get-tuple-element.61) | data formatting | bytes 3072 | tf_op jit(solution)/shard_map/squeeze | solution.py:199
  42.5 1.5 %copy.41 = f32[384,1]{1,0:T(8,128)} copy(f32[384,1]{0,1:T(1,128)} %get-tuple-element.62) | data formatting | bytes 3072 | tf_op jit(solution)/shard_map/squeeze | solution.py:200
  44.0 1.7 %subtract_exponential_fusion.scale_ref = f32[384,1]{1,0:T(8,128)S(1)} fusion(f32[384,1]{1,0:T(8,128)} %copy.42, f32[384,1]{1,0:T(8,128)} %copy.41, f32[384,1]{1,0:T(8,128)} %copy.30, f32[384,1]{1,0:T(8,128)} %copy.39, f32[384,1]{1,0:T(8,128)} %copy.29, f32[384,1]{1,0:T(8,128)} %copy.28, f32[384,1]{1,0:T(8,128)} %copy.36, f32[384,1]{1,0:T(8,128)} %copy.34, ...), kind=kLoop, calls=%fused_computation.9 | loop fusion | flops 7296 | bytes 15360 | tf_op jit(solution)/shard_map/exp | solution.py:239
  45.7 10.3 %book_terms.1 = f32[256,768]{1,0:T(8,128)S(1)} custom-call(f32[384,1024]{1,0:T(8,128)S(1)} %get-tuple-element.8.e_ref, s32[384,1]{1,0:T(8,128)S(1)} %broadcast_in_dim.94.pos_ref, f32[384,1]{1,0:T(8,128)S(1)} %subtract_exponential_fusion.scale_ref, f32[384,768]{1,0:T(8,128)S(1)} %copy-done, s32[96,1024]{1,0:T(8,128)S(1)} %bitcast.117), custom_call_target="tpu_custom_call" | custom-call | tf_op jit(solution)/shard_map/book_terms/pallas_call | solution.py:249
  56.0 0.9 copy-done.4
  57.0 1.9 %copy-done.2 = bf16[1536,1024]{1,0:T(8,128)(2,1)S(1)} copy-done((bf16[1536,1024]{1,0:T(8,128)(2,1)S(1)}, bf16[1536,1024]{1,0:T(8,128)(2,1)}, u32[]{:S(2)}) %copy-start.2) | copy-done | bytes 3145752
  58.9 4.2 %query_terms.1 = (f32[384,768]{1,0:T(8,128)S(1)}, f32[384,768]{1,0:T(8,128)S(1)}) custom-call(f32[384,1024]{1,0:T(8,128)S(1)} %get-tuple-element.8.e_ref, s32[384,1]{1,0:T(8,128)S(1)} %broadcast_in_dim.94.pos_ref, bf16[1536,1024]{1,0:T(8,128)(2,1)S(1)} %copy-done.2), custom_call_target="tpu_custom_call" | custom-call | tf_op jit(solution)/shard_map/query_terms/pallas_call | solution.py:240
  63.1 1.0 copy-done.7
  64.2 1.0 copy-done.9
  65.2 0.6 fusion.18
  65.9 1.5 %collective-permute-start.12 = (f32[32,768]{1,0:T(8,128)S(1)}, f32[32,768]{1,0:T(8,128)S(1)}, u32[]{:S(2)}, u32[]{:S(2)}) collective-permute-start(f32[32,768]{1,0:T(8,128)S(1)} %get-tuple-element.33), channel_id=1, source_target_pairs={{0,8},{8,0},{16,24},{24,16},{1,9},{9,1},{17,25},{25,17},{2,10},{10... | collective-permute-start | bytes 294920 | tf_op jit(solution)/shard_map/ppermute | solution.py:174
  67.4 1.5 %collective-permute-start.13 = (f32[32,768]{1,0:T(8,128)S(1)}, f32[32,768]{1,0:T(8,128)S(1)}, u32[]{:S(2)}, u32[]{:S(2)}) collective-permute-start(f32[32,768]{1,0:T(8,128)S(1)} %get-tuple-element.35), channel_id=1, source_target_pairs={{0,16},{8,24},{16,0},{24,8},{1,17},{9,25},{17,1},{25,9},{2,18},{10... | collective-permute-start | bytes 294920 | tf_op jit(solution)/shard_map/ppermute | solution.py:174
  69.0 0.5 collective-permute-start.14
  69.5 1.7 %collective-permute-done.12 = f32[32,768]{1,0:T(8,128)S(1)} collective-permute-done((f32[32,768]{1,0:T(8,128)S(1)}, f32[32,768]{1,0:T(8,128)S(1)}, u32[]{:S(2)}, u32[]{:S(2)}) %collective-permute-start.12) | collective-permute-done | bytes 98336 | tf_op jit(solution)/shard_map/ppermute | solution.py:174
  71.1 2.4 %collective-permute-done.13 = f32[32,768]{1,0:T(8,128)S(1)} collective-permute-done((f32[32,768]{1,0:T(8,128)S(1)}, f32[32,768]{1,0:T(8,128)S(1)}, u32[]{:S(2)}, u32[]{:S(2)}) %collective-permute-start.13) | collective-permute-done | bytes 98336 | tf_op jit(solution)/shard_map/ppermute | solution.py:174
  73.5 1.0 collective-permute-done.14
  74.6 1.6 %collective-permute-start.15 = (f32[8,768]{1,0:T(8,128)S(1)}, f32[8,768]{1,0:T(8,128)S(1)}, u32[]{:S(2)}, u32[]{:S(2)}) collective-permute-start(f32[8,768]{1,0:T(8,128)S(1)} %get-tuple-element.36), channel_id=1, source_target_pairs={{0,2},{1,3},{2,0},{3,1},{4,6},{5,7},{6,4},{7,5},{8,10},{9,11},{10,... | collective-permute-start | bytes 73736 | tf_op jit(solution)/shard_map/ppermute | solution.py:174
  76.2 0.4 collective-permute-start.16
  76.5 2.5 %collective-permute-start.17 = (f32[8,768]{1,0:T(8,128)S(1)}, f32[8,768]{1,0:T(8,128)S(1)}, u32[]{:S(2)}, u32[]{:S(2)}) collective-permute-start(f32[8,768]{1,0:T(8,128)S(1)} %get-tuple-element.37), channel_id=1, source_target_pairs={{0,6},{1,7},{2,4},{3,5},{4,2},{5,3},{6,0},{7,1},{8,14},{9,15},{10,... | collective-permute-start | bytes 73736 | tf_op jit(solution)/shard_map/ppermute | solution.py:174
  79.0 0.2 multiply_subtract_fusion
  79.2 1.9 %collective-permute-done.16 = f32[8,768]{1,0:T(8,128)S(1)} collective-permute-done((f32[8,768]{1,0:T(8,128)S(1)}, f32[8,768]{1,0:T(8,128)S(1)}, u32[]{:S(2)}, u32[]{:S(2)}) %collective-permute-start.16) | collective-permute-done | bytes 24608 | tf_op jit(solution)/shard_map/ppermute | solution.py:174
  81.1 1.2 collective-permute-done.17
  82.5 3.0 %collective-permute-start.19 = (f32[8,768]{1,0:T(8,128)S(1)}, f32[8,768]{1,0:T(8,128)S(1)}, u32[]{:S(2)}, u32[]{:S(2)}) collective-permute-start(f32[8,768]{1,0:T(8,128)S(1)} %get-tuple-element.25), channel_id=1, source_target_pairs={{0,4},{1,5},{2,6},{3,7},{4,0},{5,1},{6,2},{7,3},{8,12},{9,13},{10,... | collective-permute-start | bytes 73736 | tf_op jit(solution)/shard_map/ppermute | solution.py:174
  85.5 1.5 %collective-permute-start.20 = (f32[8,768]{1,0:T(8,128)S(1)}, f32[8,768]{1,0:T(8,128)S(1)}, u32[]{:S(2)}, u32[]{:S(2)}) collective-permute-start(f32[8,768]{1,0:T(8,128)S(1)} %get-tuple-element.25), channel_id=1, source_target_pairs={{0,6},{1,7},{2,4},{3,5},{4,2},{5,3},{6,0},{7,1},{8,14},{9,15},{10,... | collective-permute-start | bytes 73736 | tf_op jit(solution)/shard_map/ppermute | solution.py:174
  87.0 0.4 collective-permute-done.19
  87.3 3.8 %collective-permute-done.20 = f32[8,768]{1,0:T(8,128)S(1)} collective-permute-done((f32[8,768]{1,0:T(8,128)S(1)}, f32[8,768]{1,0:T(8,128)S(1)}, u32[]{:S(2)}, u32[]{:S(2)}) %collective-permute-start.20) | collective-permute-done | bytes 24608 | tf_op jit(solution)/shard_map/ppermute | solution.py:174
  91.1 1.2 collective-permute-start.21
  92.3 0.8 collective-permute-start.22
  93.1 1.5 %collective-permute-start.23 = (f32[32,768]{1,0:T(8,128)S(1)}, f32[32,768]{1,0:T(8,128)S(1)}, u32[]{:S(2)}, u32[]{:S(2)}) collective-permute-start(f32[32,768]{1,0:T(8,128)S(1)} %bitcast.132), channel_id=1, source_target_pairs={{0,24},{8,16},{16,8},{24,0},{1,25},{9,17},{17,9},{25,1},{2,26},{10... | collective-permute-start | bytes 294920 | tf_op jit(solution)/shard_map/ppermute | solution.py:174
  94.7 0.1 bitcast_add_fusion
  94.9 2.0 %collective-permute-start.5 = (f32[48,768]{1,0:T(8,128)S(1)}, f32[48,768]{1,0:T(8,128)S(1)}, u32[]{:S(2)}, u32[]{:S(2)}) collective-permute-start(f32[48,768]{1,0:T(8,128)S(1)} %get-tuple-element.32), channel_id=1, source_target_pairs={{0,4},{1,5},{2,6},{3,7},{4,0},{5,1},{6,2},{7,3},{8,12},{9,13},{10,... | collective-permute-start | bytes 442376 | tf_op jit(solution)/shard_map/ppermute | solution.py:174
  96.9 2.4 %collective-permute-start.6 = (f32[48,768]{1,0:T(8,128)S(1)}, f32[48,768]{1,0:T(8,128)S(1)}, u32[]{:S(2)}, u32[]{:S(2)}) collective-permute-start(f32[48,768]{1,0:T(8,128)S(1)} %get-tuple-element.31), channel_id=1, source_target_pairs={{0,6},{1,7},{2,4},{3,5},{4,2},{5,3},{6,0},{7,1},{8,14},{9,15},{10,... | collective-permute-start | bytes 442376 | tf_op jit(solution)/shard_map/ppermute | solution.py:174
  99.3 1.4 %collective-permute-done.4 = f32[48,768]{1,0:T(8,128)S(1)} collective-permute-done((f32[48,768]{1,0:T(8,128)S(1)}, f32[48,768]{1,0:T(8,128)S(1)}, u32[]{:S(2)}, u32[]{:S(2)}) %collective-permute-start.4) | collective-permute-done | bytes 147488 | tf_op jit(solution)/shard_map/ppermute | solution.py:174
  100.7 7.1 %collective-permute-done.5 = f32[48,768]{1,0:T(8,128)S(1)} collective-permute-done((f32[48,768]{1,0:T(8,128)S(1)}, f32[48,768]{1,0:T(8,128)S(1)}, u32[]{:S(2)}, u32[]{:S(2)}) %collective-permute-start.5) | collective-permute-done | bytes 147488 | tf_op jit(solution)/shard_map/ppermute | solution.py:174
  107.8 2.2 %collective-permute-start.7 = (f32[48,768]{1,0:T(8,128)S(1)}, f32[48,768]{1,0:T(8,128)S(1)}, u32[]{:S(2)}, u32[]{:S(2)}) collective-permute-start(f32[48,768]{1,0:T(8,128)S(1)} %get-tuple-element.27), channel_id=1, source_target_pairs={{0,2},{1,3},{2,0},{3,1},{4,6},{5,7},{6,4},{7,5},{8,10},{9,11},{10,... | collective-permute-start | bytes 442376 | tf_op jit(solution)/shard_map/ppermute | solution.py:174
  110.1 0.1 collective-permute-start.8
  110.2 2.4 %collective-permute-start.9 = (f32[48,768]{1,0:T(8,128)S(1)}, f32[48,768]{1,0:T(8,128)S(1)}, u32[]{:S(2)}, u32[]{:S(2)}) collective-permute-start(f32[48,768]{1,0:T(8,128)S(1)} %get-tuple-element.27), channel_id=1, source_target_pairs={{0,6},{1,7},{2,4},{3,5},{4,2},{5,3},{6,0},{7,1},{8,14},{9,15},{10,... | collective-permute-start | bytes 442376 | tf_op jit(solution)/shard_map/ppermute | solution.py:174
  112.6 1.7 %collective-permute-done.7 = f32[48,768]{1,0:T(8,128)S(1)} collective-permute-done((f32[48,768]{1,0:T(8,128)S(1)}, f32[48,768]{1,0:T(8,128)S(1)}, u32[]{:S(2)}, u32[]{:S(2)}) %collective-permute-start.7) | collective-permute-done | bytes 147488 | tf_op jit(solution)/shard_map/ppermute | solution.py:174
  114.3 9.3 %collective-permute-done.8 = f32[48,768]{1,0:T(8,128)S(1)} collective-permute-done((f32[48,768]{1,0:T(8,128)S(1)}, f32[48,768]{1,0:T(8,128)S(1)}, u32[]{:S(2)}, u32[]{:S(2)}) %collective-permute-start.8) | collective-permute-done | bytes 147488 | tf_op jit(solution)/shard_map/ppermute | solution.py:174
  124.0 1.7 %collective-permute-done.10 = f32[192,768]{1,0:T(8,128)S(1)} collective-permute-done((f32[192,768]{1,0:T(8,128)S(1)}, f32[192,768]{1,0:T(8,128)S(1)}, u32[]{:S(2)}, u32[]{:S(2)}) %collective-permute-start.10) | collective-permute-done | bytes 589856 | tf_op jit(solution)/shard_map/ppermute | solution.py:174
  125.8 1.0 copy-done.11
  (79 shorter events, 1.3 us)
Async XLA Ops:
  0.6 3.2 %copy-start.6 = (s32[1024,96]{0,1:T(8,128)S(1)}, s32[1024,96]{0,1:T(8,128)}, u32[]{:S(2)}) copy-start(s32[1024,96]{0,1:T(8,128)} %param.5) | copy-start | bytes 1179652
  0.6 3.2 %copy-start = (f32[384,768]{1,0:T(8,128)S(1)}, f32[384,768]{1,0:T(8,128)}, u32[]{:S(2)}) copy-start(f32[384,768]{1,0:T(8,128)} %q_ref.3) | copy-start | bytes 3538948
  3.9 1.1 copy-start.3
  15.1 1.6 %copy-start.1 = (bf16[1536,1024]{1,0:T(8,128)(2,1)}, bf16[1536,1024]{1,0:T(8,128)(2,1)S(1)}, u32[]{:S(2)}) copy-start(bf16[1536,1024]{1,0:T(8,128)(2,1)S(1)} %get-tuple-element.9.r_ref) | copy-start | bytes 9437188
  16.8 1.3 %collective-permute-start = (f32[3,384]{1,0:T(4,128)S(1)}, f32[3,384]{1,0:T(4,128)S(1)}, u32[]{:S(2)}, u32[]{:S(2)}) collective-permute-start(f32[3,384]{1,0:T(4,128)S(1)} %slice.48), channel_id=1, source_target_pairs={{0,1},{1,0},{2,3},{3,2},{4,5},{5,4},{6,7},{7,6},{8,9},{9,8},{10,11... | collective-permute-start | bytes 13832 | tf_op jit(solution)/shard_map/ppermute | solution.py:174
  19.2 4.6 %collective-permute-start.1 = (f32[3,384]{1,0:T(4,128)S(1)}, f32[3,384]{1,0:T(4,128)S(1)}, u32[]{:S(2)}, u32[]{:S(2)}) collective-permute-start(f32[3,384]{1,0:T(4,128)S(1)} %pad_maximum_fusion), channel_id=1, source_target_pairs={{0,2},{1,3},{2,0},{3,1},{4,6},{5,7},{6,4},{7,5},{8,10},{9,11},{10,... | collective-permute-start | bytes 13832 | tf_op jit(solution)/shard_map/ppermute | solution.py:174
  25.6 13.4 %collective-permute-start.2 = (f32[3,384]{1,0:T(4,128)}, f32[3,384]{1,0:T(4,128)}, u32[]{:S(2)}, u32[]{:S(2)}) collective-permute-start(f32[3,384]{1,0:T(4,128)} %pad_maximum_fusion.1), channel_id=1, source_target_pairs={{0,4},{1,5},{2,6},{3,7},{4,0},{5,1},{6,2},{7,3},{8,12},{9,13},{10,... | collective-permute-start | bytes 13832 | tf_op jit(solution)/shard_map/ppermute | solution.py:174
  56.0 0.9 copy-start.4
  56.9 8.9 %collective-permute-start.11 = (f32[128,768]{1,0:T(8,128)S(1)}, f32[128,768]{1,0:T(8,128)S(1)}, u32[]{:S(2)}, u32[]{:S(2)}) collective-permute-start(f32[128,768]{1,0:T(8,128)S(1)} %dynamic-slice_bitcast_fusion.1), channel_id=1, source_target_pairs={{0,1},{1,0},{2,3},{3,2},{4,5},{5,4},{6,7},{7,6},{8,9},{9,8},{10,11... | collective-permute-start | bytes 1179656 | tf_op jit(solution)/shard_map/ppermute | solution.py:174
  57.0 1.9 %copy-start.2 = (bf16[1536,1024]{1,0:T(8,128)(2,1)S(1)}, bf16[1536,1024]{1,0:T(8,128)(2,1)}, u32[]{:S(2)}) copy-start(bf16[1536,1024]{1,0:T(8,128)(2,1)} %copy-done.1) | copy-start | bytes 9437188
  58.9 6.3 %copy-start.13 = (f32[384]{0:T(512)S(1)}, f32[384]{0:T(512)}, u32[]{:S(2)}) copy-start(f32[384]{0:T(512)} %get-tuple-element.58) | copy-start | bytes 4612
  58.9 6.3 %copy-start.14 = (f32[384]{0:T(512)S(1)}, f32[384]{0:T(512)}, u32[]{:S(2)}) copy-start(f32[384]{0:T(512)} %get-tuple-element.15) | copy-start | bytes 4612
  58.9 6.3 %copy-start.15 = (f32[384]{0:T(512)S(1)}, f32[384]{0:T(512)}, u32[]{:S(2)}) copy-start(f32[384]{0:T(512)} %get-tuple-element.16) | copy-start | bytes 4612
  58.9 6.3 %copy-start.16 = (f32[384]{0:T(512)S(1)}, f32[384]{0:T(512)}, u32[]{:S(2)}) copy-start(f32[384]{0:T(512)} %get-tuple-element.17) | copy-start | bytes 4612
  58.9 6.3 %copy-start.17 = (f32[384]{0:T(512)S(1)}, f32[384]{0:T(512)}, u32[]{:S(2)}) copy-start(f32[384]{0:T(512)} %get-tuple-element.20) | copy-start | bytes 4612
  58.9 6.3 %copy-start.18 = (f32[384]{0:T(512)S(1)}, f32[384]{0:T(512)}, u32[]{:S(2)}) copy-start(f32[384]{0:T(512)} %get-tuple-element.21) | copy-start | bytes 4612
  58.9 6.9 %copy-start.5 = (f32[256,768]{1,0:T(8,128)S(1)}, f32[256,768]{1,0:T(8,128)}, u32[]{:S(2)}) copy-start(f32[256,768]{1,0:T(8,128)} %copy-done.4) | copy-start | bytes 2359300
  63.1 1.0 copy-start.7
  64.2 1.0 copy-start.9
  65.8 13.2 %copy-start.8 = (f32[384,768]{1,0:T(8,128)S(1)}, f32[384,768]{1,0:T(8,128)}, u32[]{:S(2)}) copy-start(f32[384,768]{1,0:T(8,128)} %copy-done.7) | copy-start | bytes 3538948
  65.8 13.2 %copy-start.10 = (f32[384,768]{1,0:T(8,128)S(1)}, f32[384,768]{1,0:T(8,128)}, u32[]{:S(2)}) copy-start(f32[384,768]{1,0:T(8,128)} %copy-done.9) | copy-start | bytes 3538948
  65.9 5.2 %collective-permute-start.12 = (f32[32,768]{1,0:T(8,128)S(1)}, f32[32,768]{1,0:T(8,128)S(1)}, u32[]{:S(2)}, u32[]{:S(2)}) collective-permute-start(f32[32,768]{1,0:T(8,128)S(1)} %get-tuple-element.33), channel_id=1, source_target_pairs={{0,8},{8,0},{16,24},{24,16},{1,9},{9,1},{17,25},{25,17},{2,10},{10... | collective-permute-start | bytes 294920 | tf_op jit(solution)/shard_map/ppermute | solution.py:174
  67.4 6.0 %collective-permute-start.13 = (f32[32,768]{1,0:T(8,128)S(1)}, f32[32,768]{1,0:T(8,128)S(1)}, u32[]{:S(2)}, u32[]{:S(2)}) collective-permute-start(f32[32,768]{1,0:T(8,128)S(1)} %get-tuple-element.35), channel_id=1, source_target_pairs={{0,16},{8,24},{16,0},{24,8},{1,17},{9,25},{17,1},{25,9},{2,18},{10... | collective-permute-start | bytes 294920 | tf_op jit(solution)/shard_map/ppermute | solution.py:174
  69.0 5.5 %collective-permute-start.14 = (f32[32,768]{1,0:T(8,128)S(1)}, f32[32,768]{1,0:T(8,128)S(1)}, u32[]{:S(2)}, u32[]{:S(2)}) collective-permute-start(f32[32,768]{1,0:T(8,128)S(1)} %get-tuple-element.34), channel_id=1, source_target_pairs={{0,24},{8,16},{16,8},{24,0},{1,25},{9,17},{17,9},{25,1},{2,26},{10... | collective-permute-start | bytes 294920 | tf_op jit(solution)/shard_map/ppermute | solution.py:174
  74.6 4.6 %collective-permute-start.15 = (f32[8,768]{1,0:T(8,128)S(1)}, f32[8,768]{1,0:T(8,128)S(1)}, u32[]{:S(2)}, u32[]{:S(2)}) collective-permute-start(f32[8,768]{1,0:T(8,128)S(1)} %get-tuple-element.36), channel_id=1, source_target_pairs={{0,2},{1,3},{2,0},{3,1},{4,6},{5,7},{6,4},{7,5},{8,10},{9,11},{10,... | collective-permute-start | bytes 73736 | tf_op jit(solution)/shard_map/ppermute | solution.py:174
  76.2 4.9 %collective-permute-start.16 = (f32[8,768]{1,0:T(8,128)S(1)}, f32[8,768]{1,0:T(8,128)S(1)}, u32[]{:S(2)}, u32[]{:S(2)}) collective-permute-start(f32[8,768]{1,0:T(8,128)S(1)} %get-tuple-element.38), channel_id=1, source_target_pairs={{0,4},{1,5},{2,6},{3,7},{4,0},{5,1},{6,2},{7,3},{8,12},{9,13},{10,... | collective-permute-start | bytes 73736 | tf_op jit(solution)/shard_map/ppermute | solution.py:174
  76.5 5.7 %collective-permute-start.17 = (f32[8,768]{1,0:T(8,128)S(1)}, f32[8,768]{1,0:T(8,128)S(1)}, u32[]{:S(2)}, u32[]{:S(2)}) collective-permute-start(f32[8,768]{1,0:T(8,128)S(1)} %get-tuple-element.37), channel_id=1, source_target_pairs={{0,6},{1,7},{2,4},{3,5},{4,2},{5,3},{6,0},{7,1},{8,14},{9,15},{10,... | collective-permute-start | bytes 73736 | tf_op jit(solution)/shard_map/ppermute | solution.py:174
  82.3 4.6 %collective-permute-start.18 = (f32[8,768]{1,0:T(8,128)S(1)}, f32[8,768]{1,0:T(8,128)S(1)}, u32[]{:S(2)}, u32[]{:S(2)}) collective-permute-start(f32[8,768]{1,0:T(8,128)S(1)} %get-tuple-element.25), channel_id=1, source_target_pairs={{0,2},{1,3},{2,0},{3,1},{4,6},{5,7},{6,4},{7,5},{8,10},{9,11},{10,... | collective-permute-start | bytes 73736 | tf_op jit(solution)/shard_map/ppermute | solution.py:174
  82.4 12.2 %collective-permute-start.3 = (f32[192,768]{1,0:T(8,128)S(1)}, f32[192,768]{1,0:T(8,128)S(1)}, u32[]{:S(2)}, u32[]{:S(2)}) collective-permute-start(f32[192,768]{1,0:T(8,128)S(1)} %dynamic-slice_bitcast_fusion), channel_id=1, source_target_pairs={{0,1},{1,0},{2,3},{3,2},{4,5},{5,4},{6,7},{7,6},{8,9},{9,8},{10,11... | collective-permute-start | bytes 1769480 | tf_op jit(solution)/shard_map/ppermute | solution.py:174
  82.5 4.8 %collective-permute-start.19 = (f32[8,768]{1,0:T(8,128)S(1)}, f32[8,768]{1,0:T(8,128)S(1)}, u32[]{:S(2)}, u32[]{:S(2)}) collective-permute-start(f32[8,768]{1,0:T(8,128)S(1)} %get-tuple-element.25), channel_id=1, source_target_pairs={{0,4},{1,5},{2,6},{3,7},{4,0},{5,1},{6,2},{7,3},{8,12},{9,13},{10,... | collective-permute-start | bytes 73736 | tf_op jit(solution)/shard_map/ppermute | solution.py:174
  85.5 5.6 %collective-permute-start.20 = (f32[8,768]{1,0:T(8,128)S(1)}, f32[8,768]{1,0:T(8,128)S(1)}, u32[]{:S(2)}, u32[]{:S(2)}) collective-permute-start(f32[8,768]{1,0:T(8,128)S(1)} %get-tuple-element.25), channel_id=1, source_target_pairs={{0,6},{1,7},{2,4},{3,5},{4,2},{5,3},{6,0},{7,1},{8,14},{9,15},{10,... | collective-permute-start | bytes 73736 | tf_op jit(solution)/shard_map/ppermute | solution.py:174
  91.1 5.8 %collective-permute-start.21 = (f32[32,768]{1,0:T(8,128)S(1)}, f32[32,768]{1,0:T(8,128)S(1)}, u32[]{:S(2)}, u32[]{:S(2)}) collective-permute-start(f32[32,768]{1,0:T(8,128)S(1)} %bitcast.130), channel_id=1, source_target_pairs={{0,8},{8,0},{16,24},{24,16},{1,9},{9,1},{17,25},{25,17},{2,10},{10... | collective-permute-start | bytes 294920 | tf_op jit(solution)/shard_map/ppermute | solution.py:174
  92.3 7.0 %collective-permute-start.22 = (f32[32,768]{1,0:T(8,128)S(1)}, f32[32,768]{1,0:T(8,128)S(1)}, u32[]{:S(2)}, u32[]{:S(2)}) collective-permute-start(f32[32,768]{1,0:T(8,128)S(1)} %bitcast.131), channel_id=1, source_target_pairs={{0,16},{8,24},{16,0},{24,8},{1,17},{9,25},{17,1},{25,9},{2,18},{10... | collective-permute-start | bytes 294920 | tf_op jit(solution)/shard_map/ppermute | solution.py:174
  93.1 16.9 %collective-permute-start.23 = (f32[32,768]{1,0:T(8,128)S(1)}, f32[32,768]{1,0:T(8,128)S(1)}, u32[]{:S(2)}, u32[]{:S(2)}) collective-permute-start(f32[32,768]{1,0:T(8,128)S(1)} %bitcast.132), channel_id=1, source_target_pairs={{0,24},{8,16},{16,8},{24,0},{1,25},{9,17},{17,9},{25,1},{2,26},{10... | collective-permute-start | bytes 294920 | tf_op jit(solution)/shard_map/ppermute | solution.py:174
  94.8 5.9 %collective-permute-start.4 = (f32[48,768]{1,0:T(8,128)S(1)}, f32[48,768]{1,0:T(8,128)S(1)}, u32[]{:S(2)}, u32[]{:S(2)}) collective-permute-start(f32[48,768]{1,0:T(8,128)S(1)} %get-tuple-element.30), channel_id=1, source_target_pairs={{0,2},{1,3},{2,0},{3,1},{4,6},{5,7},{6,4},{7,5},{8,10},{9,11},{10,... | collective-permute-start | bytes 442376 | tf_op jit(solution)/shard_map/ppermute | solution.py:174
  94.9 12.8 %collective-permute-start.5 = (f32[48,768]{1,0:T(8,128)S(1)}, f32[48,768]{1,0:T(8,128)S(1)}, u32[]{:S(2)}, u32[]{:S(2)}) collective-permute-start(f32[48,768]{1,0:T(8,128)S(1)} %get-tuple-element.32), channel_id=1, source_target_pairs={{0,4},{1,5},{2,6},{3,7},{4,0},{5,1},{6,2},{7,3},{8,12},{9,13},{10,... | collective-permute-start | bytes 442376 | tf_op jit(solution)/shard_map/ppermute | solution.py:174
  96.9 10.8 %collective-permute-start.6 = (f32[48,768]{1,0:T(8,128)S(1)}, f32[48,768]{1,0:T(8,128)S(1)}, u32[]{:S(2)}, u32[]{:S(2)}) collective-permute-start(f32[48,768]{1,0:T(8,128)S(1)} %get-tuple-element.31), channel_id=1, source_target_pairs={{0,6},{1,7},{2,4},{3,5},{4,2},{5,3},{6,0},{7,1},{8,14},{9,15},{10,... | collective-permute-start | bytes 442376 | tf_op jit(solution)/shard_map/ppermute | solution.py:174
  107.8 6.4 %collective-permute-start.7 = (f32[48,768]{1,0:T(8,128)S(1)}, f32[48,768]{1,0:T(8,128)S(1)}, u32[]{:S(2)}, u32[]{:S(2)}) collective-permute-start(f32[48,768]{1,0:T(8,128)S(1)} %get-tuple-element.27), channel_id=1, source_target_pairs={{0,2},{1,3},{2,0},{3,1},{4,6},{5,7},{6,4},{7,5},{8,10},{9,11},{10,... | collective-permute-start | bytes 442376 | tf_op jit(solution)/shard_map/ppermute | solution.py:174
  110.0 13.9 %collective-permute-start.24 = (f32[128,768]{1,0:T(8,128)S(1)}, f32[128,768]{1,0:T(8,128)S(1)}, u32[]{:S(2)}, u32[]{:S(2)}) collective-permute-start(f32[128,768]{1,0:T(8,128)S(1)} %bitcast.124), channel_id=1, source_target_pairs={{0,1},{1,0},{2,3},{3,2},{4,5},{5,4},{6,7},{7,6},{8,9},{9,8},{10,11... | collective-permute-start | bytes 1179656 | tf_op jit(solution)/shard_map/ppermute | solution.py:174
  110.1 13.4 %collective-permute-start.8 = (f32[48,768]{1,0:T(8,128)S(1)}, f32[48,768]{1,0:T(8,128)S(1)}, u32[]{:S(2)}, u32[]{:S(2)}) collective-permute-start(f32[48,768]{1,0:T(8,128)S(1)} %get-tuple-element.27), channel_id=1, source_target_pairs={{0,4},{1,5},{2,6},{3,7},{4,0},{5,1},{6,2},{7,3},{8,12},{9,13},{10,... | collective-permute-start | bytes 442376 | tf_op jit(solution)/shard_map/ppermute | solution.py:174
  110.2 13.4 %collective-permute-start.9 = (f32[48,768]{1,0:T(8,128)S(1)}, f32[48,768]{1,0:T(8,128)S(1)}, u32[]{:S(2)}, u32[]{:S(2)}) collective-permute-start(f32[48,768]{1,0:T(8,128)S(1)} %get-tuple-element.27), channel_id=1, source_target_pairs={{0,6},{1,7},{2,4},{3,5},{4,2},{5,3},{6,0},{7,1},{8,14},{9,15},{10,... | collective-permute-start | bytes 442376 | tf_op jit(solution)/shard_map/ppermute | solution.py:174
  123.6 2.1 %collective-permute-start.10 = (f32[192,768]{1,0:T(8,128)S(1)}, f32[192,768]{1,0:T(8,128)S(1)}, u32[]{:S(2)}, u32[]{:S(2)}) collective-permute-start(f32[192,768]{1,0:T(8,128)S(1)} %bitcast.120), channel_id=1, source_target_pairs={{0,1},{1,0},{2,3},{3,2},{4,5},{5,4},{6,7},{7,6},{8,9},{9,8},{10,11... | collective-permute-start | bytes 1769480 | tf_op jit(solution)/shard_map/ppermute | solution.py:174
  124.0 1.8 %copy-start.12 = (f32[2,128,768]{2,1,0:T(8,128)}, f32[2,128,768]{2,1,0:T(8,128)S(1)}, u32[]{:S(2)}) copy-start(f32[2,128,768]{2,1,0:T(8,128)S(1)} %bitcast_dynamic-update-slice_fusion.2) | copy-start | bytes 2359300
  125.7 1.0 copy-start.11

commit v2 on v0

v2 whole, which is shorter than its diff:
```python
import jax
import jax.numpy as jnp
from jax import lax
from jax.experimental import pallas as pl
from jax.experimental.pallas import tpu as pltpu
from jax.sharding import PartitionSpec as P

F32, BF16, I32 = jnp.float32, jnp.bfloat16, jnp.int32
LANES = 128
FINE = 64
VMEM = pl.BlockSpec(memory_space=pltpu.VMEM)
ANY = pl.BlockSpec(memory_space=pl.ANY)


def split2(x):
    high = x.astype(BF16)
    return high, (x - high.astype(F32)).astype(BF16)


def split3(x):
    high = x.astype(BF16)
    rest = x - high.astype(F32)
    mid = rest.astype(BF16)
    return high, mid, (rest - mid.astype(F32)).astype(BF16)


def dot(a, b):
    return jnp.dot(a, b, preferred_element_type=F32)


def dot_nt(a, b):
    return lax.dot_general(a, b, (((1,), (1,)), ((), ())), preferred_element_type=F32)


def column(row):
    return jnp.broadcast_to(row, (LANES, row.shape[1])).T


def pick_lanes(table, code):
    inner = code & (LANES - 1)
    value = None
    for w in range(table.shape[1] // LANES):
        part = jnp.take_along_axis(
            table[:, w * LANES : (w + 1) * LANES], inner, axis=1, mode="promise_in_bounds"
        )
        value = part if w == 0 else jnp.where(code >= w * LANES, part, value)
    return value


def score_kernel(
    q_hbm, codes_hbm, book_hbm, pos_hbm,
    e_ref, hits_ref, r_ref, stats_ref,
    q_ref, codes_ref, book_ref, pos_ref, qs_ref, s_ref, low_ref, book_t_ref, sems,
):
    rows, width = q_ref.shape
    subs, docs = codes_ref.shape
    loads = [
        pltpu.make_async_copy(src, dst, sems.at[i])
        for i, (src, dst) in enumerate(
            [(book_hbm, book_ref), (codes_hbm, codes_ref), (q_hbm, q_ref), (pos_hbm, pos_ref)]
        )
    ]
    for load in loads:
        load.start()
    loads[0].wait()
    book_t_ref[...] = book_ref[...].T
    loads[1].wait()
    loads[2].wait()
    loads[3].wait()
    high, mid, low = split3(q_ref[...])
    qs_ref[:, 0:width] = low
    qs_ref[:, width : 2 * width] = mid
    qs_ref[:, 2 * width : 3 * width] = high
    tile = 256
    for t in range(docs // tile):
        for sub in range(0, subs, 2):
            for d in range(t * tile, (t + 1) * tile, LANES):
                lanes = slice(d, d + LANES)
                halves = [
                    pick_lanes(
                        book_t_ref[8 * s : 8 * s + 8, :],
                        jnp.broadcast_to(codes_ref[s : s + 1, lanes], (8, LANES)),
                    )
                    for s in (sub, sub + 1)
                ]
                high, mid, low = split3(jnp.concatenate(halves, axis=0))
                r_ref[8 * sub : 8 * sub + 16, lanes] = high
                r_ref[width + 8 * sub : width + 8 * sub + 16, lanes] = mid
                low_ref[8 * sub : 8 * sub + 16, lanes] = low
        lanes = slice(t * tile, (t + 1) * tile)
        small = dot(qs_ref[:, 0 : 2 * width], r_ref[:, lanes]) + dot(
            qs_ref[:, 2 * width :], low_ref[:, lanes]
        )
        middle = dot(qs_ref[:, width:], r_ref[:, lanes])
        s_ref[:, lanes] = (small + middle) + dot(qs_ref[:, 2 * width :], r_ref[0:width, lanes])
    s = s_ref[...]
    top = jnp.max(s, axis=1, keepdims=True)
    e = jnp.exp(s - top)
    e_ref[...] = e
    total = jnp.sum(e, axis=1, keepdims=True)
    wanted = column(pos_ref[...].reshape(1, rows) - lax.axis_index("corpus") * docs)[:, 0:1]
    hits = wanted == lax.broadcasted_iota(I32, s.shape, 1)
    hits_ref[...] = jnp.where(hits, 1.0, 0.0).astype(BF16)
    own = jnp.sum(jnp.where(hits, s, 0.0), axis=1, keepdims=True)
    lane = lax.broadcasted_iota(I32, (rows, LANES), 1)
    packed = jnp.where(lane == 0, top, jnp.where(lane == 1, total, jnp.where(lane == 2, own, 0.0)))
    stats_ref[...] = packed.T[0:8, :]


def spread_kernel(e_ref, r_ref, u_ref):
    width = u_ref.shape[1]
    eh, em = split2(e_ref[...])
    rh, rm = r_ref[0:width, :], r_ref[width:, :]
    u_ref[...] = (dot_nt(em, rh) + dot_nt(eh, rm)) + dot_nt(eh, rh)


def positive_kernel(hits_ref, r_ref, q_hbm, after_ref, p_ref, qt_ref, q_ref, sem):
    rows, width = p_ref.shape
    load = pltpu.make_async_copy(q_hbm, q_ref, sem)
    load.start()
    hits = hits_ref[...]
    p_ref[...] = dot_nt(hits, r_ref[width:, :]) + dot_nt(hits, r_ref[0:width, :])
    load.wait()
    high, mid = split2(q_ref[...].T)
    qt_ref[:, 0:rows] = mid
    qt_ref[:, rows : 2 * rows] = high


def join(a, b):
    top = jnp.maximum(a[0:1], b[0:1])
    total = a[1:2] * jnp.exp(a[0:1] - top) + b[1:2] * jnp.exp(b[0:1] - top)
    return top, total, a[2:3] + b[2:3]


def join_kernel(a_ref, b_ref, after_ref, out_ref):
    top, total, own = join(a_ref[...], b_ref[...])
    out_ref[0:1, :] = top
    out_ref[1:2, :] = total
    out_ref[2:3, :] = own


def terms_kernel(a_ref, b_ref, first_ref, u_ref, p_ref, keep_ref, send_ref, loss_ref, scale_ref, scale_col):
    top, total, own = join(a_ref[...], b_ref[...])
    log_total = top + jnp.log(total)
    loss_ref[...] = (log_total - own).reshape(loss_ref.shape)
    scale = jnp.exp(first_ref[0:1, :] - log_total)
    scale_ref[...] = scale
    half = keep_ref.shape[0]
    scale_col[...] = column(scale).reshape(2, half, LANES)
    core = lax.axis_index("corpus") % 2
    keep_ref[...] = u_ref[core] * scale_col[core][:, 0:1] - p_ref[core]
    send_ref[...] = u_ref[1 - core] * scale_col[1 - core][:, 0:1] - p_ref[1 - core]


def book_kernel(
    e_ref, hits_ref, scale_ref, qt_ref, codes_ref, after_ref,
    keep_ref, send_ref, ws_ref, dg_ref, gt_ref, both_ref,
):
    rows, docs = e_ref.shape
    width, words = gt_ref.shape
    subs = codes_ref.shape[0]
    w = e_ref[...] * column(scale_ref[...])[:, 0:1] - hits_ref[...].astype(F32)
    wh, wm = split2(w)
    ws_ref[0:rows, :] = wh
    ws_ref[rows:, :] = wm
    dg_ref[...] = dot(qt_ref[...], ws_ref[...]) + dot(qt_ref[:, rows:], ws_ref[0:rows, :])
    coarse = words // FINE
    ramp = lax.broadcasted_iota(I32, (FINE, docs), 0).astype(F32).astype(BF16)
    for first in range(0, subs, 4):
        lhs, rhs = [], []
        for sub in range(first, first + 4):
            code = codes_ref[sub : sub + 1, :]
            value = dg_ref[8 * sub : 8 * sub + 8, :]
            high = value.astype(BF16).astype(F32)
            both = jnp.concatenate([high, value - high], axis=0).astype(BF16)
            outer = jnp.broadcast_to((code // FINE).astype(F32), (16, docs)).astype(BF16)
            lhs += [jnp.where(outer == jnp.bfloat16(b), both, jnp.zeros_like(both)) for b in range(coarse)]
            inner = jnp.broadcast_to((code & (FINE - 1)).astype(F32), (16, docs)).astype(BF16)
            inner = jnp.concatenate([inner] * (FINE // 16), axis=0)
            rhs.append(jnp.where(inner == ramp, jnp.ones_like(ramp), jnp.zeros_like(ramp)))
        out = dot_nt(jnp.concatenate(lhs, axis=0), jnp.concatenate(rhs, axis=0))
        for s in range(4):
            mine = out[16 * coarse * s : 16 * coarse * (s + 1), s * FINE : (s + 1) * FINE]
            parts = [mine[16 * b : 16 * b + 8, :] + mine[16 * b + 8 : 16 * b + 16, :] for b in range(coarse)]
            sub = first + s
            gt_ref[8 * sub : 8 * sub + 8, :] = jnp.concatenate(parts, axis=1)
    both_ref[...] = gt_ref[...].T.reshape(both_ref.shape)
    core = lax.axis_index("corpus") % 2
    keep_ref[...] = both_ref[core]
    send_ref[...] = both_ref[1 - core]


def call(kernel, outs, ins, scratch=(), flops=0, mib=16, name=None):
    return pl.pallas_call(
        kernel,
        out_shape=tuple(jax.ShapeDtypeStruct(shape, kind) for shape, kind in outs),
        in_specs=ins,
        out_specs=tuple(VMEM for _ in outs),
        scratch_shapes=list(scratch),
        compiler_params=pltpu.CompilerParams(vmem_limit_bytes=mib * 2**20),
        cost_estimate=pl.CostEstimate(flops=flops, bytes_accessed=2**17, transcendentals=0),
        name=name or kernel.__name__,
    )


def swap(x, axis, bits):
    return lax.ppermute(x, axis, [(i, i ^ bits) for i in range(lax.axis_size(axis))])


def place_of(axis, unit):
    return lax.axis_index(axis) // unit


def cut(keep, got, axis, unit, count, after, name):
    rows, width = keep.shape
    shape = (count, rows // count, width)

    def kernel(keep_ref, got_ref, after_ref, *outs):
        place = place_of(axis, unit)
        for k, out in enumerate(outs):
            out[...] = keep_ref[place ^ k] + got_ref[place ^ k]

    blocks = call(kernel, [(shape[1:], F32)] * count, [VMEM, VMEM, ANY], mib=4, name=name)(
        keep.reshape(shape), got.reshape(shape), after
    )
    return list(blocks)


def add(pieces, after, name):
    def kernel(*refs):
        total = refs[0][...]
        for ref in refs[1:-2]:
            total = total + ref[...]
        refs[-1][...] = total

    return call(kernel, [(pieces[0].shape, F32)], [VMEM] * len(pieces) + [ANY], mib=4, name=name)(*pieces, after)[0]


def put(pieces, axis, unit, name):
    rows, width = pieces[0].shape

    def kernel(*refs):
        place = place_of(axis, unit)
        for k, ref in enumerate(refs[:-1]):
            refs[-1][place ^ k] = ref[...]

    count = len(pieces)
    whole = call(kernel, [((count, rows, width), F32)], [VMEM] * count, mib=4, name=name)(*pieces)[0]
    return whole.reshape(count * rows, width)


def finish(own, got, name):
    rows, width = own.shape

    def kernel(own_ref, got_ref, out_hbm, sems):
        core = lax.axis_index("corpus") % 2
        copies = [
            pltpu.make_async_copy(own_ref, out_hbm.at[core], sems.at[0]),
            pltpu.make_async_copy(got_ref, out_hbm.at[1 - core], sems.at[1]),
        ]
        for copy in copies:
            copy.start()
        for copy in copies:
            copy.wait()

    whole = pl.pallas_call(
        kernel,
        out_shape=jax.ShapeDtypeStruct((2, rows, width), F32),
        in_specs=[VMEM, VMEM],
        out_specs=ANY,
        scratch_shapes=[pltpu.SemaphoreType.DMA((2,))],
        compiler_params=pltpu.CompilerParams(vmem_limit_bytes=4 * 2**20),
        name=name,
    )(own, got)
    return whole.reshape(2 * rows, width)


def local(queries, codes, positive, codebook):
    rows, width = queries.shape
    docs, subs = codes.shape
    words = codebook.shape[0]
    corpus, query = lax.axis_size("corpus"), lax.axis_size("query")
    chips = corpus // 2
    codes_t = codes.T
    work = rows * docs * width
    e, hits, r, stats = call(
        score_kernel,
        [((rows, docs), F32), ((rows, docs), BF16), ((2 * width, docs), BF16), ((8, rows), F32)],
        [ANY] * 4,
        [
            pltpu.VMEM((rows, width), F32),
            pltpu.VMEM((subs, docs), I32),
            pltpu.VMEM((words, width), F32),
            pltpu.VMEM((rows,), I32),
            pltpu.VMEM((rows, 3 * width), BF16),
            pltpu.VMEM((rows, docs), F32),
            pltpu.VMEM((width, docs), BF16),
            pltpu.VMEM((width, words), F32),
            pltpu.SemaphoreType.DMA((4,)),
        ],
        12 * work,
        24,
    )(queries, codes_t, codebook, positive)
    u = call(spread_kernel, [((rows, width), F32)], [VMEM] * 2, (), 6 * work)(e, r)[0]
    joined, got, bits, after = stats, swap(stats, "corpus", 1), 2, stats
    while bits < corpus:
        joined = call(join_kernel, [((8, rows), F32)], [VMEM] * 3, mib=4)(joined, got, after)[0]
        got = swap(joined, "corpus", bits)
        after = u
        bits *= 2
    p, qt = call(
        positive_kernel,
        [((rows, width), F32), ((width, 2 * rows), BF16)],
        [VMEM, VMEM, ANY, VMEM],
        [pltpu.VMEM((rows, width), F32), pltpu.SemaphoreType.DMA],
        4 * work,
    )(hits, r, queries, joined)
    half = rows // 2
    keep, send, loss, scale = call(
        terms_kernel,
        [((half, width), F32), ((half, width), F32), ((rows,), F32), ((1, rows), F32)],
        [VMEM] * 5,
        [pltpu.VMEM((2, half, LANES), F32)],
        mib=8,
    )(joined, got, stats, u.reshape(2, half, width), p.reshape(2, half, width))

    cuts = cut(keep, swap(send, "corpus", 1), "corpus", 2, chips, scale, "query_cut")
    got = [swap(cuts[k], "corpus", 2 * k) for k in range(1, chips)]

    part_rows = words // 2
    book_keep, book_send = call(
        book_kernel,
        [((part_rows, width), F32)] * 2,
        [VMEM] * 6,
        [
            pltpu.VMEM((2 * rows, docs), BF16),
            pltpu.VMEM((width, docs), F32),
            pltpu.VMEM((width, words), F32),
            pltpu.VMEM((2, part_rows, width), F32),
        ],
        14 * work,
    )(e, hits, scale, qt, codes_t, cuts[0])

    own = add([cuts[0]] + got, scale, "query_sum")
    blocks = [own] + [swap(own, "corpus", 2 * k) for k in range(1, chips)]
    whole = put(blocks, "corpus", 2, "query_put")
    grad_queries = finish(whole, swap(whole, "corpus", 1), "query_finish")

    cuts = cut(book_keep, swap(book_send, "corpus", 1), "query", 1, query, scale, "book_cut")
    got = [swap(cuts[k], "query", k) for k in range(1, query)]
    own = add([cuts[0]] + got, scale, "book_sum")
    bits = 2
    while bits < corpus:
        own = add([own, swap(own, "corpus", bits)], scale, "book_join")
        bits *= 2
    blocks = [own] + [swap(own, "query", k) for k in range(1, query)]
    whole = put(blocks, "query", 1, "book_put")
    grad_codebook = finish(whole, swap(whole, "corpus", 1), "book_finish")
    return grad_queries, grad_codebook, loss


def solution(mesh):
    placed = (P("query", None), P("corpus", None), P("query"), P())
    return jax.shard_map(
        local,
        mesh=mesh,
        in_specs=placed,
        out_specs=(P("query", None), P(), P("query")),
        check_vma=False,
    )
```

time: 306 us -> 80.9 us (0.26); the launches traced: 302 us -> 80.7 us
  matrix products: 120 us -> 0 us
  waiting for transfers between devices: 108 us -> 27.9 us
  blocking collectives: 50 us -> 0 us
  starting transfers between devices: 0.29 us -> 27 us
  Pallas kernels: 0 us -> 20.7 us
  between operations: 14.1 us -> 0.95 us
  local copies, waits for them, and re-layouts: 8.65 us -> 4.08 us
    dot_general x27 -> x0, matrix products: 120 us -> none  [the longest x12 60.8 us: local(): jnp.einsum('jmk,kmc->jmc', table, book_part, precision=precise, preferred...]
    psum x2 -> x0, waiting for transfers between devices: 77.7 us -> none  [the longest x1 45.4 us: local(): grad_queries = lax.psum(query_terms, 'corpus')]
    reduce_scatter x1 -> x0, waiting for transfers between devices: 29.9 us -> none  [local(): lax.psum_scatter(local_codebook, 'corpus', scatter_dimension=0, tiled=True)]
    ppermute x0 -> x21, waiting for transfers between devices: none -> 27.9 us  [swap(): lax.ppermute(x, axis, [(i, i ^ bits) for i in range(lax.axis_size(axis))])]
    ppermute x0 -> x21, starting transfers between devices: none -> 27 us  [swap(): lax.ppermute(x, axis, [(i, i ^ bits) for i in range(lax.axis_size(axis))])]
    pallas_call x0 -> x17, Pallas kernels: none -> 20.7 us  [the longest x1 7.17 us: local(): call(score_kernel, [((rows, docs), F32), ((rows, docs), BF16), ((2 * widt...]
    all_gather x1 -> x0, blocking collectives: 18.2 us -> none  [local(): grad_codebook = lax.all_gather(codebook_part, 'corpus', axis=0, tiled=True)]
    pmax x1 -> x0, blocking collectives: 18.1 us -> none  [local(): row_top = lax.pmax(local_top, 'corpus')]
  transfers between devices with their start and end apart: 3 -> 21, of which waited for: 3 -> 10; matrix products, arithmetic and copies ran while one was open for 4% -> 0% of each run, Pallas kernels for 0% -> 7%
where the time goes in v2:
time: 80.9 us; the launch traced here: 80.7 us
  waiting for transfers between devices  27.9 us (34%)
  starting transfers between devices  27 us (33%)
  Pallas kernels  20.7 us (26%)
  local copies, waits for them, and re-layouts  4.08 us (5%)
  between operations  0.95 us (1%)
    ppermute x21, waiting for transfers between devices, swap(): lax.ppermute(x, axis, [(i, i ^ bits) for i in range(lax.axis_size(axis))])  27.9 us
    ppermute x21, starting transfers between devices, swap(): lax.ppermute(x, axis, [(i, i ^ bits) for i in range(lax.axis_size(axis))])  27 us
    pallas_call x1, Pallas kernels, local(): call(score_kernel, [((rows, docs), F32), ((rows, docs), BF16), ((2 * widt...  7.17 us
    pallas_call x1, Pallas kernels, local(): call(book_kernel, [((part_rows, width), F32)] * 2, [VMEM] * 6, [pltpu.VME...  6.07 us
    unnamed x10, local copies, waits for them, and re-layouts  4.08 us
    pallas_call x1, Pallas kernels, local(): call(positive_kernel, [((rows, width), F32), ((width, 2 * rows), BF16)],...  2.22 us
    pallas_call x1, Pallas kernels, local(): call(spread_kernel, [((rows, width), F32)], [VMEM] * 2, (), 6 * work)(e, r)  2.05 us
    pallas_call x2, Pallas kernels, finish(): pl.pallas_call(kernel, out_shape=jax.ShapeDtypeStruct((2, rows, width), F...  1.93 us
  transfers between devices with their start and end apart: 21, of which 10 were waited for; matrix products, arithmetic and copies ran while one was open for 0% of the time, Pallas kernels for 7%

profile of v2, /device:TPU:0, one launch (start us, length us, event | category | flops | bytes accessed | tf_op | source)
XLA Modules:
  0.0 80.7 jit_solution(1650601425174491932)
XLA Ops:
  0.6 0.0 copy-start
  0.6 1.3 %copy-done = f32[384,768]{1,0:T(8,128)S(1)} copy-done((f32[384,768]{1,0:T(8,128)S(1)}, f32[384,768]{1,0:T(8,128)}, u32[]{:S(2)}) %copy-start) | copy-done | bytes 1179672
  1.9 0.0 copy-start.2
  1.9 1.1 %copy-done.2 = f32[256,768]{1,0:T(8,128)S(1)} copy-done((f32[256,768]{1,0:T(8,128)S(1)}, f32[256,768]{1,0:T(8,128)}, u32[]{:S(2)}) %copy-start.2) | copy-done | bytes 786456
  3.0 0.0 copy-start.3
  3.0 1.0 %copy-done.3 = s32[1024,96]{0,1:T(8,128)S(1)} copy-done((s32[1024,96]{0,1:T(8,128)S(1)}, s32[1024,96]{0,1:T(8,128)}, u32[]{:S(2)}) %copy-start.3) | copy-done | bytes 393240
  4.0 0.0 copy-start.4
  4.0 0.7 copy-done.4
  4.7 7.2 %score_kernel.1 = (f32[384,1024]{1,0:T(8,128)S(1)}, bf16[384,1024]{1,0:T(8,128)(2,1)S(1)}, bf16[1536,1024]{1,0:T(8,128)(2,1)S(1)}, f32[8,384]{1,0:T(8,128)S(1)}) custom-call(f32[384,768]{1,0:T(8,128)S(1)} %copy-done, s32[96,1024]{1,0:T(8,128)S(1)} %bitcast.21, f32[256,768]{1,0:T(8,128)S(1)} %copy-done.2, s32[384]{0:T(512)S(1)} %copy-done.4), custom_call_target="tpu_custom_call" | custom-call | flops 3623878656 | bytes 131072 | tf_op jit(solution)/shard_map/score_kernel/pallas_call | solution.py:286
  11.9 0.5 collective-permute-start
  12.4 0.8 %collective-permute-done.b_ref = f32[8,384]{1,0:T(8,128)S(1)} collective-permute-done((f32[8,384]{1,0:T(8,128)S(1)}, f32[8,384]{1,0:T(8,128)S(1)}, u32[]{:S(2)}, u32[]{:S(2)}) %collective-permute-start) | collective-permute-done | bytes 12320 | tf_op jit(solution)/shard_map/ppermute | solution.py:207
  13.3 3.0 %collective-permute-start.1 = (f32[8,384]{1,0:T(8,128)S(1)}, f32[8,384]{1,0:T(8,128)S(1)}, u32[]{:S(2)}, u32[]{:S(2)}) collective-permute-start(f32[8,384]{1,0:T(8,128)S(1)} %join_kernel.2.a_ref), channel_id=1, source_target_pairs={{0,2},{1,3},{2,0},{3,1},{4,6},{5,7},{6,4},{7,5},{8,10},{9,11},{10,... | collective-permute-start | bytes 36872 | tf_op jit(solution)/shard_map/ppermute | solution.py:207
  16.2 2.1 %spread_kernel.1.after_ref = f32[384,768]{1,0:T(8,128)S(1)} custom-call(f32[384,1024]{1,0:T(8,128)S(1)} %get-tuple-element.24.e_ref, bf16[1536,1024]{1,0:T(8,128)(2,1)S(1)} %get-tuple-element.25.r_ref), custom_call_target="tpu_custom_call" | custom-call | flops 1811939328 | bytes 131072 | tf_op jit(solution)/shard_map/spread_kernel/pallas_call | solution.py:304
  18.3 0.0 copy-start.1
  18.3 0.0 collective-permute-done.1.b_ref
  18.4 2.7 %collective-permute-start.2 = (f32[8,384]{1,0:T(8,128)S(1)}, f32[8,384]{1,0:T(8,128)S(1)}, u32[]{:S(2)}, u32[]{:S(2)}) collective-permute-start(f32[8,384]{1,0:T(8,128)S(1)} %join_kernel.3.after_ref.a_ref), channel_id=1, source_target_pairs={{0,4},{1,5},{2,6},{3,7},{4,0},{5,1},{6,2},{7,3},{8,12},{9,13},{10,... | collective-permute-start | bytes 36872 | tf_op jit(solution)/shard_map/ppermute | solution.py:207
  21.0 0.0 copy-done.1
  21.0 2.2 %positive_kernel.1 = (f32[384,768]{1,0:T(8,128)S(1)}, bf16[768,768]{1,0:T(8,128)(2,1)S(1)}) custom-call(bf16[384,1024]{1,0:T(8,128)(2,1)S(1)} %get-tuple-element.26.hits_ref, bf16[1536,1024]{1,0:T(8,128)(2,1)S(1)} %get-tuple-element.25.r_ref, f32[384,768]{1,0:T(8,128)S(1)} %copy-done.1, f32[8,384]{1,0:T(8,128)S(1)} %join_kernel.3.after_ref.a_ref), custom_call_target="tpu_custom_call" | custom-call | flops 1207959552 | bytes 131072 | tf_op jit(solution)/shard_map/positive_kernel/pallas_call | solution.py:311
  23.3 0.0 collective-permute-done.2.b_ref
  23.3 0.9 %terms_kernel.1 = (f32[192,768]{1,0:T(8,128)S(1)}, f32[192,768]{1,0:T(8,128)S(1)}, f32[384]{0:T(512)}, f32[1,384]{1,0:T(1,128)S(1)}) custom-call(f32[8,384]{1,0:T(8,128)S(1)} %join_kernel.3.after_ref.a_ref, f32[8,384]{1,0:T(8,128)S(1)} %collective-permute-done.2.b_ref, f32[8,384]{1,0:T(8,128)S(1)} %get-tuple-element.23.a_ref.after_ref.first_ref, ...), custom_call_target="tpu_custom_call" | custom-call | bytes 131072 | tf_op jit(solution)/shard_map/terms_kernel/pallas_call | solution.py:319
  24.2 0.0 collective-permute-start.3
  24.2 2.0 %collective-permute-done.3 = f32[192,768]{1,0:T(8,128)S(1)} collective-permute-done((f32[192,768]{1,0:T(8,128)S(1)}, f32[192,768]{1,0:T(8,128)S(1)}, u32[]{:S(2)}, u32[]{:S(2)}) %collective-permute-start.3) | collective-permute-done | bytes 589856 | tf_op jit(solution)/shard_map/ppermute | solution.py:207
  26.2 0.1 query_cut.1
  26.3 6.1 %book_kernel.1 = (f32[128,768]{1,0:T(8,128)S(1)}, f32[128,768]{1,0:T(8,128)S(1)}) custom-call(f32[384,1024]{1,0:T(8,128)S(1)} %get-tuple-element.24.e_ref, bf16[384,1024]{1,0:T(8,128)(2,1)S(1)} %get-tuple-element.26.hits_ref, f32[1,384]{1,0:T(1,128)S(1)} %get-tuple-element.30.after_ref.refs_4_.scale_ref.refs_2_, ...), custom_call_target="tpu_custom_call" | custom-call | flops 4227858432 | bytes 131072 | tf_op jit(solution)/shard_map/book_kernel/pallas_call | solution.py:331
  32.3 0.2 collective-permute-start.11
  32.5 1.6 %collective-permute-start.4 = (f32[48,768]{1,0:T(8,128)S(1)}, f32[48,768]{1,0:T(8,128)S(1)}, u32[]{:S(2)}, u32[]{:S(2)}) collective-permute-start(f32[48,768]{1,0:T(8,128)S(1)} %get-tuple-element.32), channel_id=1, source_target_pairs={{0,2},{1,3},{2,0},{3,1},{4,6},{5,7},{6,4},{7,5},{8,10},{9,11},{10,... | collective-permute-start | bytes 442376 | tf_op jit(solution)/shard_map/ppermute | solution.py:207
  34.1 2.4 %collective-permute-start.5 = (f32[48,768]{1,0:T(8,128)S(1)}, f32[48,768]{1,0:T(8,128)S(1)}, u32[]{:S(2)}, u32[]{:S(2)}) collective-permute-start(f32[48,768]{1,0:T(8,128)S(1)} %get-tuple-element.33), channel_id=1, source_target_pairs={{0,4},{1,5},{2,6},{3,7},{4,0},{5,1},{6,2},{7,3},{8,12},{9,13},{10,... | collective-permute-start | bytes 442376 | tf_op jit(solution)/shard_map/ppermute | solution.py:207
  36.5 0.4 collective-permute-start.6
  36.9 0.0 collective-permute-done.11
  37.0 1.6 %collective-permute-start.12 = (f32[32,768]{1,0:T(8,128)S(1)}, f32[32,768]{1,0:T(8,128)S(1)}, u32[]{:S(2)}, u32[]{:S(2)}) collective-permute-start(f32[32,768]{1,0:T(8,128)S(1)} %get-tuple-element.39), channel_id=1, source_target_pairs={{0,8},{8,0},{16,24},{24,16},{1,9},{9,1},{17,25},{25,17},{2,10},{10... | collective-permute-start | bytes 294920 | tf_op jit(solution)/shard_map/ppermute | solution.py:207
  38.5 1.5 %collective-permute-start.13 = (f32[32,768]{1,0:T(8,128)S(1)}, f32[32,768]{1,0:T(8,128)S(1)}, u32[]{:S(2)}, u32[]{:S(2)}) collective-permute-start(f32[32,768]{1,0:T(8,128)S(1)} %get-tuple-element.40), channel_id=1, source_target_pairs={{0,16},{8,24},{16,0},{24,8},{1,17},{9,25},{17,1},{25,9},{2,18},{10... | collective-permute-start | bytes 294920 | tf_op jit(solution)/shard_map/ppermute | solution.py:207
  40.1 1.1 %collective-permute-done.4.refs_1_ = f32[48,768]{1,0:T(8,128)S(1)} collective-permute-done((f32[48,768]{1,0:T(8,128)S(1)}, f32[48,768]{1,0:T(8,128)S(1)}, u32[]{:S(2)}, u32[]{:S(2)}) %collective-permute-start.4) | collective-permute-done | bytes 147488 | tf_op jit(solution)/shard_map/ppermute | solution.py:207
  41.2 2.5 %collective-permute-start.14 = (f32[32,768]{1,0:T(8,128)S(1)}, f32[32,768]{1,0:T(8,128)S(1)}, u32[]{:S(2)}, u32[]{:S(2)}) collective-permute-start(f32[32,768]{1,0:T(8,128)S(1)} %get-tuple-element.41), channel_id=1, source_target_pairs={{0,24},{8,16},{16,8},{24,0},{1,25},{9,17},{17,9},{25,1},{2,26},{10... | collective-permute-start | bytes 294920 | tf_op jit(solution)/shard_map/ppermute | solution.py:207
  43.7 4.4 %collective-permute-done.5.refs_2_ = f32[48,768]{1,0:T(8,128)S(1)} collective-permute-done((f32[48,768]{1,0:T(8,128)S(1)}, f32[48,768]{1,0:T(8,128)S(1)}, u32[]{:S(2)}, u32[]{:S(2)}) %collective-permute-start.5) | collective-permute-done | bytes 147488 | tf_op jit(solution)/shard_map/ppermute | solution.py:207
  48.1 0.0 collective-permute-done.6.refs_3_
  48.1 2.3 %collective-permute-start.9 = (f32[48,768]{1,0:T(8,128)S(1)}, f32[48,768]{1,0:T(8,128)S(1)}, u32[]{:S(2)}, u32[]{:S(2)}) collective-permute-start(f32[48,768]{1,0:T(8,128)S(1)} %query_sum.1.refs_0_), channel_id=1, source_target_pairs={{0,6},{1,7},{2,4},{3,5},{4,2},{5,3},{6,0},{7,1},{8,14},{9,15},{10,... | collective-permute-start | bytes 442376 | tf_op jit(solution)/shard_map/ppermute | solution.py:207
  50.4 2.1 %collective-permute-start.8 = (f32[48,768]{1,0:T(8,128)S(1)}, f32[48,768]{1,0:T(8,128)S(1)}, u32[]{:S(2)}, u32[]{:S(2)}) collective-permute-start(f32[48,768]{1,0:T(8,128)S(1)} %query_sum.1.refs_0_), channel_id=1, source_target_pairs={{0,4},{1,5},{2,6},{3,7},{4,0},{5,1},{6,2},{7,3},{8,12},{9,13},{10,... | collective-permute-start | bytes 442376 | tf_op jit(solution)/shard_map/ppermute | solution.py:207
  52.5 0.0 collective-permute-done.12.refs_1_
  52.5 0.1 collective-permute-start.7
  52.6 0.0 collective-permute-done.13.refs_2_
  52.6 0.0 collective-permute-done.14.refs_3_
  52.6 2.0 %collective-permute-start.15 = (f32[32,768]{1,0:T(8,128)S(1)}, f32[32,768]{1,0:T(8,128)S(1)}, u32[]{:S(2)}, u32[]{:S(2)}) collective-permute-start(f32[32,768]{1,0:T(8,128)S(1)} %book_sum.1.refs_0_), channel_id=1, source_target_pairs={{0,2},{1,3},{2,0},{3,1},{4,6},{5,7},{6,4},{7,5},{8,10},{9,11},{10,... | collective-permute-start | bytes 294920 | tf_op jit(solution)/shard_map/ppermute | solution.py:207
  54.6 9.0 %collective-permute-done.15.refs_1_ = f32[32,768]{1,0:T(8,128)S(1)} collective-permute-done((f32[32,768]{1,0:T(8,128)S(1)}, f32[32,768]{1,0:T(8,128)S(1)}, u32[]{:S(2)}, u32[]{:S(2)}) %collective-permute-start.15) | collective-permute-done | bytes 98336 | tf_op jit(solution)/shard_map/ppermute | solution.py:207
  63.7 0.6 collective-permute-start.16
  64.3 0.0 collective-permute-done.9.refs_3_
  64.3 0.0 collective-permute-done.8.refs_2_
  64.3 0.0 collective-permute-done.7.refs_1_
  64.3 0.1 query_put.1
  64.3 0.1 collective-permute-start.10
  64.4 5.7 %collective-permute-done.16.refs_1_ = f32[32,768]{1,0:T(8,128)S(1)} collective-permute-done((f32[32,768]{1,0:T(8,128)S(1)}, f32[32,768]{1,0:T(8,128)S(1)}, u32[]{:S(2)}, u32[]{:S(2)}) %collective-permute-start.16) | collective-permute-done | bytes 98336 | tf_op jit(solution)/shard_map/ppermute | solution.py:207
  70.1 2.5 %collective-permute-start.19 = (f32[32,768]{1,0:T(8,128)S(1)}, f32[32,768]{1,0:T(8,128)S(1)}, u32[]{:S(2)}, u32[]{:S(2)}) collective-permute-start(f32[32,768]{1,0:T(8,128)S(1)} %book_join.3.refs_0_), channel_id=1, source_target_pairs={{0,24},{8,16},{16,8},{24,0},{1,25},{9,17},{17,9},{25,1},{2,26},{10... | collective-permute-start | bytes 294920 | tf_op jit(solution)/shard_map/ppermute | solution.py:207
  72.7 0.5 collective-permute-start.18
  73.2 0.5 collective-permute-start.17
  73.7 2.0 %collective-permute-done.19.refs_3_ = f32[32,768]{1,0:T(8,128)S(1)} collective-permute-done((f32[32,768]{1,0:T(8,128)S(1)}, f32[32,768]{1,0:T(8,128)S(1)}, u32[]{:S(2)}, u32[]{:S(2)}) %collective-permute-start.19) | collective-permute-done | bytes 98336 | tf_op jit(solution)/shard_map/ppermute | solution.py:207
  75.7 1.6 %collective-permute-done.18.refs_2_ = f32[32,768]{1,0:T(8,128)S(1)} collective-permute-done((f32[32,768]{1,0:T(8,128)S(1)}, f32[32,768]{1,0:T(8,128)S(1)}, u32[]{:S(2)}, u32[]{:S(2)}) %collective-permute-start.18) | collective-permute-done | bytes 98336 | tf_op jit(solution)/shard_map/ppermute | solution.py:207
  77.3 0.5 collective-permute-done.17.refs_1_
  77.8 0.1 collective-permute-start.20
  77.9 0.0 collective-permute-done.10.got_ref
  77.9 1.0 %query_finish.1 = f32[2,192,768]{2,1,0:T(8,128)} custom-call(f32[192,768]{1,0:T(8,128)S(1)} %bitcast.13, f32[192,768]{1,0:T(8,128)S(1)} %collective-permute-done.10.got_ref), custom_call_target="tpu_custom_call" | custom-call | tf_op jit(solution)/shard_map/query_finish/pallas_call | solution.py:266
  79.0 0.7 collective-permute-done.20.got_ref
  79.6 0.9 %book_finish.1 = f32[2,128,768]{2,1,0:T(8,128)} custom-call(f32[128,768]{1,0:T(8,128)S(1)} %bitcast.15, f32[128,768]{1,0:T(8,128)S(1)} %collective-permute-done.20.got_ref), custom_call_target="tpu_custom_call" | custom-call | tf_op jit(solution)/shard_map/book_finish/pallas_call | solution.py:266
  (8 shorter events, 0.2 us)
Async XLA Ops:
  0.6 1.3 %copy-start = (f32[384,768]{1,0:T(8,128)S(1)}, f32[384,768]{1,0:T(8,128)}, u32[]{:S(2)}) copy-start(f32[384,768]{1,0:T(8,128)} %q_hbm.3) | copy-start | bytes 3538948
  1.9 1.1 %copy-start.2 = (f32[256,768]{1,0:T(8,128)S(1)}, f32[256,768]{1,0:T(8,128)}, u32[]{:S(2)}) copy-start(f32[256,768]{1,0:T(8,128)} %book_hbm.1) | copy-start | bytes 2359300
  3.0 1.0 %copy-start.3 = (s32[1024,96]{0,1:T(8,128)S(1)}, s32[1024,96]{0,1:T(8,128)}, u32[]{:S(2)}) copy-start(s32[1024,96]{0,1:T(8,128)} %param.5) | copy-start | bytes 1179652
  4.0 0.7 copy-start.4
  11.9 1.4 %collective-permute-start = (f32[8,384]{1,0:T(8,128)S(1)}, f32[8,384]{1,0:T(8,128)S(1)}, u32[]{:S(2)}, u32[]{:S(2)}) collective-permute-start(f32[8,384]{1,0:T(8,128)S(1)} %get-tuple-element.23.a_ref.after_ref.first_ref), channel_id=1, source_target_pairs={{0,1},{1,0},{2,3},{3,2},{4,5},{5,4},{6,7},{7,6},{8,9},{9,8},{10,11... | collective-permute-start | bytes 36872 | tf_op jit(solution)/shard_map/ppermute | solution.py:207
  13.3 5.1 %collective-permute-start.1 = (f32[8,384]{1,0:T(8,128)S(1)}, f32[8,384]{1,0:T(8,128)S(1)}, u32[]{:S(2)}, u32[]{:S(2)}) collective-permute-start(f32[8,384]{1,0:T(8,128)S(1)} %join_kernel.2.a_ref), channel_id=1, source_target_pairs={{0,2},{1,3},{2,0},{3,1},{4,6},{5,7},{6,4},{7,5},{8,10},{9,11},{10,... | collective-permute-start | bytes 36872 | tf_op jit(solution)/shard_map/ppermute | solution.py:207
  18.3 2.7 %copy-start.1 = (f32[384,768]{1,0:T(8,128)S(1)}, f32[384,768]{1,0:T(8,128)}, u32[]{:S(2)}) copy-start(f32[384,768]{1,0:T(8,128)} %q_hbm.3) | copy-start | bytes 3538948
  18.4 4.9 %collective-permute-start.2 = (f32[8,384]{1,0:T(8,128)S(1)}, f32[8,384]{1,0:T(8,128)S(1)}, u32[]{:S(2)}, u32[]{:S(2)}) collective-permute-start(f32[8,384]{1,0:T(8,128)S(1)} %join_kernel.3.after_ref.a_ref), channel_id=1, source_target_pairs={{0,4},{1,5},{2,6},{3,7},{4,0},{5,1},{6,2},{7,3},{8,12},{9,13},{10,... | collective-permute-start | bytes 36872 | tf_op jit(solution)/shard_map/ppermute | solution.py:207
  24.2 2.0 %collective-permute-start.3 = (f32[192,768]{1,0:T(8,128)S(1)}, f32[192,768]{1,0:T(8,128)S(1)}, u32[]{:S(2)}, u32[]{:S(2)}) collective-permute-start(f32[192,768]{1,0:T(8,128)S(1)} %get-tuple-element.29), channel_id=1, source_target_pairs={{0,1},{1,0},{2,3},{3,2},{4,5},{5,4},{6,7},{7,6},{8,9},{9,8},{10,11... | collective-permute-start | bytes 1769480 | tf_op jit(solution)/shard_map/ppermute | solution.py:207
  32.3 4.6 %collective-permute-start.11 = (f32[128,768]{1,0:T(8,128)S(1)}, f32[128,768]{1,0:T(8,128)S(1)}, u32[]{:S(2)}, u32[]{:S(2)}) collective-permute-start(f32[128,768]{1,0:T(8,128)S(1)} %get-tuple-element.37), channel_id=1, source_target_pairs={{0,1},{1,0},{2,3},{3,2},{4,5},{5,4},{6,7},{7,6},{8,9},{9,8},{10,11... | collective-permute-start | bytes 1179656 | tf_op jit(solution)/shard_map/ppermute | solution.py:207
  32.5 8.7 %collective-permute-start.4 = (f32[48,768]{1,0:T(8,128)S(1)}, f32[48,768]{1,0:T(8,128)S(1)}, u32[]{:S(2)}, u32[]{:S(2)}) collective-permute-start(f32[48,768]{1,0:T(8,128)S(1)} %get-tuple-element.32), channel_id=1, source_target_pairs={{0,2},{1,3},{2,0},{3,1},{4,6},{5,7},{6,4},{7,5},{8,10},{9,11},{10,... | collective-permute-start | bytes 442376 | tf_op jit(solution)/shard_map/ppermute | solution.py:207
  34.1 14.0 %collective-permute-start.5 = (f32[48,768]{1,0:T(8,128)S(1)}, f32[48,768]{1,0:T(8,128)S(1)}, u32[]{:S(2)}, u32[]{:S(2)}) collective-permute-start(f32[48,768]{1,0:T(8,128)S(1)} %get-tuple-element.33), channel_id=1, source_target_pairs={{0,4},{1,5},{2,6},{3,7},{4,0},{5,1},{6,2},{7,3},{8,12},{9,13},{10,... | collective-permute-start | bytes 442376 | tf_op jit(solution)/shard_map/ppermute | solution.py:207
  36.5 11.6 %collective-permute-start.6 = (f32[48,768]{1,0:T(8,128)S(1)}, f32[48,768]{1,0:T(8,128)S(1)}, u32[]{:S(2)}, u32[]{:S(2)}) collective-permute-start(f32[48,768]{1,0:T(8,128)S(1)} %get-tuple-element.34), channel_id=1, source_target_pairs={{0,6},{1,7},{2,4},{3,5},{4,2},{5,3},{6,0},{7,1},{8,14},{9,15},{10,... | collective-permute-start | bytes 442376 | tf_op jit(solution)/shard_map/ppermute | solution.py:207
  37.0 15.5 %collective-permute-start.12 = (f32[32,768]{1,0:T(8,128)S(1)}, f32[32,768]{1,0:T(8,128)S(1)}, u32[]{:S(2)}, u32[]{:S(2)}) collective-permute-start(f32[32,768]{1,0:T(8,128)S(1)} %get-tuple-element.39), channel_id=1, source_target_pairs={{0,8},{8,0},{16,24},{24,16},{1,9},{9,1},{17,25},{25,17},{2,10},{10... | collective-permute-start | bytes 294920 | tf_op jit(solution)/shard_map/ppermute | solution.py:207
  38.5 14.0 %collective-permute-start.13 = (f32[32,768]{1,0:T(8,128)S(1)}, f32[32,768]{1,0:T(8,128)S(1)}, u32[]{:S(2)}, u32[]{:S(2)}) collective-permute-start(f32[32,768]{1,0:T(8,128)S(1)} %get-tuple-element.40), channel_id=1, source_target_pairs={{0,16},{8,24},{16,0},{24,8},{1,17},{9,25},{17,1},{25,9},{2,18},{10... | collective-permute-start | bytes 294920 | tf_op jit(solution)/shard_map/ppermute | solution.py:207
  41.2 11.4 %collective-permute-start.14 = (f32[32,768]{1,0:T(8,128)S(1)}, f32[32,768]{1,0:T(8,128)S(1)}, u32[]{:S(2)}, u32[]{:S(2)}) collective-permute-start(f32[32,768]{1,0:T(8,128)S(1)} %get-tuple-element.41), channel_id=1, source_target_pairs={{0,24},{8,16},{16,8},{24,0},{1,25},{9,17},{17,9},{25,1},{2,26},{10... | collective-permute-start | bytes 294920 | tf_op jit(solution)/shard_map/ppermute | solution.py:207
  48.1 16.1 %collective-permute-start.9 = (f32[48,768]{1,0:T(8,128)S(1)}, f32[48,768]{1,0:T(8,128)S(1)}, u32[]{:S(2)}, u32[]{:S(2)}) collective-permute-start(f32[48,768]{1,0:T(8,128)S(1)} %query_sum.1.refs_0_), channel_id=1, source_target_pairs={{0,6},{1,7},{2,4},{3,5},{4,2},{5,3},{6,0},{7,1},{8,14},{9,15},{10,... | collective-permute-start | bytes 442376 | tf_op jit(solution)/shard_map/ppermute | solution.py:207
  50.4 13.8 %collective-permute-start.8 = (f32[48,768]{1,0:T(8,128)S(1)}, f32[48,768]{1,0:T(8,128)S(1)}, u32[]{:S(2)}, u32[]{:S(2)}) collective-permute-start(f32[48,768]{1,0:T(8,128)S(1)} %query_sum.1.refs_0_), channel_id=1, source_target_pairs={{0,4},{1,5},{2,6},{3,7},{4,0},{5,1},{6,2},{7,3},{8,12},{9,13},{10,... | collective-permute-start | bytes 442376 | tf_op jit(solution)/shard_map/ppermute | solution.py:207
  52.5 11.8 %collective-permute-start.7 = (f32[48,768]{1,0:T(8,128)S(1)}, f32[48,768]{1,0:T(8,128)S(1)}, u32[]{:S(2)}, u32[]{:S(2)}) collective-permute-start(f32[48,768]{1,0:T(8,128)S(1)} %query_sum.1.refs_0_), channel_id=1, source_target_pairs={{0,2},{1,3},{2,0},{3,1},{4,6},{5,7},{6,4},{7,5},{8,10},{9,11},{10,... | collective-permute-start | bytes 442376 | tf_op jit(solution)/shard_map/ppermute | solution.py:207
  52.6 11.0 %collective-permute-start.15 = (f32[32,768]{1,0:T(8,128)S(1)}, f32[32,768]{1,0:T(8,128)S(1)}, u32[]{:S(2)}, u32[]{:S(2)}) collective-permute-start(f32[32,768]{1,0:T(8,128)S(1)} %book_sum.1.refs_0_), channel_id=1, source_target_pairs={{0,2},{1,3},{2,0},{3,1},{4,6},{5,7},{6,4},{7,5},{8,10},{9,11},{10,... | collective-permute-start | bytes 294920 | tf_op jit(solution)/shard_map/ppermute | solution.py:207
  63.7 6.5 %collective-permute-start.16 = (f32[32,768]{1,0:T(8,128)S(1)}, f32[32,768]{1,0:T(8,128)S(1)}, u32[]{:S(2)}, u32[]{:S(2)}) collective-permute-start(f32[32,768]{1,0:T(8,128)S(1)} %book_join.2.refs_0_), channel_id=1, source_target_pairs={{0,4},{1,5},{2,6},{3,7},{4,0},{5,1},{6,2},{7,3},{8,12},{9,13},{10,... | collective-permute-start | bytes 294920 | tf_op jit(solution)/shard_map/ppermute | solution.py:207
  64.3 13.6 %collective-permute-start.10 = (f32[192,768]{1,0:T(8,128)S(1)}, f32[192,768]{1,0:T(8,128)S(1)}, u32[]{:S(2)}, u32[]{:S(2)}) collective-permute-start(f32[192,768]{1,0:T(8,128)S(1)} %bitcast.12), channel_id=1, source_target_pairs={{0,1},{1,0},{2,3},{3,2},{4,5},{5,4},{6,7},{7,6},{8,9},{9,8},{10,11... | collective-permute-start | bytes 1769480 | tf_op jit(solution)/shard_map/ppermute | solution.py:207
  70.1 5.6 %collective-permute-start.19 = (f32[32,768]{1,0:T(8,128)S(1)}, f32[32,768]{1,0:T(8,128)S(1)}, u32[]{:S(2)}, u32[]{:S(2)}) collective-permute-start(f32[32,768]{1,0:T(8,128)S(1)} %book_join.3.refs_0_), channel_id=1, source_target_pairs={{0,24},{8,16},{16,8},{24,0},{1,25},{9,17},{17,9},{25,1},{2,26},{10... | collective-permute-start | bytes 294920 | tf_op jit(solution)/shard_map/ppermute | solution.py:207
  72.7 4.6 %collective-permute-start.18 = (f32[32,768]{1,0:T(8,128)S(1)}, f32[32,768]{1,0:T(8,128)S(1)}, u32[]{:S(2)}, u32[]{:S(2)}) collective-permute-start(f32[32,768]{1,0:T(8,128)S(1)} %book_join.3.refs_0_), channel_id=1, source_target_pairs={{0,16},{8,24},{16,0},{24,8},{1,17},{9,25},{17,1},{25,9},{2,18},{10... | collective-permute-start | bytes 294920 | tf_op jit(solution)/shard_map/ppermute | solution.py:207
  73.2 4.6 %collective-permute-start.17 = (f32[32,768]{1,0:T(8,128)S(1)}, f32[32,768]{1,0:T(8,128)S(1)}, u32[]{:S(2)}, u32[]{:S(2)}) collective-permute-start(f32[32,768]{1,0:T(8,128)S(1)} %book_join.3.refs_0_), channel_id=1, source_target_pairs={{0,8},{8,0},{16,24},{24,16},{1,9},{9,1},{17,25},{25,17},{2,10},{10... | collective-permute-start | bytes 294920 | tf_op jit(solution)/shard_map/ppermute | solution.py:207
  77.8 1.8 %collective-permute-start.20 = (f32[128,768]{1,0:T(8,128)S(1)}, f32[128,768]{1,0:T(8,128)S(1)}, u32[]{:S(2)}, u32[]{:S(2)}) collective-permute-start(f32[128,768]{1,0:T(8,128)S(1)} %bitcast.14), channel_id=1, source_target_pairs={{0,1},{1,0},{2,3},{3,2},{4,5},{5,4},{6,7},{7,6},{8,9},{9,8},{10,11... | collective-permute-start | bytes 1179656 | tf_op jit(solution)/shard_map/ppermute | solution.py:207

commit v3 on v2

--- a/solution.py
+++ b/solution.py
@@ -10,6 +10,7 @@
 FINE = 64
 VMEM = pl.BlockSpec(memory_space=pltpu.VMEM)
 ANY = pl.BlockSpec(memory_space=pl.ANY)
+HBM = pl.BlockSpec(memory_space=pltpu.HBM)
 
 
 def split2(x):
@@ -49,8 +50,8 @@
 
 def score_kernel(
     q_hbm, codes_hbm, book_hbm, pos_hbm,
-    e_ref, hits_ref, r_ref, stats_ref,
-    q_ref, codes_ref, book_ref, pos_ref, qs_ref, s_ref, low_ref, book_t_ref, sems,
+    q_ref, e_ref, hits_ref, r_ref, stats_ref,
+    codes_ref, book_ref, pos_ref, qs_ref, s_ref, low_ref, book_t_ref, sems,
 ):
     rows, width = q_ref.shape
     subs, docs = codes_ref.shape
@@ -114,13 +115,14 @@
     u_ref[...] = (dot_nt(em, rh) + dot_nt(eh, rm)) + dot_nt(eh, rh)
 
 
-def positive_kernel(hits_ref, r_ref, q_hbm, after_ref, p_ref, qt_ref, q_ref, sem):
-    rows, width = p_ref.shape
-    load = pltpu.make_async_copy(q_hbm, q_ref, sem)
-    load.start()
+def positive_kernel(hits_ref, r_ref, after_ref, p_ref):
+    width = p_ref.shape[1]
     hits = hits_ref[...]
     p_ref[...] = dot_nt(hits, r_ref[width:, :]) + dot_nt(hits, r_ref[0:width, :])
-    load.wait()
+
+
+def turn_kernel(q_ref, qt_ref):
+    rows = q_ref.shape[0]
     high, mid = split2(q_ref[...].T)
     qt_ref[:, 0:rows] = mid
     qt_ref[:, rows : 2 * rows] = high
@@ -153,7 +155,7 @@
 
 
 def book_kernel(
-    e_ref, hits_ref, scale_ref, qt_ref, codes_ref, after_ref,
+    e_ref, hits_ref, scale_ref, qt_ref, codes_ref,
     keep_ref, send_ref, ws_ref, dg_ref, gt_ref, both_ref,
 ):
     rows, docs = e_ref.shape
@@ -220,39 +222,90 @@
         for k, out in enumerate(outs):
             out[...] = keep_ref[place ^ k] + got_ref[place ^ k]
 
-    blocks = call(kernel, [(shape[1:], F32)] * count, [VMEM, VMEM, ANY], mib=4, name=name)(
+    blocks = call(kernel, [(shape[1:], F32)] * count, [VMEM, VMEM, VMEM], mib=4, name=name)(
         keep.reshape(shape), got.reshape(shape), after
     )
     return list(blocks)
 
 
 def add(pieces, after, name):
+    count = len(pieces)
+
     def kernel(*refs):
         total = refs[0][...]
-        for ref in refs[1:-2]:
+        for ref in refs[1:count]:
             total = total + ref[...]
         refs[-1][...] = total
 
-    return call(kernel, [(pieces[0].shape, F32)], [VMEM] * len(pieces) + [ANY], mib=4, name=name)(*pieces, after)[0]
-
-
-def put(pieces, axis, unit, name):
+    return call(kernel, [(pieces[0].shape, F32)], [VMEM] * (count + len(after)), mib=4, name=name)(
+        *pieces, *after
+    )[0]
+
+
+def bit_at(step, core, count):
+    return (step + core * (count // 2)) % count
+
+
+def chip_swap(x, step):
+    corpus = lax.axis_size("corpus")
+    count = (corpus // 2).bit_length() - 1
+    return lax.ppermute(x, "corpus", [(i, i ^ (2 << bit_at(step, i % 2, count))) for i in range(corpus)])
+
+
+def my_half(step):
+    count = (lax.axis_size("corpus") // 2).bit_length() - 1
+    me = lax.axis_index("corpus")
+    return (me >> (1 + bit_at(step, me % 2, count))) & 1
+
+
+def halve(keep, got, step, after, name):
+    rows, width = keep.shape
+    shape = (2, rows // 2, width)
+
+    def kernel(keep_ref, got_ref, *refs):
+        mine = my_half(step)
+        refs[-2][...] = keep_ref[mine] + got_ref[mine]
+        refs[-1][...] = keep_ref[1 - mine] + got_ref[1 - mine]
+
+    return call(kernel, [(shape[1:], F32)] * 2, [VMEM] * (2 + len(after)), mib=4, name=name)(
+        keep.reshape(shape), got.reshape(shape), *after
+    )
+
+
+def rejoin(own, got, step, after, name):
+    rows, width = own.shape
+
+    def kernel(own_ref, got_ref, *refs):
+        mine = my_half(step)
+        refs[-1][mine] = own_ref[...]
+        refs[-1][1 - mine] = got_ref[...]
+
+    whole = call(kernel, [((2, rows, width), F32)], [VMEM] * (2 + len(after)), mib=4, name=name)(own, got, *after)[0]
+    return whole.reshape(2 * rows, width)
+
+
+def put(pieces, axis, unit, after, name):
     rows, width = pieces[0].shape
+
+    count = len(pieces)
 
     def kernel(*refs):
         place = place_of(axis, unit)
-        for k, ref in enumerate(refs[:-1]):
+        for k, ref in enumerate(refs[:count]):
             refs[-1][place ^ k] = ref[...]
 
-    count = len(pieces)
-    whole = call(kernel, [((count, rows, width), F32)], [VMEM] * count, mib=4, name=name)(*pieces)[0]
+    whole = call(kernel, [((count, rows, width), F32)], [VMEM] * (count + len(after)), mib=4, name=name)(
+        *pieces, *after
+    )[0]
     return whole.reshape(count * rows, width)
 
 
-def finish(own, got, name):
+def finish(own, got, after, name):
     rows, width = own.shape
 
-    def kernel(own_ref, got_ref, out_hbm, sems):
+    def kernel(own_ref, got_ref, *refs):
+        out_hbm, token_ref, sems = refs[len(after) :]
+        token_ref[...] = own_ref[0:8, 0:LANES]
         core = lax.axis_index("corpus") % 2
         copies = [
             pltpu.make_async_copy(own_ref, out_hbm.at[core], sems.at[0]),
@@ -263,16 +316,16 @@
         for copy in copies:
             copy.wait()
 
-    whole = pl.pallas_call(
+    whole, token = pl.pallas_call(
         kernel,
-        out_shape=jax.ShapeDtypeStruct((2, rows, width), F32),
-        in_specs=[VMEM, VMEM],
-        out_specs=ANY,
+        out_shape=(jax.ShapeDtypeStruct((2, rows, width), F32), jax.ShapeDtypeStruct((8, LANES), F32)),
+        in_specs=[VMEM] * (2 + len(after)),
+        out_specs=(ANY, VMEM),
         scratch_shapes=[pltpu.SemaphoreType.DMA((2,))],
         compiler_params=pltpu.CompilerParams(vmem_limit_bytes=4 * 2**20),
         name=name,
-    )(own, got)
-    return whole.reshape(2 * rows, width)
+    )(own, got, *after)
+    return whole.reshape(2 * rows, width), token
 
 
 def local(queries, codes, positive, codebook):
@@ -283,12 +336,11 @@
     chips = corpus // 2
     codes_t = codes.T
     work = rows * docs * width
-    e, hits, r, stats = call(
+    q, e, hits, r, stats = call(
         score_kernel,
-        [((rows, docs), F32), ((rows, docs), BF16), ((2 * width, docs), BF16), ((8, rows), F32)],
-        [ANY] * 4,
+        [((rows, width), F32), ((rows, docs), F32), ((rows, docs), BF16), ((2 * width, docs), BF16), ((8, rows), F32)],
+        [HBM] * 4,
         [
-            pltpu.VMEM((rows, width), F32),
             pltpu.VMEM((subs, docs), I32),
             pltpu.VMEM((words, width), F32),
             pltpu.VMEM((rows,), I32),
@@ -300,21 +352,16 @@
         ],
         12 * work,
         24,
-    )(queries, codes_t, codebook, positive)
+    )(*[pltpu.with_memory_space_constraint(x, pltpu.HBM) for x in (queries, codes_t, codebook, positive)])
     u = call(spread_kernel, [((rows, width), F32)], [VMEM] * 2, (), 6 * work)(e, r)[0]
-    joined, got, bits, after = stats, swap(stats, "corpus", 1), 2, stats
+    qt = call(turn_kernel, [((width, 2 * rows), BF16)], [VMEM], (), work)(q)[0]
+    joined, got, bits, after = stats, swap(stats, "corpus", 1), 2, qt
     while bits < corpus:
         joined = call(join_kernel, [((8, rows), F32)], [VMEM] * 3, mib=4)(joined, got, after)[0]
         got = swap(joined, "corpus", bits)
         after = u
         bits *= 2
-    p, qt = call(
-        positive_kernel,
-        [((rows, width), F32), ((width, 2 * rows), BF16)],
-        [VMEM, VMEM, ANY, VMEM],
-        [pltpu.VMEM((rows, width), F32), pltpu.SemaphoreType.DMA],
-        4 * work,
-    )(hits, r, queries, joined)
+    p = call(positive_kernel, [((rows, width), F32)], [VMEM] * 3, (), 4 * work)(hits, r, joined)[0]
     half = rows // 2
     keep, send, loss, scale = call(
         terms_kernel,
@@ -324,14 +371,11 @@
         mib=8,
     )(joined, got, stats, u.reshape(2, half, width), p.reshape(2, half, width))
 
-    cuts = cut(keep, swap(send, "corpus", 1), "corpus", 2, chips, scale, "query_cut")
-    got = [swap(cuts[k], "corpus", 2 * k) for k in range(1, chips)]
-
     part_rows = words // 2
     book_keep, book_send = call(
         book_kernel,
         [((part_rows, width), F32)] * 2,
-        [VMEM] * 6,
+        [VMEM] * 5,
         [
             pltpu.VMEM((2 * rows, docs), BF16),
             pltpu.VMEM((width, docs), F32),
@@ -339,23 +383,32 @@
             pltpu.VMEM((2, part_rows, width), F32),
         ],
         14 * work,
-    )(e, hits, scale, qt, codes_t, cuts[0])
-
-    own = add([cuts[0]] + got, scale, "query_sum")
-    blocks = [own] + [swap(own, "corpus", 2 * k) for k in range(1, chips)]
-    whole = put(blocks, "corpus", 2, "query_put")
-    grad_queries = finish(whole, swap(whole, "corpus", 1), "query_finish")
-
-    cuts = cut(book_keep, swap(book_send, "corpus", 1), "query", 1, query, scale, "book_cut")
-    got = [swap(cuts[k], "query", k) for k in range(1, query)]
-    own = add([cuts[0]] + got, scale, "book_sum")
-    bits = 2
-    while bits < corpus:
-        own = add([own, swap(own, "corpus", bits)], scale, "book_join")
-        bits *= 2
-    blocks = [own] + [swap(own, "query", k) for k in range(1, query)]
-    whole = put(blocks, "query", 1, "book_put")
-    grad_codebook = finish(whole, swap(whole, "corpus", 1), "book_finish")
+    )(e, hits, scale, qt, codes_t)
+
+    bits = chips.bit_length() - 1
+    q_keep, q_send = halve(keep, swap(send, "corpus", 1), 0, [], "query_halve")
+    b_cuts = cut(book_keep, swap(book_send, "corpus", 1), "query", 1, query, scale, "book_cut")
+    b_got = [swap(b_cuts[k], "query", k) for k in range(1, query)]
+    b_own = b_sum = add([b_cuts[0]] + b_got, [], "book_sum")
+    for step in range(bits - 1):
+        q_got = chip_swap(q_send, step)
+        if step < bits - 2:
+            q_keep, q_send = halve(q_keep, q_got, step + 1, [], "query_halve")
+    q_own = add([q_keep, q_got], [b_sum], "query_add")
+    for step in range(bits - 1):
+        b_own = add([b_own, chip_swap(b_own, step)], [], "book_join")
+    b_mid = b_own
+    b_last = chip_swap(b_own, bits - 1)
+    q_last = chip_swap(q_own, bits - 1)
+    b_own = add([b_own, b_last], [], "book_join")
+    q_own = add([q_own, q_last], [b_own], "query_all")
+    blocks = [b_own] + [swap(b_own, "query", k) for k in range(1, query)]
+    b_whole = put(blocks, "query", 1, [], "book_put")
+    q_whole = q_own
+    for step in reversed(range(bits - 1)):
+        q_whole = rejoin(q_whole, chip_swap(q_whole, step), step, [b_whole], "query_put")
+    grad_codebook, token = finish(b_whole, swap(b_whole, "corpus", 1), [], "book_finish")
+    grad_queries, token = finish(q_whole, swap(q_whole, "corpus", 1), [token], "query_finish")
     return grad_queries, grad_codebook, loss
 
 

time: 80.9 us -> 69.5 us (0.86)
  waiting for transfers between devices: 27.9 us -> 21.3 us
  local copies, waits for them, and re-layouts: 4.08 us -> 0.06 us
  starting transfers between devices: 27 us -> 25.1 us
  Pallas kernels: 20.7 us -> 21.9 us
    ppermute x21 -> x13, waiting for transfers between devices: 27.9 us -> 12.3 us  [swap(): lax.ppermute(x, axis, [(i, i ^ bits) for i in range(lax.axis_size(axis))])]
    ppermute x21 -> x13, starting transfers between devices: 27 us -> 14.3 us  [swap(): lax.ppermute(x, axis, [(i, i ^ bits) for i in range(lax.axis_size(axis))])]
    ppermute x0 -> x5, starting transfers between devices: none -> 10.8 us  [chip_swap(): lax.ppermute(x, 'corpus', [(i, i ^ 2 << bit_at(step, i % 2, count)) for i...]
    ppermute x0 -> x5, waiting for transfers between devices: none -> 9.08 us  [chip_swap(): lax.ppermute(x, 'corpus', [(i, i ^ 2 << bit_at(step, i % 2, count)) for i...]
    unnamed x10 -> x2, local copies, waits for them, and re-layouts: 4.08 us -> 0.06 us
    pallas_call x13 -> x15, Pallas kernels: 17.7 us -> 18.9 us  [the longest x1 8 us: local(): call(score_kernel, [((rows, width), F32), ((rows, docs), F32), ((rows, do...]
  transfers between devices with their start and end apart: 21 -> 18, of which waited for: 10 -> 11; matrix products, arithmetic and copies ran while one was open for 0% -> 0% of each run, Pallas kernels for 7% -> 16%
where the time goes in v3:
time: 69.5 us; the launch traced here: 69.3 us
  starting transfers between devices  25.1 us (36%)
  Pallas kernels  21.9 us (32%)
  waiting for transfers between devices  21.3 us (31%)
  between operations  0.94 us (1%)
    ppermute x13, starting transfers between devices, swap(): lax.ppermute(x, axis, [(i, i ^ bits) for i in range(lax.axis_size(axis))])  14.3 us
    ppermute x13, waiting for transfers between devices, swap(): lax.ppermute(x, axis, [(i, i ^ bits) for i in range(lax.axis_size(axis))])  12.3 us
    ppermute x5, starting transfers between devices, chip_swap(): lax.ppermute(x, 'corpus', [(i, i ^ 2 << bit_at(step, i % 2, count)) for i...  10.8 us
    ppermute x5, waiting for transfers between devices, chip_swap(): lax.ppermute(x, 'corpus', [(i, i ^ 2 << bit_at(step, i % 2, count)) for i...  9.08 us
    pallas_call x1, Pallas kernels, local(): call(score_kernel, [((rows, width), F32), ((rows, docs), F32), ((rows, do...  8 us
    pallas_call x1, Pallas kernels, local(): call(book_kernel, [((part_rows, width), F32)] * 2, [VMEM] * 5, [pltpu.VME...  6.21 us
    pallas_call x2, Pallas kernels, finish(): pl.pallas_call(kernel, out_shape=(jax.ShapeDtypeStruct((2, rows, width),...  2.52 us
    pallas_call x1, Pallas kernels, local(): call(spread_kernel, [((rows, width), F32)], [VMEM] * 2, (), 6 * work)(e, r)  2.03 us
  transfers between devices with their start and end apart: 18, of which 11 were waited for; matrix products, arithmetic and copies ran while one was open for 0% of the time, Pallas kernels for 16%

profile of v3, /device:TPU:0, one launch (start us, length us, event | category | flops | bytes accessed | tf_op | source)
XLA Modules:
  0.0 69.3 jit_solution(874276469105426432)
XLA Ops:
  0.6 8.0 %score_kernel.1 = (f32[384,768]{1,0:T(8,128)S(1)}, f32[384,1024]{1,0:T(8,128)S(1)}, bf16[384,1024]{1,0:T(8,128)(2,1)S(1)}, bf16[1536,1024]{1,0:T(8,128)(2,1)S(1)}, f32[8,384]{1,0:T(8,128)S(1)}) custom-call(f32[384,768]{1,0:T(8,128)} %q_hbm.1, s32[96,1024]{1,0:T(8,128)} %bitcast.22, f32[256,768]{1,0:T(8,128)} %book_hbm.1, s32[384]{0:T(512)} %pos_hbm.1), custom_call_target="tpu_custom_call" | custom-call | flops 3623878656 | bytes 131072 | tf_op jit(solution)/shard_map/score_kernel/pallas_call | solution.py:339
  8.6 0.5 collective-permute-start
  9.1 0.4 turn_kernel.1.after_ref.qt_ref
  9.5 0.5 collective-permute-done.b_ref
  10.0 3.0 %collective-permute-start.1 = (f32[8,384]{1,0:T(8,128)S(1)}, f32[8,384]{1,0:T(8,128)S(1)}, u32[]{:S(2)}, u32[]{:S(2)}) collective-permute-start(f32[8,384]{1,0:T(8,128)S(1)} %join_kernel.2.a_ref), channel_id=1, source_target_pairs={{0,2},{1,3},{2,0},{3,1},{4,6},{5,7},{6,4},{7,5},{8,10},{9,11},{10,... | collective-permute-start | bytes 36872 | tf_op jit(solution)/shard_map/ppermute | solution.py:209
  13.0 2.0 %spread_kernel.1.after_ref = f32[384,768]{1,0:T(8,128)S(1)} custom-call(f32[384,1024]{1,0:T(8,128)S(1)} %get-tuple-element.25.e_ref, bf16[1536,1024]{1,0:T(8,128)(2,1)S(1)} %get-tuple-element.26.r_ref), custom_call_target="tpu_custom_call" | custom-call | flops 1811939328 | bytes 131072 | tf_op jit(solution)/shard_map/spread_kernel/pallas_call | solution.py:356
  15.0 0.0 collective-permute-done.1.b_ref
  15.1 2.7 %collective-permute-start.2 = (f32[8,384]{1,0:T(8,128)S(1)}, f32[8,384]{1,0:T(8,128)S(1)}, u32[]{:S(2)}, u32[]{:S(2)}) collective-permute-start(f32[8,384]{1,0:T(8,128)S(1)} %join_kernel.3.after_ref.a_ref), channel_id=1, source_target_pairs={{0,4},{1,5},{2,6},{3,7},{4,0},{5,1},{6,2},{7,3},{8,12},{9,13},{10,... | collective-permute-start | bytes 36872 | tf_op jit(solution)/shard_map/ppermute | solution.py:209
  17.8 1.4 %positive_kernel.1 = f32[384,768]{1,0:T(8,128)S(1)} custom-call(bf16[384,1024]{1,0:T(8,128)(2,1)S(1)} %get-tuple-element.27.hits_ref, bf16[1536,1024]{1,0:T(8,128)(2,1)S(1)} %get-tuple-element.26.r_ref, f32[8,384]{1,0:T(8,128)S(1)} %join_kernel.3.after_ref.a_ref), custom_call_target="tpu_custom_call" | custom-call | flops 1207959552 | bytes 131072 | tf_op jit(solution)/shard_map/positive_kernel/pallas_call | solution.py:364
  19.2 0.5 collective-permute-done.2.b_ref
  19.7 0.0 copy-start
  19.7 0.9 %terms_kernel.1 = (f32[192,768]{1,0:T(8,128)S(1)}, f32[192,768]{1,0:T(8,128)S(1)}, f32[384]{0:T(512)}, f32[1,384]{1,0:T(1,128)S(1)}) custom-call(f32[8,384]{1,0:T(8,128)S(1)} %join_kernel.3.after_ref.a_ref, f32[8,384]{1,0:T(8,128)S(1)} %collective-permute-done.2.b_ref, f32[8,384]{1,0:T(8,128)S(1)} %get-tuple-element.23.a_ref.first_ref, ...), custom_call_target="tpu_custom_call" | custom-call | bytes 131072 | tf_op jit(solution)/shard_map/terms_kernel/pallas_call | solution.py:366
  20.6 0.0 collective-permute-start.3
  20.7 0.1 copy-done
  20.7 6.2 %book_kernel.1 = (f32[128,768]{1,0:T(8,128)S(1)}, f32[128,768]{1,0:T(8,128)S(1)}) custom-call(f32[384,1024]{1,0:T(8,128)S(1)} %get-tuple-element.25.e_ref, bf16[384,1024]{1,0:T(8,128)(2,1)S(1)} %get-tuple-element.27.hits_ref, f32[1,384]{1,0:T(1,128)S(1)} %get-tuple-element.32.scale_ref.after_ref, bf16[768,768]{1,0:T(8,128)(2,1)S(1)} %turn_kernel.1.after_ref.qt_ref, ...), custom_call_target="tpu_custom_call" | custom-call | flops 4227858432 | bytes 131072 | tf_op jit(solution)/shard_map/book_kernel/pallas_call | solution.py:375
  26.9 0.5 collective-permute-start.5
  27.4 0.0 collective-permute-done.3
  27.4 0.1 query_halve.1
  27.5 1.7 %collective-permute-start.4 = (f32[96,768]{1,0:T(8,128)S(1)}, f32[96,768]{1,0:T(8,128)S(1)}, u32[]{:S(2)}, u32[]{:S(2)}) collective-permute-start(f32[96,768]{1,0:T(8,128)S(1)} %get-tuple-element.31), channel_id=1, source_target_pairs={{0,2},{1,5},{2,0},{3,7},{4,6},{5,1},{6,4},{7,3},{8,10},{9,13},{10,... | collective-permute-start | bytes 884744 | tf_op jit(solution)/shard_map/ppermute | solution.py:252
  29.2 0.0 collective-permute-done.5
  29.3 1.6 %collective-permute-start.6 = (f32[32,768]{1,0:T(8,128)S(1)}, f32[32,768]{1,0:T(8,128)S(1)}, u32[]{:S(2)}, u32[]{:S(2)}) collective-permute-start(f32[32,768]{1,0:T(8,128)S(1)} %get-tuple-element.36), channel_id=1, source_target_pairs={{0,8},{8,0},{16,24},{24,16},{1,9},{9,1},{17,25},{25,17},{2,10},{10... | collective-permute-start | bytes 294920 | tf_op jit(solution)/shard_map/ppermute | solution.py:209
  30.9 1.5 %collective-permute-start.7 = (f32[32,768]{1,0:T(8,128)S(1)}, f32[32,768]{1,0:T(8,128)S(1)}, u32[]{:S(2)}, u32[]{:S(2)}) collective-permute-start(f32[32,768]{1,0:T(8,128)S(1)} %get-tuple-element.37), channel_id=1, source_target_pairs={{0,16},{8,24},{16,0},{24,8},{1,17},{9,25},{17,1},{25,9},{2,18},{10... | collective-permute-start | bytes 294920 | tf_op jit(solution)/shard_map/ppermute | solution.py:209
  32.4 0.5 collective-permute-start.8
  32.8 2.0 %collective-permute-done.6.refs_1_ = f32[32,768]{1,0:T(8,128)S(1)} collective-permute-done((f32[32,768]{1,0:T(8,128)S(1)}, f32[32,768]{1,0:T(8,128)S(1)}, u32[]{:S(2)}, u32[]{:S(2)}) %collective-permute-start.6) | collective-permute-done | bytes 98336 | tf_op jit(solution)/shard_map/ppermute | solution.py:209
  34.8 2.4 %collective-permute-done.7.refs_2_ = f32[32,768]{1,0:T(8,128)S(1)} collective-permute-done((f32[32,768]{1,0:T(8,128)S(1)}, f32[32,768]{1,0:T(8,128)S(1)}, u32[]{:S(2)}, u32[]{:S(2)}) %collective-permute-start.7) | collective-permute-done | bytes 98336 | tf_op jit(solution)/shard_map/ppermute | solution.py:209
  37.2 1.0 %collective-permute-done.8.refs_3_ = f32[32,768]{1,0:T(8,128)S(1)} collective-permute-done((f32[32,768]{1,0:T(8,128)S(1)}, f32[32,768]{1,0:T(8,128)S(1)}, u32[]{:S(2)}, u32[]{:S(2)}) %collective-permute-start.8) | collective-permute-done | bytes 98336 | tf_op jit(solution)/shard_map/ppermute | solution.py:209
  38.2 0.0 collective-permute-done.4.refs_1_
  38.3 2.4 %collective-permute-start.9 = (f32[96,768]{1,0:T(8,128)S(1)}, f32[96,768]{1,0:T(8,128)S(1)}, u32[]{:S(2)}, u32[]{:S(2)}) collective-permute-start(f32[96,768]{1,0:T(8,128)S(1)} %query_add.1.refs_0_), channel_id=1, source_target_pairs={{0,4},{1,3},{2,6},{3,1},{4,0},{5,7},{6,2},{7,5},{8,12},{9,11},{10,... | collective-permute-start | bytes 884744 | tf_op jit(solution)/shard_map/ppermute | solution.py:252
  40.6 1.2 %collective-permute-start.10 = (f32[32,768]{1,0:T(8,128)S(1)}, f32[32,768]{1,0:T(8,128)S(1)}, u32[]{:S(2)}, u32[]{:S(2)}) collective-permute-start(f32[32,768]{1,0:T(8,128)S(1)} %book_sum.1.refs_2_.refs_0_), channel_id=1, source_target_pairs={{0,2},{1,5},{2,0},{3,7},{4,6},{5,1},{6,4},{7,3},{8,10},{9,13},{10,... | collective-permute-start | bytes 294920 | tf_op jit(solution)/shard_map/ppermute | solution.py:252
  41.8 6.5 %collective-permute-done.10.refs_1_ = f32[32,768]{1,0:T(8,128)S(1)} collective-permute-done((f32[32,768]{1,0:T(8,128)S(1)}, f32[32,768]{1,0:T(8,128)S(1)}, u32[]{:S(2)}, u32[]{:S(2)}) %collective-permute-start.10) | collective-permute-done | bytes 98336 | tf_op jit(solution)/shard_map/ppermute | solution.py:252
  48.3 3.1 %collective-permute-start.11 = (f32[32,768]{1,0:T(8,128)S(1)}, f32[32,768]{1,0:T(8,128)S(1)}, u32[]{:S(2)}, u32[]{:S(2)}) collective-permute-start(f32[32,768]{1,0:T(8,128)S(1)} %book_join.2.refs_0_), channel_id=1, source_target_pairs={{0,4},{1,3},{2,6},{3,1},{4,0},{5,7},{6,2},{7,5},{8,12},{9,11},{10,... | collective-permute-start | bytes 294920 | tf_op jit(solution)/shard_map/ppermute | solution.py:252
  51.4 2.6 %collective-permute-done.11.refs_1_ = f32[32,768]{1,0:T(8,128)S(1)} collective-permute-done((f32[32,768]{1,0:T(8,128)S(1)}, f32[32,768]{1,0:T(8,128)S(1)}, u32[]{:S(2)}, u32[]{:S(2)}) %collective-permute-start.11) | collective-permute-done | bytes 98336 | tf_op jit(solution)/shard_map/ppermute | solution.py:252
  54.0 0.0 collective-permute-done.9.refs_1_
  54.0 2.5 %collective-permute-start.12 = (f32[96,768]{1,0:T(8,128)S(1)}, f32[96,768]{1,0:T(8,128)S(1)}, u32[]{:S(2)}, u32[]{:S(2)}) collective-permute-start(f32[96,768]{1,0:T(8,128)S(1)} %query_all.1.own_ref), channel_id=1, source_target_pairs={{0,2},{1,5},{2,0},{3,7},{4,6},{5,1},{6,4},{7,3},{8,10},{9,13},{10,... | collective-permute-start | bytes 884744 | tf_op jit(solution)/shard_map/ppermute | solution.py:252
  56.5 1.7 %collective-permute-start.15 = (f32[32,768]{1,0:T(8,128)S(1)}, f32[32,768]{1,0:T(8,128)S(1)}, u32[]{:S(2)}, u32[]{:S(2)}) collective-permute-start(f32[32,768]{1,0:T(8,128)S(1)} %book_join.3.refs_2_.refs_0_), channel_id=1, source_target_pairs={{0,24},{8,16},{16,8},{24,0},{1,25},{9,17},{17,9},{25,1},{2,26},{10... | collective-permute-start | bytes 294920 | tf_op jit(solution)/shard_map/ppermute | solution.py:209
  58.3 1.0 %collective-permute-start.14 = (f32[32,768]{1,0:T(8,128)S(1)}, f32[32,768]{1,0:T(8,128)S(1)}, u32[]{:S(2)}, u32[]{:S(2)}) collective-permute-start(f32[32,768]{1,0:T(8,128)S(1)} %book_join.3.refs_2_.refs_0_), channel_id=1, source_target_pairs={{0,16},{8,24},{16,0},{24,8},{1,17},{9,25},{17,1},{25,9},{2,18},{10... | collective-permute-start | bytes 294920 | tf_op jit(solution)/shard_map/ppermute | solution.py:209
  59.3 0.8 %collective-permute-start.13 = (f32[32,768]{1,0:T(8,128)S(1)}, f32[32,768]{1,0:T(8,128)S(1)}, u32[]{:S(2)}, u32[]{:S(2)}) collective-permute-start(f32[32,768]{1,0:T(8,128)S(1)} %book_join.3.refs_2_.refs_0_), channel_id=1, source_target_pairs={{0,8},{8,0},{16,24},{24,16},{1,9},{9,1},{17,25},{25,17},{2,10},{10... | collective-permute-start | bytes 294920 | tf_op jit(solution)/shard_map/ppermute | solution.py:209
  60.0 2.0 %collective-permute-done.15.refs_3_ = f32[32,768]{1,0:T(8,128)S(1)} collective-permute-done((f32[32,768]{1,0:T(8,128)S(1)}, f32[32,768]{1,0:T(8,128)S(1)}, u32[]{:S(2)}, u32[]{:S(2)}) %collective-permute-start.15) | collective-permute-done | bytes 98336 | tf_op jit(solution)/shard_map/ppermute | solution.py:209
  62.1 1.0 %collective-permute-done.14.refs_2_ = f32[32,768]{1,0:T(8,128)S(1)} collective-permute-done((f32[32,768]{1,0:T(8,128)S(1)}, f32[32,768]{1,0:T(8,128)S(1)}, u32[]{:S(2)}, u32[]{:S(2)}) %collective-permute-start.14) | collective-permute-done | bytes 98336 | tf_op jit(solution)/shard_map/ppermute | solution.py:209
  63.1 0.8 %collective-permute-done.13.refs_1_ = f32[32,768]{1,0:T(8,128)S(1)} collective-permute-done((f32[32,768]{1,0:T(8,128)S(1)}, f32[32,768]{1,0:T(8,128)S(1)}, u32[]{:S(2)}, u32[]{:S(2)}) %collective-permute-start.13) | collective-permute-done | bytes 98336 | tf_op jit(solution)/shard_map/ppermute | solution.py:209
  63.9 0.0 collective-permute-done.12.got_ref
  63.9 0.1 query_put.1
  64.0 0.1 collective-permute-start.16
  64.1 0.5 collective-permute-start.17
  64.6 2.1 %collective-permute-done.17.got_ref = f32[128,768]{1,0:T(8,128)S(1)} collective-permute-done((f32[128,768]{1,0:T(8,128)S(1)}, f32[128,768]{1,0:T(8,128)S(1)}, u32[]{:S(2)}, u32[]{:S(2)}) %collective-permute-start.17) | collective-permute-done | bytes 393248 | tf_op jit(solution)/shard_map/ppermute | solution.py:209
  66.6 0.9 %book_finish.1 = (f32[2,128,768]{2,1,0:T(8,128)}, f32[8,128]{1,0:T(8,128)S(1)}) custom-call(f32[128,768]{1,0:T(8,128)S(1)} %bitcast.15, f32[128,768]{1,0:T(8,128)S(1)} %collective-permute-done.17.got_ref), custom_call_target="tpu_custom_call" | custom-call | tf_op jit(solution)/shard_map/book_finish/pallas_call | solution.py:319
  67.5 0.0 collective-permute-done.16.got_ref
  67.5 1.6 %query_finish.1 = (f32[2,192,768]{2,1,0:T(8,128)}, f32[8,128]{1,0:T(8,128)}) custom-call(f32[192,768]{1,0:T(8,128)S(1)} %bitcast.17, f32[192,768]{1,0:T(8,128)S(1)} %collective-permute-done.16.got_ref, f32[8,128]{1,0:T(8,128)S(1)} %get-tuple-element.39.refs_0_), custom_call_target="tpu_custom_call" | custom-call | tf_op jit(solution)/shard_map/query_finish/pallas_call | solution.py:319
  (9 shorter events, 0.2 us)
Async XLA Ops:
  8.6 1.3 %collective-permute-start = (f32[8,384]{1,0:T(8,128)S(1)}, f32[8,384]{1,0:T(8,128)S(1)}, u32[]{:S(2)}, u32[]{:S(2)}) collective-permute-start(f32[8,384]{1,0:T(8,128)S(1)} %get-tuple-element.23.a_ref.first_ref), channel_id=1, source_target_pairs={{0,1},{1,0},{2,3},{3,2},{4,5},{5,4},{6,7},{7,6},{8,9},{9,8},{10,11... | collective-permute-start | bytes 36872 | tf_op jit(solution)/shard_map/ppermute | solution.py:209
  10.0 5.0 %collective-permute-start.1 = (f32[8,384]{1,0:T(8,128)S(1)}, f32[8,384]{1,0:T(8,128)S(1)}, u32[]{:S(2)}, u32[]{:S(2)}) collective-permute-start(f32[8,384]{1,0:T(8,128)S(1)} %join_kernel.2.a_ref), channel_id=1, source_target_pairs={{0,2},{1,3},{2,0},{3,1},{4,6},{5,7},{6,4},{7,5},{8,10},{9,11},{10,... | collective-permute-start | bytes 36872 | tf_op jit(solution)/shard_map/ppermute | solution.py:209
  15.1 4.7 %collective-permute-start.2 = (f32[8,384]{1,0:T(8,128)S(1)}, f32[8,384]{1,0:T(8,128)S(1)}, u32[]{:S(2)}, u32[]{:S(2)}) collective-permute-start(f32[8,384]{1,0:T(8,128)S(1)} %join_kernel.3.after_ref.a_ref), channel_id=1, source_target_pairs={{0,4},{1,5},{2,6},{3,7},{4,0},{5,1},{6,2},{7,3},{8,12},{9,13},{10,... | collective-permute-start | bytes 36872 | tf_op jit(solution)/shard_map/ppermute | solution.py:209
  19.7 1.0 %copy-start = (s32[1024,96]{0,1:T(8,128)S(1)}, s32[1024,96]{0,1:T(8,128)}, u32[]{:S(2)}) copy-start(s32[1024,96]{0,1:T(8,128)} %param.5) | copy-start | bytes 1179652
  20.6 6.8 %collective-permute-start.3 = (f32[192,768]{1,0:T(8,128)S(1)}, f32[192,768]{1,0:T(8,128)S(1)}, u32[]{:S(2)}, u32[]{:S(2)}) collective-permute-start(f32[192,768]{1,0:T(8,128)S(1)} %get-tuple-element.29), channel_id=1, source_target_pairs={{0,1},{1,0},{2,3},{3,2},{4,5},{5,4},{6,7},{7,6},{8,9},{9,8},{10,11... | collective-permute-start | bytes 1769480 | tf_op jit(solution)/shard_map/ppermute | solution.py:209
  26.9 2.3 %collective-permute-start.5 = (f32[128,768]{1,0:T(8,128)S(1)}, f32[128,768]{1,0:T(8,128)S(1)}, u32[]{:S(2)}, u32[]{:S(2)}) collective-permute-start(f32[128,768]{1,0:T(8,128)S(1)} %get-tuple-element.34), channel_id=1, source_target_pairs={{0,1},{1,0},{2,3},{3,2},{4,5},{5,4},{6,7},{7,6},{8,9},{9,8},{10,11... | collective-permute-start | bytes 1179656 | tf_op jit(solution)/shard_map/ppermute | solution.py:209
  27.5 10.7 %collective-permute-start.4 = (f32[96,768]{1,0:T(8,128)S(1)}, f32[96,768]{1,0:T(8,128)S(1)}, u32[]{:S(2)}, u32[]{:S(2)}) collective-permute-start(f32[96,768]{1,0:T(8,128)S(1)} %get-tuple-element.31), channel_id=1, source_target_pairs={{0,2},{1,5},{2,0},{3,7},{4,6},{5,1},{6,4},{7,3},{8,10},{9,13},{10,... | collective-permute-start | bytes 884744 | tf_op jit(solution)/shard_map/ppermute | solution.py:252
  29.3 5.6 %collective-permute-start.6 = (f32[32,768]{1,0:T(8,128)S(1)}, f32[32,768]{1,0:T(8,128)S(1)}, u32[]{:S(2)}, u32[]{:S(2)}) collective-permute-start(f32[32,768]{1,0:T(8,128)S(1)} %get-tuple-element.36), channel_id=1, source_target_pairs={{0,8},{8,0},{16,24},{24,16},{1,9},{9,1},{17,25},{25,17},{2,10},{10... | collective-permute-start | bytes 294920 | tf_op jit(solution)/shard_map/ppermute | solution.py:209
  30.9 6.4 %collective-permute-start.7 = (f32[32,768]{1,0:T(8,128)S(1)}, f32[32,768]{1,0:T(8,128)S(1)}, u32[]{:S(2)}, u32[]{:S(2)}) collective-permute-start(f32[32,768]{1,0:T(8,128)S(1)} %get-tuple-element.37), channel_id=1, source_target_pairs={{0,16},{8,24},{16,0},{24,8},{1,17},{9,25},{17,1},{25,9},{2,18},{10... | collective-permute-start | bytes 294920 | tf_op jit(solution)/shard_map/ppermute | solution.py:209
  32.4 5.8 %collective-permute-start.8 = (f32[32,768]{1,0:T(8,128)S(1)}, f32[32,768]{1,0:T(8,128)S(1)}, u32[]{:S(2)}, u32[]{:S(2)}) collective-permute-start(f32[32,768]{1,0:T(8,128)S(1)} %get-tuple-element.38), channel_id=1, source_target_pairs={{0,24},{8,16},{16,8},{24,0},{1,25},{9,17},{17,9},{25,1},{2,26},{10... | collective-permute-start | bytes 294920 | tf_op jit(solution)/shard_map/ppermute | solution.py:209
  38.3 15.7 %collective-permute-start.9 = (f32[96,768]{1,0:T(8,128)S(1)}, f32[96,768]{1,0:T(8,128)S(1)}, u32[]{:S(2)}, u32[]{:S(2)}) collective-permute-start(f32[96,768]{1,0:T(8,128)S(1)} %query_add.1.refs_0_), channel_id=1, source_target_pairs={{0,4},{1,3},{2,6},{3,1},{4,0},{5,7},{6,2},{7,5},{8,12},{9,11},{10,... | collective-permute-start | bytes 884744 | tf_op jit(solution)/shard_map/ppermute | solution.py:252
  40.6 7.7 %collective-permute-start.10 = (f32[32,768]{1,0:T(8,128)S(1)}, f32[32,768]{1,0:T(8,128)S(1)}, u32[]{:S(2)}, u32[]{:S(2)}) collective-permute-start(f32[32,768]{1,0:T(8,128)S(1)} %book_sum.1.refs_2_.refs_0_), channel_id=1, source_target_pairs={{0,2},{1,5},{2,0},{3,7},{4,6},{5,1},{6,4},{7,3},{8,10},{9,13},{10,... | collective-permute-start | bytes 294920 | tf_op jit(solution)/shard_map/ppermute | solution.py:252
  48.3 5.6 %collective-permute-start.11 = (f32[32,768]{1,0:T(8,128)S(1)}, f32[32,768]{1,0:T(8,128)S(1)}, u32[]{:S(2)}, u32[]{:S(2)}) collective-permute-start(f32[32,768]{1,0:T(8,128)S(1)} %book_join.2.refs_0_), channel_id=1, source_target_pairs={{0,4},{1,3},{2,6},{3,1},{4,0},{5,7},{6,2},{7,5},{8,12},{9,11},{10,... | collective-permute-start | bytes 294920 | tf_op jit(solution)/shard_map/ppermute | solution.py:252
  54.0 9.9 %collective-permute-start.12 = (f32[96,768]{1,0:T(8,128)S(1)}, f32[96,768]{1,0:T(8,128)S(1)}, u32[]{:S(2)}, u32[]{:S(2)}) collective-permute-start(f32[96,768]{1,0:T(8,128)S(1)} %query_all.1.own_ref), channel_id=1, source_target_pairs={{0,2},{1,5},{2,0},{3,7},{4,6},{5,1},{6,4},{7,3},{8,10},{9,13},{10,... | collective-permute-start | bytes 884744 | tf_op jit(solution)/shard_map/ppermute | solution.py:252
  56.5 5.5 %collective-permute-start.15 = (f32[32,768]{1,0:T(8,128)S(1)}, f32[32,768]{1,0:T(8,128)S(1)}, u32[]{:S(2)}, u32[]{:S(2)}) collective-permute-start(f32[32,768]{1,0:T(8,128)S(1)} %book_join.3.refs_2_.refs_0_), channel_id=1, source_target_pairs={{0,24},{8,16},{16,8},{24,0},{1,25},{9,17},{17,9},{25,1},{2,26},{10... | collective-permute-start | bytes 294920 | tf_op jit(solution)/shard_map/ppermute | solution.py:209
  58.3 4.8 %collective-permute-start.14 = (f32[32,768]{1,0:T(8,128)S(1)}, f32[32,768]{1,0:T(8,128)S(1)}, u32[]{:S(2)}, u32[]{:S(2)}) collective-permute-start(f32[32,768]{1,0:T(8,128)S(1)} %book_join.3.refs_2_.refs_0_), channel_id=1, source_target_pairs={{0,16},{8,24},{16,0},{24,8},{1,17},{9,25},{17,1},{25,9},{2,18},{10... | collective-permute-start | bytes 294920 | tf_op jit(solution)/shard_map/ppermute | solution.py:209
  59.3 4.6 %collective-permute-start.13 = (f32[32,768]{1,0:T(8,128)S(1)}, f32[32,768]{1,0:T(8,128)S(1)}, u32[]{:S(2)}, u32[]{:S(2)}) collective-permute-start(f32[32,768]{1,0:T(8,128)S(1)} %book_join.3.refs_2_.refs_0_), channel_id=1, source_target_pairs={{0,8},{8,0},{16,24},{24,16},{1,9},{9,1},{17,25},{25,17},{2,10},{10... | collective-permute-start | bytes 294920 | tf_op jit(solution)/shard_map/ppermute | solution.py:209
  64.0 3.5 %collective-permute-start.16 = (f32[192,768]{1,0:T(8,128)S(1)}, f32[192,768]{1,0:T(8,128)S(1)}, u32[]{:S(2)}, u32[]{:S(2)}) collective-permute-start(f32[192,768]{1,0:T(8,128)S(1)} %bitcast.16), channel_id=1, source_target_pairs={{0,1},{1,0},{2,3},{3,2},{4,5},{5,4},{6,7},{7,6},{8,9},{9,8},{10,11... | collective-permute-start | bytes 1769480 | tf_op jit(solution)/shard_map/ppermute | solution.py:209
  64.1 2.6 %collective-permute-start.17 = (f32[128,768]{1,0:T(8,128)S(1)}, f32[128,768]{1,0:T(8,128)S(1)}, u32[]{:S(2)}, u32[]{:S(2)}) collective-permute-start(f32[128,768]{1,0:T(8,128)S(1)} %bitcast.14), channel_id=1, source_target_pairs={{0,1},{1,0},{2,3},{3,2},{4,5},{5,4},{6,7},{7,6},{8,9},{9,8},{10,11... | collective-permute-start | bytes 1179656 | tf_op jit(solution)/shard_map/ppermute | solution.py:209

commit v4 on v3

--- a/solution.py
+++ b/solution.py
@@ -50,8 +50,8 @@
 
 def score_kernel(
     q_hbm, codes_hbm, book_hbm, pos_hbm,
-    q_ref, e_ref, hits_ref, r_ref, stats_ref,
-    codes_ref, book_ref, pos_ref, qs_ref, s_ref, low_ref, book_t_ref, sems,
+    q_ref, codes_ref, e_ref, hits_ref, r_ref, stats_ref,
+    book_ref, pos_ref, qs_ref, s_ref, low_ref, book_t_ref, sems,
 ):
     rows, width = q_ref.shape
     subs, docs = codes_ref.shape
@@ -66,12 +66,6 @@
     loads[0].wait()
     book_t_ref[...] = book_ref[...].T
     loads[1].wait()
-    loads[2].wait()
-    loads[3].wait()
-    high, mid, low = split3(q_ref[...])
-    qs_ref[:, 0:width] = low
-    qs_ref[:, width : 2 * width] = mid
-    qs_ref[:, 2 * width : 3 * width] = high
     tile = 256
     for t in range(docs // tile):
         for sub in range(0, subs, 2):
@@ -88,6 +82,13 @@
                 r_ref[8 * sub : 8 * sub + 16, lanes] = high
                 r_ref[width + 8 * sub : width + 8 * sub + 16, lanes] = mid
                 low_ref[8 * sub : 8 * sub + 16, lanes] = low
+        if t == 0:
+            loads[2].wait()
+            loads[3].wait()
+            high, mid, low = split3(q_ref[...])
+            qs_ref[:, 0:width] = low
+            qs_ref[:, width : 2 * width] = mid
+            qs_ref[:, 2 * width : 3 * width] = high
         lanes = slice(t * tile, (t + 1) * tile)
         small = dot(qs_ref[:, 0 : 2 * width], r_ref[:, lanes]) + dot(
             qs_ref[:, 2 * width :], low_ref[:, lanes]
@@ -141,31 +142,32 @@
     out_ref[2:3, :] = own
 
 
-def terms_kernel(a_ref, b_ref, first_ref, u_ref, p_ref, keep_ref, send_ref, loss_ref, scale_ref, scale_col):
+def terms_kernel(a_ref, b_ref, first_ref, u_ref, p_ref, keep_ref, send_ref, loss_ref, scale_ref):
     top, total, own = join(a_ref[...], b_ref[...])
     log_total = top + jnp.log(total)
-    loss_ref[...] = (log_total - own).reshape(loss_ref.shape)
+    loss_ref[...] = log_total - own
     scale = jnp.exp(first_ref[0:1, :] - log_total)
     scale_ref[...] = scale
     half = keep_ref.shape[0]
-    scale_col[...] = column(scale).reshape(2, half, LANES)
     core = lax.axis_index("corpus") % 2
-    keep_ref[...] = u_ref[core] * scale_col[core][:, 0:1] - p_ref[core]
-    send_ref[...] = u_ref[1 - core] * scale_col[1 - core][:, 0:1] - p_ref[1 - core]
-
-
-def book_kernel(
-    e_ref, hits_ref, scale_ref, qt_ref, codes_ref,
-    keep_ref, send_ref, ws_ref, dg_ref, gt_ref, both_ref,
-):
-    rows, docs = e_ref.shape
-    width, words = gt_ref.shape
-    subs = codes_ref.shape[0]
+    first, second = scale[:, :half], scale[:, half:]
+    keep_ref[...] = u_ref[core] * column(jnp.where(core == 0, first, second))[:, 0:1] - p_ref[core]
+    send_ref[...] = u_ref[1 - core] * column(jnp.where(core == 0, second, first))[:, 0:1] - p_ref[1 - core]
+
+
+def doc_kernel(e_ref, hits_ref, scale_ref, qt_ref, dg_ref, ws_ref):
+    rows = e_ref.shape[0]
     w = e_ref[...] * column(scale_ref[...])[:, 0:1] - hits_ref[...].astype(F32)
     wh, wm = split2(w)
     ws_ref[0:rows, :] = wh
     ws_ref[rows:, :] = wm
     dg_ref[...] = dot(qt_ref[...], ws_ref[...]) + dot(qt_ref[:, rows:], ws_ref[0:rows, :])
+
+
+def book_kernel(dg_ref, codes_ref, after_ref, keep_ref, *refs):
+    sends, (gt_ref, both_ref) = refs[:-2], refs[-2:]
+    width, words = gt_ref.shape
+    subs, docs = codes_ref.shape
     coarse = words // FINE
     ramp = lax.broadcasted_iota(I32, (FINE, docs), 0).astype(F32).astype(BF16)
     for first in range(0, subs, 4):
@@ -189,7 +191,9 @@
     both_ref[...] = gt_ref[...].T.reshape(both_ref.shape)
     core = lax.axis_index("corpus") % 2
     keep_ref[...] = both_ref[core]
-    send_ref[...] = both_ref[1 - core]
+    piece = width // len(sends)
+    for i, send_ref in enumerate(sends):
+        send_ref[...] = both_ref[1 - core, :, i * piece : (i + 1) * piece]
 
 
 def call(kernel, outs, ins, scratch=(), flops=0, mib=16, name=None):
@@ -213,33 +217,43 @@
     return lax.axis_index(axis) // unit
 
 
-def cut(keep, got, axis, unit, count, after, name):
+def cut(keep, got, axis, unit, count, name):
     rows, width = keep.shape
-    shape = (count, rows // count, width)
-
-    def kernel(keep_ref, got_ref, after_ref, *outs):
+    rows //= count
+
+    def kernel(keep_ref, *refs):
         place = place_of(axis, unit)
-        for k, out in enumerate(outs):
-            out[...] = keep_ref[place ^ k] + got_ref[place ^ k]
-
-    blocks = call(kernel, [(shape[1:], F32)] * count, [VMEM, VMEM, VMEM], mib=4, name=name)(
-        keep.reshape(shape), got.reshape(shape), after
+        first = 0
+        for got_ref in refs[: len(got)]:
+            lanes = slice(first, first + got_ref.shape[2])
+            for k, out in enumerate(refs[len(got) :]):
+                out[:, lanes] = keep_ref[place ^ k, :, lanes] + got_ref[place ^ k]
+            first = lanes.stop
+
+    return call(kernel, [((rows, width), F32)] * count, [VMEM] * (1 + len(got)), mib=4, name=name)(
+        keep.reshape(count, rows, width), *[g.reshape(count, rows, g.shape[1]) for g in got]
     )
-    return list(blocks)
-
-
-def add(pieces, after, name):
-    count = len(pieces)
-
-    def kernel(*refs):
-        total = refs[0][...]
-        for ref in refs[1:count]:
-            total = total + ref[...]
-        refs[-1][...] = total
-
-    return call(kernel, [(pieces[0].shape, F32)], [VMEM] * (count + len(after)), mib=4, name=name)(
-        *pieces, *after
-    )[0]
+
+
+def add(whole, arrived, after, name, cuts=0):
+    arrived = [x if isinstance(x, list) else [x] for x in arrived]
+    flat = [block for x in arrived for block in x]
+    rows, width = whole.shape
+
+    def kernel(whole_ref, *refs):
+        out, *blocks = refs[len(flat) + len(after) :]
+        refs = iter(refs)
+        total = whole_ref[...]
+        for x in arrived:
+            total = total + jnp.concatenate([next(refs)[...] for _ in x], axis=1)
+        out[...] = total
+        for i, block in enumerate(blocks):
+            block[...] = total[:, i * (width // cuts) : (i + 1) * (width // cuts)]
+
+    outs = [((rows, width), F32)] + [((rows, width // max(cuts, 1)), F32)] * cuts
+    specs = [VMEM] * (1 + len(flat) + len(after))
+    total, *blocks = call(kernel, outs, specs, mib=4, name=name)(whole, *flat, *after)
+    return (total, blocks) if cuts else total
 
 
 def bit_at(step, core, count):
@@ -274,13 +288,16 @@
 
 def rejoin(own, got, step, after, name):
     rows, width = own.shape
-
-    def kernel(own_ref, got_ref, *refs):
+    piece = width // len(got)
+
+    def kernel(own_ref, *refs):
         mine = my_half(step)
         refs[-1][mine] = own_ref[...]
-        refs[-1][1 - mine] = got_ref[...]
-
-    whole = call(kernel, [((2, rows, width), F32)], [VMEM] * (2 + len(after)), mib=4, name=name)(own, got, *after)[0]
+        for i, got_ref in enumerate(refs[: len(got)]):
+            refs[-1][1 - mine, :, i * piece : (i + 1) * piece] = got_ref[...]
+
+    specs = [VMEM] * (1 + len(got) + len(after))
+    whole = call(kernel, [((2, rows, width), F32)], specs, mib=4, name=name)(own, *got, *after)[0]
     return whole.reshape(2 * rows, width)
 
 
@@ -300,32 +317,48 @@
     return whole.reshape(count * rows, width)
 
 
-def finish(own, got, after, name):
-    rows, width = own.shape
-
-    def kernel(own_ref, got_ref, *refs):
-        out_hbm, token_ref, sems = refs[len(after) :]
-        token_ref[...] = own_ref[0:8, 0:LANES]
-        core = lax.axis_index("corpus") % 2
-        copies = [
-            pltpu.make_async_copy(own_ref, out_hbm.at[core], sems.at[0]),
-            pltpu.make_async_copy(got_ref, out_hbm.at[1 - core], sems.at[1]),
+def finish(own, got, loss):
+    count = len(own)
+    shapes = tuple(pltpu.HBM((2,) + x.shape, F32) for x in own)
+    rows = loss.shape[1]
+
+    def stores(place, halves, outs, sems):
+        return [
+            pltpu.make_async_copy(half, out.at[place], sems.at[i])
+            for i, (half, out) in enumerate(zip(halves, outs))
         ]
+
+    def run(copies):
         for copy in copies:
             copy.start()
         for copy in copies:
             copy.wait()
 
-    whole, token = pl.pallas_call(
-        kernel,
-        out_shape=(jax.ShapeDtypeStruct((2, rows, width), F32), jax.ShapeDtypeStruct((8, LANES), F32)),
-        in_specs=[VMEM] * (2 + len(after)),
-        out_specs=(ANY, VMEM),
-        scratch_shapes=[pltpu.SemaphoreType.DMA((2,))],
-        compiler_params=pltpu.CompilerParams(vmem_limit_bytes=4 * 2**20),
-        name=name,
-    )(own, got, *after)
-    return whole.reshape(2 * rows, width), token
+    def first(*refs):
+        loss_ref, *halves = refs[: count + 1]
+        loss_out, *outs = refs[count + 1 : 2 * count + 2]
+        line, sems = refs[-2:]
+        line[...] = loss_ref[...].reshape(rows)
+        run(
+            stores(lax.axis_index("corpus") % 2, halves, outs, sems)
+            + [pltpu.make_async_copy(line, loss_out, sems.at[count])]
+        )
+
+    def second(*refs):
+        run(stores(1 - lax.axis_index("corpus") % 2, refs[count : 2 * count], refs[2 * count : 3 * count], refs[-1]))
+
+    params = pltpu.CompilerParams(vmem_limit_bytes=4 * 2**20)
+    loss, *half = pl.pallas_call(
+        first, out_shape=(pltpu.HBM((rows,), F32),) + shapes, in_specs=[VMEM] * (count + 1),
+        out_specs=(HBM,) * (count + 1), compiler_params=params, name="finish_own",
+        scratch_shapes=[pltpu.VMEM((rows,), F32), pltpu.SemaphoreType.DMA((count + 1,))],
+    )(loss, *own)
+    whole = pl.pallas_call(
+        second, out_shape=shapes, in_specs=[HBM] * count + [VMEM] * count, out_specs=(HBM,) * count,
+        scratch_shapes=[pltpu.SemaphoreType.DMA((count,))], compiler_params=params,
+        input_output_aliases={i: i for i in range(count)}, name="finish_got",
+    )(*half, *got)
+    return [w.reshape(2 * x.shape[0], x.shape[1]) for w, x in zip(whole, own)] + [loss]
 
 
 def local(queries, codes, positive, codebook):
@@ -336,12 +369,11 @@
     chips = corpus // 2
     codes_t = codes.T
     work = rows * docs * width
-    q, e, hits, r, stats = call(
+    q, codes_here, e, hits, r, stats = call(
         score_kernel,
-        [((rows, width), F32), ((rows, docs), F32), ((rows, docs), BF16), ((2 * width, docs), BF16), ((8, rows), F32)],
+        [((rows, width), F32), ((subs, docs), I32), ((rows, docs), F32), ((rows, docs), BF16), ((2 * width, docs), BF16), ((8, rows), F32)],
         [HBM] * 4,
         [
-            pltpu.VMEM((subs, docs), I32),
             pltpu.VMEM((words, width), F32),
             pltpu.VMEM((rows,), I32),
             pltpu.VMEM((rows, 3 * width), BF16),
@@ -365,50 +397,47 @@
     half = rows // 2
     keep, send, loss, scale = call(
         terms_kernel,
-        [((half, width), F32), ((half, width), F32), ((rows,), F32), ((1, rows), F32)],
+        [((half, width), F32), ((half, width), F32), ((1, rows), F32), ((1, rows), F32)],
         [VMEM] * 5,
-        [pltpu.VMEM((2, half, LANES), F32)],
         mib=8,
     )(joined, got, stats, u.reshape(2, half, width), p.reshape(2, half, width))
 
+    bits = chips.bit_length() - 1
     part_rows = words // 2
-    book_keep, book_send = call(
+    dg = call(
+        doc_kernel, [((width, docs), F32)], [VMEM] * 4, [pltpu.VMEM((2 * rows, docs), BF16)], 6 * work
+    )(e, hits, scale, qt)[0]
+    q_keep, q_send = halve(keep, swap(send, "corpus", 1), 0, [dg], "query_halve")
+    book_keep, *book_send = call(
         book_kernel,
-        [((part_rows, width), F32)] * 2,
-        [VMEM] * 5,
-        [
-            pltpu.VMEM((2 * rows, docs), BF16),
-            pltpu.VMEM((width, docs), F32),
-            pltpu.VMEM((width, words), F32),
-            pltpu.VMEM((2, part_rows, width), F32),
-        ],
-        14 * work,
-    )(e, hits, scale, qt, codes_t)
-
-    bits = chips.bit_length() - 1
-    q_keep, q_send = halve(keep, swap(send, "corpus", 1), 0, [], "query_halve")
-    b_cuts = cut(book_keep, swap(book_send, "corpus", 1), "query", 1, query, scale, "book_cut")
+        [((part_rows, width), F32)] + [((part_rows, width // 2), F32)] * 2,
+        [VMEM] * 3,
+        [pltpu.VMEM((width, words), F32), pltpu.VMEM((2, part_rows, width), F32)],
+        8 * work,
+    )(dg, codes_here, q_keep)
+
+    b_cuts = cut(book_keep, [swap(x, "corpus", 1) for x in book_send], "query", 1, query, "book_cut")
     b_got = [swap(b_cuts[k], "query", k) for k in range(1, query)]
-    b_own = b_sum = add([b_cuts[0]] + b_got, [], "book_sum")
+    b_own = b_sum = add(b_cuts[0], b_got, [], "book_sum")
     for step in range(bits - 1):
         q_got = chip_swap(q_send, step)
         if step < bits - 2:
             q_keep, q_send = halve(q_keep, q_got, step + 1, [], "query_halve")
-    q_own = add([q_keep, q_got], [b_sum], "query_add")
+    q_own, q_parts = add(q_keep, [q_got], [b_cuts[0]], "query_add", 1)
     for step in range(bits - 1):
-        b_own = add([b_own, chip_swap(b_own, step)], [], "book_join")
+        b_own = add(b_own, [chip_swap(b_own, step)], [], "book_join")
     b_mid = b_own
-    b_last = chip_swap(b_own, bits - 1)
-    q_last = chip_swap(q_own, bits - 1)
-    b_own = add([b_own, b_last], [], "book_join")
-    q_own = add([q_own, q_last], [b_own], "query_all")
+    b_own = b_last = add(b_own, [chip_swap(b_own, bits - 1)], [], "book_join")
     blocks = [b_own] + [swap(b_own, "query", k) for k in range(1, query)]
     b_whole = put(blocks, "query", 1, [], "book_put")
-    q_whole = q_own
+    b_got = swap(b_whole, "corpus", 1)
+    q_whole, q_parts = add(q_own, [[chip_swap(x, bits - 1) for x in q_parts]], [b_last], "query_all", 1)
     for step in reversed(range(bits - 1)):
-        q_whole = rejoin(q_whole, chip_swap(q_whole, step), step, [b_whole], "query_put")
-    grad_codebook, token = finish(b_whole, swap(b_whole, "corpus", 1), [], "book_finish")
-    grad_queries, token = finish(q_whole, swap(q_whole, "corpus", 1), [token], "query_finish")
+        q_got = [chip_swap(x, step) for x in q_parts]
+        q_whole, q_parts = rejoin(q_whole, q_got, step, [b_whole], "query_put"), None
+        q_parts = [q_whole]
+    q_got = swap(q_whole, "corpus", 1)
+    grad_queries, grad_codebook, loss = finish([q_whole, b_whole], [q_got, b_got], loss)
     return grad_queries, grad_codebook, loss
 
 

time: 69.5 us -> 64.6 us (0.929)
  waiting for transfers between devices: 21.3 us -> 17.2 us
  Pallas kernels: 21.9 us -> 20.9 us
    ppermute x5, waiting for transfers between devices: 9.08 us -> 6.18 us  [chip_swap(): lax.ppermute(x, 'corpus', [(i, i ^ 2 << bit_at(step, i % 2, count)) for i...]
    ppermute x13 -> x14, waiting for transfers between devices: 12.3 us -> 11 us  [swap(): lax.ppermute(x, axis, [(i, i ^ bits) for i in range(lax.axis_size(axis))])]
    pallas_call x12 -> x13, Pallas kernels: 17.9 us -> 16.9 us  [the longest x1 7.87 us: local(): call(score_kernel, [((rows, width), F32), ((subs, docs), I32), ((rows, do...]
    ppermute x13 -> x14, starting transfers between devices: 14.3 us -> 15.3 us  [swap(): lax.ppermute(x, axis, [(i, i ^ bits) for i in range(lax.axis_size(axis))])]
  transfers between devices with their start and end apart: 18 -> 19, of which waited for: 11 -> 12; matrix products, arithmetic and copies ran while one was open for 0% -> 0% of each run, Pallas kernels for 16% -> 18%
where the time goes in v4:
time: 64.6 us; the launch traced here: 64.5 us
  starting transfers between devices  25.5 us (39%)
  Pallas kernels  20.9 us (32%)
  waiting for transfers between devices  17.2 us (27%)
  between operations  0.96 us (1%)
    ppermute x14, starting transfers between devices, swap(): lax.ppermute(x, axis, [(i, i ^ bits) for i in range(lax.axis_size(axis))])  15.3 us
    ppermute x14, waiting for transfers between devices, swap(): lax.ppermute(x, axis, [(i, i ^ bits) for i in range(lax.axis_size(axis))])  11 us
    ppermute x5, starting transfers between devices, chip_swap(): lax.ppermute(x, 'corpus', [(i, i ^ 2 << bit_at(step, i % 2, count)) for i...  10.2 us
    pallas_call x1, Pallas kernels, local(): call(score_kernel, [((rows, width), F32), ((subs, docs), I32), ((rows, do...  7.87 us
    ppermute x5, waiting for transfers between devices, chip_swap(): lax.ppermute(x, 'corpus', [(i, i ^ 2 << bit_at(step, i % 2, count)) for i...  6.18 us
    pallas_call x1, Pallas kernels, local(): call(book_kernel, [((part_rows, width), F32)] + [((part_rows, width // 2)...  3.99 us
    pallas_call x1, Pallas kernels, local(): call(doc_kernel, [((width, docs), F32)], [VMEM] * 4, [pltpu.VMEM((2 * row...  2.46 us
    pallas_call x1, Pallas kernels, local(): call(spread_kernel, [((rows, width), F32)], [VMEM] * 2, (), 6 * work)(e, r)  2.07 us
  transfers between devices with their start and end apart: 19, of which 12 were waited for; matrix products, arithmetic and copies ran while one was open for 0% of the time, Pallas kernels for 18%

profile of v4, /device:TPU:0, one launch (start us, length us, event | category | flops | bytes accessed | tf_op | source)
XLA Modules:
  0.0 64.5 jit_solution(5522382750363733351)
XLA Ops:
  0.6 7.9 %score_kernel.1 = (f32[384,768]{1,0:T(8,128)S(1)}, s32[96,1024]{1,0:T(8,128)S(1)}, f32[384,1024]{1,0:T(8,128)S(1)}, bf16[384,1024]{1,0:T(8,128)(2,1)S(1)}, bf16[...) custom-call(f32[384,768]{1,0:T(8,128)} %q_hbm.1, s32[96,1024]{1,0:T(8,128)} %bitcast.26, f32[256,768]{1,0:T(8,128)} %book_hbm.1, ...), custom_call_target="tpu_custom_call" | custom-call | flops 3623878656 | bytes 131072 | tf_op jit(solution)/shard_map/score_kernel/pallas_call | solution.py:372
  8.5 0.5 collective-permute-start
  9.0 0.4 turn_kernel.1.after_ref.qt_ref
  9.4 0.5 collective-permute-done.b_ref
  9.9 3.0 %collective-permute-start.1 = (f32[8,384]{1,0:T(8,128)S(1)}, f32[8,384]{1,0:T(8,128)S(1)}, u32[]{:S(2)}, u32[]{:S(2)}) collective-permute-start(f32[8,384]{1,0:T(8,128)S(1)} %join_kernel.2.a_ref), channel_id=1, source_target_pairs={{0,2},{1,3},{2,0},{3,1},{4,6},{5,7},{6,4},{7,5},{8,10},{9,11},{10,... | collective-permute-start | bytes 36872 | tf_op jit(solution)/shard_map/ppermute | solution.py:213
  12.9 2.1 %spread_kernel.1.after_ref = f32[384,768]{1,0:T(8,128)S(1)} custom-call(f32[384,1024]{1,0:T(8,128)S(1)} %get-tuple-element.33.e_ref, bf16[1536,1024]{1,0:T(8,128)(2,1)S(1)} %get-tuple-element.34.r_ref), custom_call_target="tpu_custom_call" | custom-call | flops 1811939328 | bytes 131072 | tf_op jit(solution)/shard_map/spread_kernel/pallas_call | solution.py:388
  14.9 0.0 collective-permute-done.1.b_ref
  15.0 2.7 %collective-permute-start.2 = (f32[8,384]{1,0:T(8,128)S(1)}, f32[8,384]{1,0:T(8,128)S(1)}, u32[]{:S(2)}, u32[]{:S(2)}) collective-permute-start(f32[8,384]{1,0:T(8,128)S(1)} %join_kernel.3.after_ref.a_ref), channel_id=1, source_target_pairs={{0,4},{1,5},{2,6},{3,7},{4,0},{5,1},{6,2},{7,3},{8,12},{9,13},{10,... | collective-permute-start | bytes 36872 | tf_op jit(solution)/shard_map/ppermute | solution.py:213
  17.7 1.4 %positive_kernel.1 = f32[384,768]{1,0:T(8,128)S(1)} custom-call(bf16[384,1024]{1,0:T(8,128)(2,1)S(1)} %get-tuple-element.35.hits_ref, bf16[1536,1024]{1,0:T(8,128)(2,1)S(1)} %get-tuple-element.34.r_ref, f32[8,384]{1,0:T(8,128)S(1)} %join_kernel.3.after_ref.a_ref), custom_call_target="tpu_custom_call" | custom-call | flops 1207959552 | bytes 131072 | tf_op jit(solution)/shard_map/positive_kernel/pallas_call | solution.py:396
  19.1 0.6 collective-permute-done.2.b_ref
  19.6 0.4 terms_kernel.1
  20.0 0.1 collective-permute-start.3
  20.1 2.5 %doc_kernel.1.refs_0_.dg_ref = f32[768,1024]{1,0:T(8,128)S(1)} custom-call(f32[384,1024]{1,0:T(8,128)S(1)} %get-tuple-element.33.e_ref, bf16[384,1024]{1,0:T(8,128)(2,1)S(1)} %get-tuple-element.35.hits_ref, f32[1,384]{1,0:T(1,128)S(1)} %get-tuple-element.39.scale_ref, bf16[768,768]{1,0:T(8,128)(2,1)S(1)} %turn_kernel.1.after_ref.qt_ref), custom_call_target="tpu_custom_call" | custom-call | flops 1811939328 | bytes 131072 | tf_op jit(solution)/shard_map/doc_kernel/pallas_call | solution.py:407
  22.6 0.0 collective-permute-done.3
  22.6 0.1 query_halve.1
  22.7 1.7 %collective-permute-start.4 = (f32[96,768]{1,0:T(8,128)S(1)}, f32[96,768]{1,0:T(8,128)S(1)}, u32[]{:S(2)}, u32[]{:S(2)}) collective-permute-start(f32[96,768]{1,0:T(8,128)S(1)} %get-tuple-element.41), channel_id=1, source_target_pairs={{0,2},{1,5},{2,0},{3,7},{4,6},{5,1},{6,4},{7,3},{8,10},{9,13},{10,... | collective-permute-start | bytes 884744 | tf_op jit(solution)/shard_map/ppermute | solution.py:266
  24.3 4.0 %book_kernel.1 = (f32[128,768]{1,0:T(8,128)S(1)}, f32[128,384]{1,0:T(8,128)S(1)}, f32[128,384]{1,0:T(8,128)S(1)}) custom-call(f32[768,1024]{1,0:T(8,128)S(1)} %doc_kernel.1.refs_0_.dg_ref, s32[96,1024]{1,0:T(8,128)S(1)} %get-tuple-element.42.codes_ref, f32[96,768]{1,0:T(8,128)S(1)} %get-tuple-element.40.after_ref.whole_ref), custom_call_target="tpu_custom_call" | custom-call | flops 2415919104 | bytes 131072 | tf_op jit(solution)/shard_map/book_kernel/pallas_call | solution.py:411
  28.3 1.3 %collective-permute-start.5 = (f32[128,384]{1,0:T(8,128)S(1)}, f32[128,384]{1,0:T(8,128)S(1)}, u32[]{:S(2)}, u32[]{:S(2)}) collective-permute-start(f32[128,384]{1,0:T(8,128)S(1)} %get-tuple-element.44), channel_id=1, source_target_pairs={{0,1},{1,0},{2,3},{3,2},{4,5},{5,4},{6,7},{7,6},{8,9},{9,8},{10,11... | collective-permute-start | bytes 589832 | tf_op jit(solution)/shard_map/ppermute | solution.py:213
  29.6 0.1 collective-permute-start.6
  29.7 1.0 %collective-permute-done.5 = f32[128,384]{1,0:T(8,128)S(1)} collective-permute-done((f32[128,384]{1,0:T(8,128)S(1)}, f32[128,384]{1,0:T(8,128)S(1)}, u32[]{:S(2)}, u32[]{:S(2)}) %collective-permute-start.5) | collective-permute-done | bytes 196640 | tf_op jit(solution)/shard_map/ppermute | solution.py:213
  30.7 0.4 collective-permute-done.6
  31.1 1.6 %collective-permute-start.8 = (f32[32,768]{1,0:T(8,128)S(1)}, f32[32,768]{1,0:T(8,128)S(1)}, u32[]{:S(2)}, u32[]{:S(2)}) collective-permute-start(f32[32,768]{1,0:T(8,128)S(1)} %get-tuple-element.49), channel_id=1, source_target_pairs={{0,8},{8,0},{16,24},{24,16},{1,9},{9,1},{17,25},{25,17},{2,10},{10... | collective-permute-start | bytes 294920 | tf_op jit(solution)/shard_map/ppermute | solution.py:213
  32.7 1.5 %collective-permute-start.9 = (f32[32,768]{1,0:T(8,128)S(1)}, f32[32,768]{1,0:T(8,128)S(1)}, u32[]{:S(2)}, u32[]{:S(2)}) collective-permute-start(f32[32,768]{1,0:T(8,128)S(1)} %get-tuple-element.50), channel_id=1, source_target_pairs={{0,16},{8,24},{16,0},{24,8},{1,17},{9,25},{17,1},{25,9},{2,18},{10... | collective-permute-start | bytes 294920 | tf_op jit(solution)/shard_map/ppermute | solution.py:213
  34.2 0.5 collective-permute-start.10
  34.7 0.0 collective-permute-done.4.refs_0_
  34.7 1.7 %collective-permute-start.7 = (f32[96,768]{1,0:T(8,128)S(1)}, f32[96,768]{1,0:T(8,128)S(1)}, u32[]{:S(2)}, u32[]{:S(2)}) collective-permute-start(f32[96,768]{1,0:T(8,128)S(1)} %get-tuple-element.48), channel_id=1, source_target_pairs={{0,4},{1,3},{2,6},{3,1},{4,0},{5,7},{6,2},{7,5},{8,12},{9,11},{10,... | collective-permute-start | bytes 884744 | tf_op jit(solution)/shard_map/ppermute | solution.py:266
  36.4 0.0 collective-permute-done.8.refs_0_
  36.4 2.1 %collective-permute-done.9.refs_1_ = f32[32,768]{1,0:T(8,128)S(1)} collective-permute-done((f32[32,768]{1,0:T(8,128)S(1)}, f32[32,768]{1,0:T(8,128)S(1)}, u32[]{:S(2)}, u32[]{:S(2)}) %collective-permute-start.9) | collective-permute-done | bytes 98336 | tf_op jit(solution)/shard_map/ppermute | solution.py:213
  38.5 1.2 %collective-permute-done.10.refs_2_ = f32[32,768]{1,0:T(8,128)S(1)} collective-permute-done((f32[32,768]{1,0:T(8,128)S(1)}, f32[32,768]{1,0:T(8,128)S(1)}, u32[]{:S(2)}, u32[]{:S(2)}) %collective-permute-start.10) | collective-permute-done | bytes 98336 | tf_op jit(solution)/shard_map/ppermute | solution.py:213
  39.7 1.7 %collective-permute-start.11 = (f32[32,768]{1,0:T(8,128)S(1)}, f32[32,768]{1,0:T(8,128)S(1)}, u32[]{:S(2)}, u32[]{:S(2)}) collective-permute-start(f32[32,768]{1,0:T(8,128)S(1)} %book_sum.1.whole_ref), channel_id=1, source_target_pairs={{0,2},{1,5},{2,0},{3,7},{4,6},{5,1},{6,4},{7,3},{8,10},{9,13},{10,... | collective-permute-start | bytes 294920 | tf_op jit(solution)/shard_map/ppermute | solution.py:266
  41.4 3.0 %collective-permute-done.11.refs_0_ = f32[32,768]{1,0:T(8,128)S(1)} collective-permute-done((f32[32,768]{1,0:T(8,128)S(1)}, f32[32,768]{1,0:T(8,128)S(1)}, u32[]{:S(2)}, u32[]{:S(2)}) %collective-permute-start.11) | collective-permute-done | bytes 98336 | tf_op jit(solution)/shard_map/ppermute | solution.py:266
  44.4 2.6 %collective-permute-start.12 = (f32[32,768]{1,0:T(8,128)S(1)}, f32[32,768]{1,0:T(8,128)S(1)}, u32[]{:S(2)}, u32[]{:S(2)}) collective-permute-start(f32[32,768]{1,0:T(8,128)S(1)} %book_join.2.whole_ref), channel_id=1, source_target_pairs={{0,4},{1,3},{2,6},{3,1},{4,0},{5,7},{6,2},{7,5},{8,12},{9,11},{10,... | collective-permute-start | bytes 294920 | tf_op jit(solution)/shard_map/ppermute | solution.py:266
  47.0 3.1 %collective-permute-done.12.refs_0_ = f32[32,768]{1,0:T(8,128)S(1)} collective-permute-done((f32[32,768]{1,0:T(8,128)S(1)}, f32[32,768]{1,0:T(8,128)S(1)}, u32[]{:S(2)}, u32[]{:S(2)}) %collective-permute-start.12) | collective-permute-done | bytes 98336 | tf_op jit(solution)/shard_map/ppermute | solution.py:266
  50.1 0.0 collective-permute-done.7.refs_0_
  50.2 2.6 %collective-permute-start.13 = (f32[96,768]{1,0:T(8,128)S(1)}, f32[96,768]{1,0:T(8,128)S(1)}, u32[]{:S(2)}, u32[]{:S(2)}) collective-permute-start(f32[96,768]{1,0:T(8,128)S(1)} %get-tuple-element.53), channel_id=1, source_target_pairs={{0,2},{1,5},{2,0},{3,7},{4,6},{5,1},{6,4},{7,3},{8,10},{9,13},{10,... | collective-permute-start | bytes 884744 | tf_op jit(solution)/shard_map/ppermute | solution.py:266
  52.8 2.2 %collective-permute-start.16 = (f32[32,768]{1,0:T(8,128)S(1)}, f32[32,768]{1,0:T(8,128)S(1)}, u32[]{:S(2)}, u32[]{:S(2)}) collective-permute-start(f32[32,768]{1,0:T(8,128)S(1)} %book_join.3.refs_1_.refs_0_), channel_id=1, source_target_pairs={{0,24},{8,16},{16,8},{24,0},{1,25},{9,17},{17,9},{25,1},{2,26},{10... | collective-permute-start | bytes 294920 | tf_op jit(solution)/shard_map/ppermute | solution.py:213
  55.1 0.9 %collective-permute-start.15 = (f32[32,768]{1,0:T(8,128)S(1)}, f32[32,768]{1,0:T(8,128)S(1)}, u32[]{:S(2)}, u32[]{:S(2)}) collective-permute-start(f32[32,768]{1,0:T(8,128)S(1)} %book_join.3.refs_1_.refs_0_), channel_id=1, source_target_pairs={{0,16},{8,24},{16,0},{24,8},{1,17},{9,25},{17,1},{25,9},{2,18},{10... | collective-permute-start | bytes 294920 | tf_op jit(solution)/shard_map/ppermute | solution.py:213
  56.0 0.4 collective-permute-start.14
  56.3 2.9 %collective-permute-done.16.refs_3_ = f32[32,768]{1,0:T(8,128)S(1)} collective-permute-done((f32[32,768]{1,0:T(8,128)S(1)}, f32[32,768]{1,0:T(8,128)S(1)}, u32[]{:S(2)}, u32[]{:S(2)}) %collective-permute-start.16) | collective-permute-done | bytes 98336 | tf_op jit(solution)/shard_map/ppermute | solution.py:213
  59.2 0.8 %collective-permute-done.15.refs_2_ = f32[32,768]{1,0:T(8,128)S(1)} collective-permute-done((f32[32,768]{1,0:T(8,128)S(1)}, f32[32,768]{1,0:T(8,128)S(1)}, u32[]{:S(2)}, u32[]{:S(2)}) %collective-permute-start.15) | collective-permute-done | bytes 98336 | tf_op jit(solution)/shard_map/ppermute | solution.py:213
  60.1 0.5 collective-permute-done.14.refs_1_
  60.6 0.0 collective-permute-done.13.refs_0_
  60.6 0.1 query_put.1
  60.7 0.2 collective-permute-start.17
  60.9 0.4 collective-permute-start.18
  61.3 1.0 %finish_own.1 = (f32[384]{0:T(512)}, f32[2,192,768]{2,1,0:T(8,128)}, f32[2,128,768]{2,1,0:T(8,128)}) custom-call(f32[1,384]{1,0:T(1,128)S(1)} %get-tuple-element.36.refs_0_, f32[192,768]{1,0:T(8,128)S(1)} %bitcast.18, f32[128,768]{1,0:T(8,128)S(1)} %bitcast.16), custom_call_target="tpu_custom_call" | custom-call | tf_op jit(solution)/shard_map/finish_own/pallas_call | solution.py:351
  62.3 1.1 %collective-permute-done.18.refs_3_ = f32[128,768]{1,0:T(8,128)S(1)} collective-permute-done((f32[128,768]{1,0:T(8,128)S(1)}, f32[128,768]{1,0:T(8,128)S(1)}, u32[]{:S(2)}, u32[]{:S(2)}) %collective-permute-start.18) | collective-permute-done | bytes 393248 | tf_op jit(solution)/shard_map/ppermute | solution.py:213
  63.3 0.0 collective-permute-done.17.refs_2_
  63.3 1.0 %finish_got.1 = (f32[2,192,768]{2,1,0:T(8,128)}, f32[2,128,768]{2,1,0:T(8,128)}) custom-call(f32[2,192,768]{2,1,0:T(8,128)} %get-tuple-element.54.refs_0_, f32[2,128,768]{2,1,0:T(8,128)} %get-tuple-element.55.refs_1_, f32[192,768]{1,0:T(8,128)S(1)} %collective-permute-done.17.refs_2_, ...), custom_call_target="tpu_custom_call", output_to_operand_aliasing={{0}: (0, {}), {1}: (1, {})} | custom-call | tf_op jit(solution)/shard_map/finish_got/pallas_call | solution.py:356
  (9 shorter events, 0.2 us)
Async XLA Ops:
  8.5 1.4 %collective-permute-start = (f32[8,384]{1,0:T(8,128)S(1)}, f32[8,384]{1,0:T(8,128)S(1)}, u32[]{:S(2)}, u32[]{:S(2)}) collective-permute-start(f32[8,384]{1,0:T(8,128)S(1)} %get-tuple-element.31.a_ref.first_ref), channel_id=1, source_target_pairs={{0,1},{1,0},{2,3},{3,2},{4,5},{5,4},{6,7},{7,6},{8,9},{9,8},{10,11... | collective-permute-start | bytes 36872 | tf_op jit(solution)/shard_map/ppermute | solution.py:213
  9.9 5.1 %collective-permute-start.1 = (f32[8,384]{1,0:T(8,128)S(1)}, f32[8,384]{1,0:T(8,128)S(1)}, u32[]{:S(2)}, u32[]{:S(2)}) collective-permute-start(f32[8,384]{1,0:T(8,128)S(1)} %join_kernel.2.a_ref), channel_id=1, source_target_pairs={{0,2},{1,3},{2,0},{3,1},{4,6},{5,7},{6,4},{7,5},{8,10},{9,11},{10,... | collective-permute-start | bytes 36872 | tf_op jit(solution)/shard_map/ppermute | solution.py:213
  15.0 4.7 %collective-permute-start.2 = (f32[8,384]{1,0:T(8,128)S(1)}, f32[8,384]{1,0:T(8,128)S(1)}, u32[]{:S(2)}, u32[]{:S(2)}) collective-permute-start(f32[8,384]{1,0:T(8,128)S(1)} %join_kernel.3.after_ref.a_ref), channel_id=1, source_target_pairs={{0,4},{1,5},{2,6},{3,7},{4,0},{5,1},{6,2},{7,3},{8,12},{9,13},{10,... | collective-permute-start | bytes 36872 | tf_op jit(solution)/shard_map/ppermute | solution.py:213
  20.0 2.6 %collective-permute-start.3 = (f32[192,768]{1,0:T(8,128)S(1)}, f32[192,768]{1,0:T(8,128)S(1)}, u32[]{:S(2)}, u32[]{:S(2)}) collective-permute-start(f32[192,768]{1,0:T(8,128)S(1)} %get-tuple-element.38), channel_id=1, source_target_pairs={{0,1},{1,0},{2,3},{3,2},{4,5},{5,4},{6,7},{7,6},{8,9},{9,8},{10,11... | collective-permute-start | bytes 1769480 | tf_op jit(solution)/shard_map/ppermute | solution.py:213
  22.7 12.0 %collective-permute-start.4 = (f32[96,768]{1,0:T(8,128)S(1)}, f32[96,768]{1,0:T(8,128)S(1)}, u32[]{:S(2)}, u32[]{:S(2)}) collective-permute-start(f32[96,768]{1,0:T(8,128)S(1)} %get-tuple-element.41), channel_id=1, source_target_pairs={{0,2},{1,5},{2,0},{3,7},{4,6},{5,1},{6,4},{7,3},{8,10},{9,13},{10,... | collective-permute-start | bytes 884744 | tf_op jit(solution)/shard_map/ppermute | solution.py:266
  28.3 2.4 %collective-permute-start.5 = (f32[128,384]{1,0:T(8,128)S(1)}, f32[128,384]{1,0:T(8,128)S(1)}, u32[]{:S(2)}, u32[]{:S(2)}) collective-permute-start(f32[128,384]{1,0:T(8,128)S(1)} %get-tuple-element.44), channel_id=1, source_target_pairs={{0,1},{1,0},{2,3},{3,2},{4,5},{5,4},{6,7},{7,6},{8,9},{9,8},{10,11... | collective-permute-start | bytes 589832 | tf_op jit(solution)/shard_map/ppermute | solution.py:213
  29.6 1.4 %collective-permute-start.6 = (f32[128,384]{1,0:T(8,128)S(1)}, f32[128,384]{1,0:T(8,128)S(1)}, u32[]{:S(2)}, u32[]{:S(2)}) collective-permute-start(f32[128,384]{1,0:T(8,128)S(1)} %get-tuple-element.45), channel_id=1, source_target_pairs={{0,1},{1,0},{2,3},{3,2},{4,5},{5,4},{6,7},{7,6},{8,9},{9,8},{10,11... | collective-permute-start | bytes 589832 | tf_op jit(solution)/shard_map/ppermute | solution.py:213
  31.1 5.3 %collective-permute-start.8 = (f32[32,768]{1,0:T(8,128)S(1)}, f32[32,768]{1,0:T(8,128)S(1)}, u32[]{:S(2)}, u32[]{:S(2)}) collective-permute-start(f32[32,768]{1,0:T(8,128)S(1)} %get-tuple-element.49), channel_id=1, source_target_pairs={{0,8},{8,0},{16,24},{24,16},{1,9},{9,1},{17,25},{25,17},{2,10},{10... | collective-permute-start | bytes 294920 | tf_op jit(solution)/shard_map/ppermute | solution.py:213
  32.7 5.8 %collective-permute-start.9 = (f32[32,768]{1,0:T(8,128)S(1)}, f32[32,768]{1,0:T(8,128)S(1)}, u32[]{:S(2)}, u32[]{:S(2)}) collective-permute-start(f32[32,768]{1,0:T(8,128)S(1)} %get-tuple-element.50), channel_id=1, source_target_pairs={{0,16},{8,24},{16,0},{24,8},{1,17},{9,25},{17,1},{25,9},{2,18},{10... | collective-permute-start | bytes 294920 | tf_op jit(solution)/shard_map/ppermute | solution.py:213
  34.2 5.5 %collective-permute-start.10 = (f32[32,768]{1,0:T(8,128)S(1)}, f32[32,768]{1,0:T(8,128)S(1)}, u32[]{:S(2)}, u32[]{:S(2)}) collective-permute-start(f32[32,768]{1,0:T(8,128)S(1)} %get-tuple-element.51), channel_id=1, source_target_pairs={{0,24},{8,16},{16,8},{24,0},{1,25},{9,17},{17,9},{25,1},{2,26},{10... | collective-permute-start | bytes 294920 | tf_op jit(solution)/shard_map/ppermute | solution.py:213
  34.7 15.4 %collective-permute-start.7 = (f32[96,768]{1,0:T(8,128)S(1)}, f32[96,768]{1,0:T(8,128)S(1)}, u32[]{:S(2)}, u32[]{:S(2)}) collective-permute-start(f32[96,768]{1,0:T(8,128)S(1)} %get-tuple-element.48), channel_id=1, source_target_pairs={{0,4},{1,3},{2,6},{3,1},{4,0},{5,7},{6,2},{7,5},{8,12},{9,11},{10,... | collective-permute-start | bytes 884744 | tf_op jit(solution)/shard_map/ppermute | solution.py:266
  39.7 4.7 %collective-permute-start.11 = (f32[32,768]{1,0:T(8,128)S(1)}, f32[32,768]{1,0:T(8,128)S(1)}, u32[]{:S(2)}, u32[]{:S(2)}) collective-permute-start(f32[32,768]{1,0:T(8,128)S(1)} %book_sum.1.whole_ref), channel_id=1, source_target_pairs={{0,2},{1,5},{2,0},{3,7},{4,6},{5,1},{6,4},{7,3},{8,10},{9,13},{10,... | collective-permute-start | bytes 294920 | tf_op jit(solution)/shard_map/ppermute | solution.py:266
  44.4 5.7 %collective-permute-start.12 = (f32[32,768]{1,0:T(8,128)S(1)}, f32[32,768]{1,0:T(8,128)S(1)}, u32[]{:S(2)}, u32[]{:S(2)}) collective-permute-start(f32[32,768]{1,0:T(8,128)S(1)} %book_join.2.whole_ref), channel_id=1, source_target_pairs={{0,4},{1,3},{2,6},{3,1},{4,0},{5,7},{6,2},{7,5},{8,12},{9,11},{10,... | collective-permute-start | bytes 294920 | tf_op jit(solution)/shard_map/ppermute | solution.py:266
  50.2 10.4 %collective-permute-start.13 = (f32[96,768]{1,0:T(8,128)S(1)}, f32[96,768]{1,0:T(8,128)S(1)}, u32[]{:S(2)}, u32[]{:S(2)}) collective-permute-start(f32[96,768]{1,0:T(8,128)S(1)} %get-tuple-element.53), channel_id=1, source_target_pairs={{0,2},{1,5},{2,0},{3,7},{4,6},{5,1},{6,4},{7,3},{8,10},{9,13},{10,... | collective-permute-start | bytes 884744 | tf_op jit(solution)/shard_map/ppermute | solution.py:266
  52.8 6.4 %collective-permute-start.16 = (f32[32,768]{1,0:T(8,128)S(1)}, f32[32,768]{1,0:T(8,128)S(1)}, u32[]{:S(2)}, u32[]{:S(2)}) collective-permute-start(f32[32,768]{1,0:T(8,128)S(1)} %book_join.3.refs_1_.refs_0_), channel_id=1, source_target_pairs={{0,24},{8,16},{16,8},{24,0},{1,25},{9,17},{17,9},{25,1},{2,26},{10... | collective-permute-start | bytes 294920 | tf_op jit(solution)/shard_map/ppermute | solution.py:213
  55.1 5.0 %collective-permute-start.15 = (f32[32,768]{1,0:T(8,128)S(1)}, f32[32,768]{1,0:T(8,128)S(1)}, u32[]{:S(2)}, u32[]{:S(2)}) collective-permute-start(f32[32,768]{1,0:T(8,128)S(1)} %book_join.3.refs_1_.refs_0_), channel_id=1, source_target_pairs={{0,16},{8,24},{16,0},{24,8},{1,17},{9,25},{17,1},{25,9},{2,18},{10... | collective-permute-start | bytes 294920 | tf_op jit(solution)/shard_map/ppermute | solution.py:213
  56.0 4.6 %collective-permute-start.14 = (f32[32,768]{1,0:T(8,128)S(1)}, f32[32,768]{1,0:T(8,128)S(1)}, u32[]{:S(2)}, u32[]{:S(2)}) collective-permute-start(f32[32,768]{1,0:T(8,128)S(1)} %book_join.3.refs_1_.refs_0_), channel_id=1, source_target_pairs={{0,8},{8,0},{16,24},{24,16},{1,9},{9,1},{17,25},{25,17},{2,10},{10... | collective-permute-start | bytes 294920 | tf_op jit(solution)/shard_map/ppermute | solution.py:213
  60.7 2.6 %collective-permute-start.17 = (f32[192,768]{1,0:T(8,128)S(1)}, f32[192,768]{1,0:T(8,128)S(1)}, u32[]{:S(2)}, u32[]{:S(2)}) collective-permute-start(f32[192,768]{1,0:T(8,128)S(1)} %bitcast.17), channel_id=1, source_target_pairs={{0,1},{1,0},{2,3},{3,2},{4,5},{5,4},{6,7},{7,6},{8,9},{9,8},{10,11... | collective-permute-start | bytes 1769480 | tf_op jit(solution)/shard_map/ppermute | solution.py:213
  60.9 2.4 %collective-permute-start.18 = (f32[128,768]{1,0:T(8,128)S(1)}, f32[128,768]{1,0:T(8,128)S(1)}, u32[]{:S(2)}, u32[]{:S(2)}) collective-permute-start(f32[128,768]{1,0:T(8,128)S(1)} %bitcast.15), channel_id=1, source_target_pairs={{0,1},{1,0},{2,3},{3,2},{4,5},{5,4},{6,7},{7,6},{8,9},{9,8},{10,11... | collective-permute-start | bytes 1179656 | tf_op jit(solution)/shard_map/ppermute | solution.py:213

commit v5 on v4

--- a/solution.py
+++ b/solution.py
@@ -417,8 +417,8 @@
     )(dg, codes_here, q_keep)
 
     b_cuts = cut(book_keep, [swap(x, "corpus", 1) for x in book_send], "query", 1, query, "book_cut")
-    b_got = [swap(b_cuts[k], "query", k) for k in range(1, query)]
-    b_own = b_sum = add(b_cuts[0], b_got, [], "book_sum")
+    b_got = [swap(b_cuts[k], "query", k) for k in reversed(range(1, query))][::-1]
+    b_own = b_sum = add(b_cuts[0], b_got[::-1], [], "book_sum")
     for step in range(bits - 1):
         q_got = chip_swap(q_send, step)
         if step < bits - 2:

time: 64.6 us -> 64.6 us (level)
    ppermute x14, waiting for transfers between devices: 11 us -> 10.3 us  [swap(): lax.ppermute(x, axis, [(i, i ^ bits) for i in range(lax.axis_size(axis))])]
  transfers between devices with their start and end apart: 19 -> 19, of which waited for: 12 -> 13; matrix products, arithmetic and copies ran while one was open for 0% -> 0% of each run, Pallas kernels for 18% -> 18%
where the time goes in v5:
time: 64.6 us; the launch traced here: 64.5 us
  starting transfers between devices  25.6 us (40%)
  Pallas kernels  20.9 us (32%)
  waiting for transfers between devices  17.1 us (26%)
  between operations  0.94 us (1%)
    ppermute x14, starting transfers between devices, swap(): lax.ppermute(x, axis, [(i, i ^ bits) for i in range(lax.axis_size(axis))])  15.3 us
    ppermute x5, starting transfers between devices, chip_swap(): lax.ppermute(x, 'corpus', [(i, i ^ 2 << bit_at(step, i % 2, count)) for i...  10.3 us
    ppermute x14, waiting for transfers between devices, swap(): lax.ppermute(x, axis, [(i, i ^ bits) for i in range(lax.axis_size(axis))])  10.3 us
    pallas_call x1, Pallas kernels, local(): call(score_kernel, [((rows, width), F32), ((subs, docs), I32), ((rows, do...  7.87 us
    ppermute x5, waiting for transfers between devices, chip_swap(): lax.ppermute(x, 'corpus', [(i, i ^ 2 << bit_at(step, i % 2, count)) for i...  6.8 us
    pallas_call x1, Pallas kernels, local(): call(book_kernel, [((part_rows, width), F32)] + [((part_rows, width // 2)...  3.99 us
    pallas_call x1, Pallas kernels, local(): call(doc_kernel, [((width, docs), F32)], [VMEM] * 4, [pltpu.VMEM((2 * row...  2.46 us
    pallas_call x1, Pallas kernels, local(): call(spread_kernel, [((rows, width), F32)], [VMEM] * 2, (), 6 * work)(e, r)  2.07 us
  transfers between devices with their start and end apart: 19, of which 13 were waited for; matrix products, arithmetic and copies ran while one was open for 0% of the time, Pallas kernels for 18%

profile of v5, /device:TPU:0, one launch (start us, length us, event | category | flops | bytes accessed | tf_op | source)
XLA Modules:
  0.0 64.5 jit_solution(13532022602413567074)
XLA Ops:
  0.6 7.9 %score_kernel.1 = (f32[384,768]{1,0:T(8,128)S(1)}, s32[96,1024]{1,0:T(8,128)S(1)}, f32[384,1024]{1,0:T(8,128)S(1)}, bf16[384,1024]{1,0:T(8,128)(2,1)S(1)}, bf16[...) custom-call(f32[384,768]{1,0:T(8,128)} %q_hbm.1, s32[96,1024]{1,0:T(8,128)} %bitcast.26, f32[256,768]{1,0:T(8,128)} %book_hbm.1, ...), custom_call_target="tpu_custom_call" | custom-call | flops 3623878656 | bytes 131072 | tf_op jit(solution)/shard_map/score_kernel/pallas_call | solution.py:372
  8.5 0.5 collective-permute-start
  9.0 0.4 turn_kernel.1.after_ref.qt_ref
  9.4 0.5 collective-permute-done.b_ref
  9.9 3.0 %collective-permute-start.1 = (f32[8,384]{1,0:T(8,128)S(1)}, f32[8,384]{1,0:T(8,128)S(1)}, u32[]{:S(2)}, u32[]{:S(2)}) collective-permute-start(f32[8,384]{1,0:T(8,128)S(1)} %join_kernel.2.a_ref), channel_id=1, source_target_pairs={{0,2},{1,3},{2,0},{3,1},{4,6},{5,7},{6,4},{7,5},{8,10},{9,11},{10,... | collective-permute-start | bytes 36872 | tf_op jit(solution)/shard_map/ppermute | solution.py:213
  12.9 2.1 %spread_kernel.1.after_ref = f32[384,768]{1,0:T(8,128)S(1)} custom-call(f32[384,1024]{1,0:T(8,128)S(1)} %get-tuple-element.33.e_ref, bf16[1536,1024]{1,0:T(8,128)(2,1)S(1)} %get-tuple-element.34.r_ref), custom_call_target="tpu_custom_call" | custom-call | flops 1811939328 | bytes 131072 | tf_op jit(solution)/shard_map/spread_kernel/pallas_call | solution.py:388
  14.9 0.0 collective-permute-done.1.b_ref
  15.0 2.7 %collective-permute-start.2 = (f32[8,384]{1,0:T(8,128)S(1)}, f32[8,384]{1,0:T(8,128)S(1)}, u32[]{:S(2)}, u32[]{:S(2)}) collective-permute-start(f32[8,384]{1,0:T(8,128)S(1)} %join_kernel.3.after_ref.a_ref), channel_id=1, source_target_pairs={{0,4},{1,5},{2,6},{3,7},{4,0},{5,1},{6,2},{7,3},{8,12},{9,13},{10,... | collective-permute-start | bytes 36872 | tf_op jit(solution)/shard_map/ppermute | solution.py:213
  17.7 1.4 %positive_kernel.1 = f32[384,768]{1,0:T(8,128)S(1)} custom-call(bf16[384,1024]{1,0:T(8,128)(2,1)S(1)} %get-tuple-element.35.hits_ref, bf16[1536,1024]{1,0:T(8,128)(2,1)S(1)} %get-tuple-element.34.r_ref, f32[8,384]{1,0:T(8,128)S(1)} %join_kernel.3.after_ref.a_ref), custom_call_target="tpu_custom_call" | custom-call | flops 1207959552 | bytes 131072 | tf_op jit(solution)/shard_map/positive_kernel/pallas_call | solution.py:396
  19.1 0.6 collective-permute-done.2.b_ref
  19.6 0.4 terms_kernel.1
  20.0 0.1 collective-permute-start.3
  20.1 2.5 %doc_kernel.1.refs_0_.dg_ref = f32[768,1024]{1,0:T(8,128)S(1)} custom-call(f32[384,1024]{1,0:T(8,128)S(1)} %get-tuple-element.33.e_ref, bf16[384,1024]{1,0:T(8,128)(2,1)S(1)} %get-tuple-element.35.hits_ref, f32[1,384]{1,0:T(1,128)S(1)} %get-tuple-element.39.scale_ref, bf16[768,768]{1,0:T(8,128)(2,1)S(1)} %turn_kernel.1.after_ref.qt_ref), custom_call_target="tpu_custom_call" | custom-call | flops 1811939328 | bytes 131072 | tf_op jit(solution)/shard_map/doc_kernel/pallas_call | solution.py:407
  22.6 0.0 collective-permute-done.3
  22.6 0.1 query_halve.1
  22.7 1.7 %collective-permute-start.4 = (f32[96,768]{1,0:T(8,128)S(1)}, f32[96,768]{1,0:T(8,128)S(1)}, u32[]{:S(2)}, u32[]{:S(2)}) collective-permute-start(f32[96,768]{1,0:T(8,128)S(1)} %get-tuple-element.41), channel_id=1, source_target_pairs={{0,2},{1,5},{2,0},{3,7},{4,6},{5,1},{6,4},{7,3},{8,10},{9,13},{10,... | collective-permute-start | bytes 884744 | tf_op jit(solution)/shard_map/ppermute | solution.py:266
  24.3 4.0 %book_kernel.1 = (f32[128,768]{1,0:T(8,128)S(1)}, f32[128,384]{1,0:T(8,128)S(1)}, f32[128,384]{1,0:T(8,128)S(1)}) custom-call(f32[768,1024]{1,0:T(8,128)S(1)} %doc_kernel.1.refs_0_.dg_ref, s32[96,1024]{1,0:T(8,128)S(1)} %get-tuple-element.42.codes_ref, f32[96,768]{1,0:T(8,128)S(1)} %get-tuple-element.40.after_ref.whole_ref), custom_call_target="tpu_custom_call" | custom-call | flops 2415919104 | bytes 131072 | tf_op jit(solution)/shard_map/book_kernel/pallas_call | solution.py:411
  28.3 1.3 %collective-permute-start.5 = (f32[128,384]{1,0:T(8,128)S(1)}, f32[128,384]{1,0:T(8,128)S(1)}, u32[]{:S(2)}, u32[]{:S(2)}) collective-permute-start(f32[128,384]{1,0:T(8,128)S(1)} %get-tuple-element.44), channel_id=1, source_target_pairs={{0,1},{1,0},{2,3},{3,2},{4,5},{5,4},{6,7},{7,6},{8,9},{9,8},{10,11... | collective-permute-start | bytes 589832 | tf_op jit(solution)/shard_map/ppermute | solution.py:213
  29.6 0.1 collective-permute-start.6
  29.7 1.0 %collective-permute-done.5 = f32[128,384]{1,0:T(8,128)S(1)} collective-permute-done((f32[128,384]{1,0:T(8,128)S(1)}, f32[128,384]{1,0:T(8,128)S(1)}, u32[]{:S(2)}, u32[]{:S(2)}) %collective-permute-start.5) | collective-permute-done | bytes 196640 | tf_op jit(solution)/shard_map/ppermute | solution.py:213
  30.7 0.4 collective-permute-done.6
  31.1 2.5 %collective-permute-start.8 = (f32[32,768]{1,0:T(8,128)S(1)}, f32[32,768]{1,0:T(8,128)S(1)}, u32[]{:S(2)}, u32[]{:S(2)}) collective-permute-start(f32[32,768]{1,0:T(8,128)S(1)} %get-tuple-element.49), channel_id=1, source_target_pairs={{0,24},{8,16},{16,8},{24,0},{1,25},{9,17},{17,9},{25,1},{2,26},{10... | collective-permute-start | bytes 294920 | tf_op jit(solution)/shard_map/ppermute | solution.py:213
  33.6 0.5 collective-permute-start.9
  34.1 0.5 collective-permute-start.10
  34.7 0.0 collective-permute-done.4.refs_0_
  34.7 1.7 %collective-permute-start.7 = (f32[96,768]{1,0:T(8,128)S(1)}, f32[96,768]{1,0:T(8,128)S(1)}, u32[]{:S(2)}, u32[]{:S(2)}) collective-permute-start(f32[96,768]{1,0:T(8,128)S(1)} %get-tuple-element.48), channel_id=1, source_target_pairs={{0,4},{1,3},{2,6},{3,1},{4,0},{5,7},{6,2},{7,5},{8,12},{9,11},{10,... | collective-permute-start | bytes 884744 | tf_op jit(solution)/shard_map/ppermute | solution.py:266
  36.4 0.7 %collective-permute-done.8.refs_0_ = f32[32,768]{1,0:T(8,128)S(1)} collective-permute-done((f32[32,768]{1,0:T(8,128)S(1)}, f32[32,768]{1,0:T(8,128)S(1)}, u32[]{:S(2)}, u32[]{:S(2)}) %collective-permute-start.8) | collective-permute-done | bytes 98336 | tf_op jit(solution)/shard_map/ppermute | solution.py:213
  37.2 2.0 %collective-permute-done.9.refs_1_ = f32[32,768]{1,0:T(8,128)S(1)} collective-permute-done((f32[32,768]{1,0:T(8,128)S(1)}, f32[32,768]{1,0:T(8,128)S(1)}, u32[]{:S(2)}, u32[]{:S(2)}) %collective-permute-start.9) | collective-permute-done | bytes 98336 | tf_op jit(solution)/shard_map/ppermute | solution.py:213
  39.2 0.0 collective-permute-done.10.refs_2_
  39.2 1.7 %collective-permute-start.11 = (f32[32,768]{1,0:T(8,128)S(1)}, f32[32,768]{1,0:T(8,128)S(1)}, u32[]{:S(2)}, u32[]{:S(2)}) collective-permute-start(f32[32,768]{1,0:T(8,128)S(1)} %book_sum.1.whole_ref), channel_id=1, source_target_pairs={{0,2},{1,5},{2,0},{3,7},{4,6},{5,1},{6,4},{7,3},{8,10},{9,13},{10,... | collective-permute-start | bytes 294920 | tf_op jit(solution)/shard_map/ppermute | solution.py:266
  40.9 3.5 %collective-permute-done.11.refs_0_ = f32[32,768]{1,0:T(8,128)S(1)} collective-permute-done((f32[32,768]{1,0:T(8,128)S(1)}, f32[32,768]{1,0:T(8,128)S(1)}, u32[]{:S(2)}, u32[]{:S(2)}) %collective-permute-start.11) | collective-permute-done | bytes 98336 | tf_op jit(solution)/shard_map/ppermute | solution.py:266
  44.4 2.6 %collective-permute-start.12 = (f32[32,768]{1,0:T(8,128)S(1)}, f32[32,768]{1,0:T(8,128)S(1)}, u32[]{:S(2)}, u32[]{:S(2)}) collective-permute-start(f32[32,768]{1,0:T(8,128)S(1)} %book_join.2.whole_ref), channel_id=1, source_target_pairs={{0,4},{1,3},{2,6},{3,1},{4,0},{5,7},{6,2},{7,5},{8,12},{9,11},{10,... | collective-permute-start | bytes 294920 | tf_op jit(solution)/shard_map/ppermute | solution.py:266
  47.0 3.1 %collective-permute-done.12.refs_0_ = f32[32,768]{1,0:T(8,128)S(1)} collective-permute-done((f32[32,768]{1,0:T(8,128)S(1)}, f32[32,768]{1,0:T(8,128)S(1)}, u32[]{:S(2)}, u32[]{:S(2)}) %collective-permute-start.12) | collective-permute-done | bytes 98336 | tf_op jit(solution)/shard_map/ppermute | solution.py:266
  50.1 0.0 collective-permute-done.7.refs_0_
  50.2 2.7 %collective-permute-start.13 = (f32[96,768]{1,0:T(8,128)S(1)}, f32[96,768]{1,0:T(8,128)S(1)}, u32[]{:S(2)}, u32[]{:S(2)}) collective-permute-start(f32[96,768]{1,0:T(8,128)S(1)} %get-tuple-element.53), channel_id=1, source_target_pairs={{0,2},{1,5},{2,0},{3,7},{4,6},{5,1},{6,4},{7,3},{8,10},{9,13},{10,... | collective-permute-start | bytes 884744 | tf_op jit(solution)/shard_map/ppermute | solution.py:266
  52.9 2.1 %collective-permute-start.16 = (f32[32,768]{1,0:T(8,128)S(1)}, f32[32,768]{1,0:T(8,128)S(1)}, u32[]{:S(2)}, u32[]{:S(2)}) collective-permute-start(f32[32,768]{1,0:T(8,128)S(1)} %book_join.3.refs_1_.refs_0_), channel_id=1, source_target_pairs={{0,24},{8,16},{16,8},{24,0},{1,25},{9,17},{17,9},{25,1},{2,26},{10... | collective-permute-start | bytes 294920 | tf_op jit(solution)/shard_map/ppermute | solution.py:213
  55.1 0.8 %collective-permute-start.15 = (f32[32,768]{1,0:T(8,128)S(1)}, f32[32,768]{1,0:T(8,128)S(1)}, u32[]{:S(2)}, u32[]{:S(2)}) collective-permute-start(f32[32,768]{1,0:T(8,128)S(1)} %book_join.3.refs_1_.refs_0_), channel_id=1, source_target_pairs={{0,16},{8,24},{16,0},{24,8},{1,17},{9,25},{17,1},{25,9},{2,18},{10... | collective-permute-start | bytes 294920 | tf_op jit(solution)/shard_map/ppermute | solution.py:213
  55.9 0.6 collective-permute-start.14
  56.4 2.7 %collective-permute-done.16.refs_3_ = f32[32,768]{1,0:T(8,128)S(1)} collective-permute-done((f32[32,768]{1,0:T(8,128)S(1)}, f32[32,768]{1,0:T(8,128)S(1)}, u32[]{:S(2)}, u32[]{:S(2)}) %collective-permute-start.16) | collective-permute-done | bytes 98336 | tf_op jit(solution)/shard_map/ppermute | solution.py:213
  59.2 0.9 %collective-permute-done.15.refs_2_ = f32[32,768]{1,0:T(8,128)S(1)} collective-permute-done((f32[32,768]{1,0:T(8,128)S(1)}, f32[32,768]{1,0:T(8,128)S(1)}, u32[]{:S(2)}, u32[]{:S(2)}) %collective-permute-start.15) | collective-permute-done | bytes 98336 | tf_op jit(solution)/shard_map/ppermute | solution.py:213
  60.1 0.4 collective-permute-done.14.refs_1_
  60.5 0.1 collective-permute-done.13.refs_0_
  60.7 0.1 query_put.1
  60.7 0.2 collective-permute-start.17
  60.9 0.4 collective-permute-start.18
  61.3 1.0 %finish_own.1 = (f32[384]{0:T(512)}, f32[2,192,768]{2,1,0:T(8,128)}, f32[2,128,768]{2,1,0:T(8,128)}) custom-call(f32[1,384]{1,0:T(1,128)S(1)} %get-tuple-element.36.refs_0_, f32[192,768]{1,0:T(8,128)S(1)} %bitcast.18, f32[128,768]{1,0:T(8,128)S(1)} %bitcast.16), custom_call_target="tpu_custom_call" | custom-call | tf_op jit(solution)/shard_map/finish_own/pallas_call | solution.py:351
  62.3 1.1 %collective-permute-done.18.refs_3_ = f32[128,768]{1,0:T(8,128)S(1)} collective-permute-done((f32[128,768]{1,0:T(8,128)S(1)}, f32[128,768]{1,0:T(8,128)S(1)}, u32[]{:S(2)}, u32[]{:S(2)}) %collective-permute-start.18) | collective-permute-done | bytes 393248 | tf_op jit(solution)/shard_map/ppermute | solution.py:213
  63.4 0.0 collective-permute-done.17.refs_2_
  63.4 1.0 %finish_got.1 = (f32[2,192,768]{2,1,0:T(8,128)}, f32[2,128,768]{2,1,0:T(8,128)}) custom-call(f32[2,192,768]{2,1,0:T(8,128)} %get-tuple-element.54.refs_0_, f32[2,128,768]{2,1,0:T(8,128)} %get-tuple-element.55.refs_1_, f32[192,768]{1,0:T(8,128)S(1)} %collective-permute-done.17.refs_2_, ...), custom_call_target="tpu_custom_call", output_to_operand_aliasing={{0}: (0, {}), {1}: (1, {})} | custom-call | tf_op jit(solution)/shard_map/finish_got/pallas_call | solution.py:356
  (9 shorter events, 0.2 us)
Async XLA Ops:
  8.5 1.4 %collective-permute-start = (f32[8,384]{1,0:T(8,128)S(1)}, f32[8,384]{1,0:T(8,128)S(1)}, u32[]{:S(2)}, u32[]{:S(2)}) collective-permute-start(f32[8,384]{1,0:T(8,128)S(1)} %get-tuple-element.31.a_ref.first_ref), channel_id=1, source_target_pairs={{0,1},{1,0},{2,3},{3,2},{4,5},{5,4},{6,7},{7,6},{8,9},{9,8},{10,11... | collective-permute-start | bytes 36872 | tf_op jit(solution)/shard_map/ppermute | solution.py:213
  9.9 5.1 %collective-permute-start.1 = (f32[8,384]{1,0:T(8,128)S(1)}, f32[8,384]{1,0:T(8,128)S(1)}, u32[]{:S(2)}, u32[]{:S(2)}) collective-permute-start(f32[8,384]{1,0:T(8,128)S(1)} %join_kernel.2.a_ref), channel_id=1, source_target_pairs={{0,2},{1,3},{2,0},{3,1},{4,6},{5,7},{6,4},{7,5},{8,10},{9,11},{10,... | collective-permute-start | bytes 36872 | tf_op jit(solution)/shard_map/ppermute | solution.py:213
  15.0 4.7 %collective-permute-start.2 = (f32[8,384]{1,0:T(8,128)S(1)}, f32[8,384]{1,0:T(8,128)S(1)}, u32[]{:S(2)}, u32[]{:S(2)}) collective-permute-start(f32[8,384]{1,0:T(8,128)S(1)} %join_kernel.3.after_ref.a_ref), channel_id=1, source_target_pairs={{0,4},{1,5},{2,6},{3,7},{4,0},{5,1},{6,2},{7,3},{8,12},{9,13},{10,... | collective-permute-start | bytes 36872 | tf_op jit(solution)/shard_map/ppermute | solution.py:213
  20.0 2.6 %collective-permute-start.3 = (f32[192,768]{1,0:T(8,128)S(1)}, f32[192,768]{1,0:T(8,128)S(1)}, u32[]{:S(2)}, u32[]{:S(2)}) collective-permute-start(f32[192,768]{1,0:T(8,128)S(1)} %get-tuple-element.38), channel_id=1, source_target_pairs={{0,1},{1,0},{2,3},{3,2},{4,5},{5,4},{6,7},{7,6},{8,9},{9,8},{10,11... | collective-permute-start | bytes 1769480 | tf_op jit(solution)/shard_map/ppermute | solution.py:213
  22.7 12.0 %collective-permute-start.4 = (f32[96,768]{1,0:T(8,128)S(1)}, f32[96,768]{1,0:T(8,128)S(1)}, u32[]{:S(2)}, u32[]{:S(2)}) collective-permute-start(f32[96,768]{1,0:T(8,128)S(1)} %get-tuple-element.41), channel_id=1, source_target_pairs={{0,2},{1,5},{2,0},{3,7},{4,6},{5,1},{6,4},{7,3},{8,10},{9,13},{10,... | collective-permute-start | bytes 884744 | tf_op jit(solution)/shard_map/ppermute | solution.py:266
  28.3 2.4 %collective-permute-start.5 = (f32[128,384]{1,0:T(8,128)S(1)}, f32[128,384]{1,0:T(8,128)S(1)}, u32[]{:S(2)}, u32[]{:S(2)}) collective-permute-start(f32[128,384]{1,0:T(8,128)S(1)} %get-tuple-element.44), channel_id=1, source_target_pairs={{0,1},{1,0},{2,3},{3,2},{4,5},{5,4},{6,7},{7,6},{8,9},{9,8},{10,11... | collective-permute-start | bytes 589832 | tf_op jit(solution)/shard_map/ppermute | solution.py:213
  29.6 1.4 %collective-permute-start.6 = (f32[128,384]{1,0:T(8,128)S(1)}, f32[128,384]{1,0:T(8,128)S(1)}, u32[]{:S(2)}, u32[]{:S(2)}) collective-permute-start(f32[128,384]{1,0:T(8,128)S(1)} %get-tuple-element.45), channel_id=1, source_target_pairs={{0,1},{1,0},{2,3},{3,2},{4,5},{5,4},{6,7},{7,6},{8,9},{9,8},{10,11... | collective-permute-start | bytes 589832 | tf_op jit(solution)/shard_map/ppermute | solution.py:213
  31.1 6.0 %collective-permute-start.8 = (f32[32,768]{1,0:T(8,128)S(1)}, f32[32,768]{1,0:T(8,128)S(1)}, u32[]{:S(2)}, u32[]{:S(2)}) collective-permute-start(f32[32,768]{1,0:T(8,128)S(1)} %get-tuple-element.49), channel_id=1, source_target_pairs={{0,24},{8,16},{16,8},{24,0},{1,25},{9,17},{17,9},{25,1},{2,26},{10... | collective-permute-start | bytes 294920 | tf_op jit(solution)/shard_map/ppermute | solution.py:213
  33.6 5.6 %collective-permute-start.9 = (f32[32,768]{1,0:T(8,128)S(1)}, f32[32,768]{1,0:T(8,128)S(1)}, u32[]{:S(2)}, u32[]{:S(2)}) collective-permute-start(f32[32,768]{1,0:T(8,128)S(1)} %get-tuple-element.50), channel_id=1, source_target_pairs={{0,16},{8,24},{16,0},{24,8},{1,17},{9,25},{17,1},{25,9},{2,18},{10... | collective-permute-start | bytes 294920 | tf_op jit(solution)/shard_map/ppermute | solution.py:213
  34.1 5.1 %collective-permute-start.10 = (f32[32,768]{1,0:T(8,128)S(1)}, f32[32,768]{1,0:T(8,128)S(1)}, u32[]{:S(2)}, u32[]{:S(2)}) collective-permute-start(f32[32,768]{1,0:T(8,128)S(1)} %get-tuple-element.51), channel_id=1, source_target_pairs={{0,8},{8,0},{16,24},{24,16},{1,9},{9,1},{17,25},{25,17},{2,10},{10... | collective-permute-start | bytes 294920 | tf_op jit(solution)/shard_map/ppermute | solution.py:213
  34.7 15.4 %collective-permute-start.7 = (f32[96,768]{1,0:T(8,128)S(1)}, f32[96,768]{1,0:T(8,128)S(1)}, u32[]{:S(2)}, u32[]{:S(2)}) collective-permute-start(f32[96,768]{1,0:T(8,128)S(1)} %get-tuple-element.48), channel_id=1, source_target_pairs={{0,4},{1,3},{2,6},{3,1},{4,0},{5,7},{6,2},{7,5},{8,12},{9,11},{10,... | collective-permute-start | bytes 884744 | tf_op jit(solution)/shard_map/ppermute | solution.py:266
  39.2 5.2 %collective-permute-start.11 = (f32[32,768]{1,0:T(8,128)S(1)}, f32[32,768]{1,0:T(8,128)S(1)}, u32[]{:S(2)}, u32[]{:S(2)}) collective-permute-start(f32[32,768]{1,0:T(8,128)S(1)} %book_sum.1.whole_ref), channel_id=1, source_target_pairs={{0,2},{1,5},{2,0},{3,7},{4,6},{5,1},{6,4},{7,3},{8,10},{9,13},{10,... | collective-permute-start | bytes 294920 | tf_op jit(solution)/shard_map/ppermute | solution.py:266
  44.4 5.7 %collective-permute-start.12 = (f32[32,768]{1,0:T(8,128)S(1)}, f32[32,768]{1,0:T(8,128)S(1)}, u32[]{:S(2)}, u32[]{:S(2)}) collective-permute-start(f32[32,768]{1,0:T(8,128)S(1)} %book_join.2.whole_ref), channel_id=1, source_target_pairs={{0,4},{1,3},{2,6},{3,1},{4,0},{5,7},{6,2},{7,5},{8,12},{9,11},{10,... | collective-permute-start | bytes 294920 | tf_op jit(solution)/shard_map/ppermute | solution.py:266
  50.2 10.4 %collective-permute-start.13 = (f32[96,768]{1,0:T(8,128)S(1)}, f32[96,768]{1,0:T(8,128)S(1)}, u32[]{:S(2)}, u32[]{:S(2)}) collective-permute-start(f32[96,768]{1,0:T(8,128)S(1)} %get-tuple-element.53), channel_id=1, source_target_pairs={{0,2},{1,5},{2,0},{3,7},{4,6},{5,1},{6,4},{7,3},{8,10},{9,13},{10,... | collective-permute-start | bytes 884744 | tf_op jit(solution)/shard_map/ppermute | solution.py:266
  52.9 6.2 %collective-permute-start.16 = (f32[32,768]{1,0:T(8,128)S(1)}, f32[32,768]{1,0:T(8,128)S(1)}, u32[]{:S(2)}, u32[]{:S(2)}) collective-permute-start(f32[32,768]{1,0:T(8,128)S(1)} %book_join.3.refs_1_.refs_0_), channel_id=1, source_target_pairs={{0,24},{8,16},{16,8},{24,0},{1,25},{9,17},{17,9},{25,1},{2,26},{10... | collective-permute-start | bytes 294920 | tf_op jit(solution)/shard_map/ppermute | solution.py:213
  55.1 5.0 %collective-permute-start.15 = (f32[32,768]{1,0:T(8,128)S(1)}, f32[32,768]{1,0:T(8,128)S(1)}, u32[]{:S(2)}, u32[]{:S(2)}) collective-permute-start(f32[32,768]{1,0:T(8,128)S(1)} %book_join.3.refs_1_.refs_0_), channel_id=1, source_target_pairs={{0,16},{8,24},{16,0},{24,8},{1,17},{9,25},{17,1},{25,9},{2,18},{10... | collective-permute-start | bytes 294920 | tf_op jit(solution)/shard_map/ppermute | solution.py:213
  55.9 4.6 %collective-permute-start.14 = (f32[32,768]{1,0:T(8,128)S(1)}, f32[32,768]{1,0:T(8,128)S(1)}, u32[]{:S(2)}, u32[]{:S(2)}) collective-permute-start(f32[32,768]{1,0:T(8,128)S(1)} %book_join.3.refs_1_.refs_0_), channel_id=1, source_target_pairs={{0,8},{8,0},{16,24},{24,16},{1,9},{9,1},{17,25},{25,17},{2,10},{10... | collective-permute-start | bytes 294920 | tf_op jit(solution)/shard_map/ppermute | solution.py:213
  60.7 2.6 %collective-permute-start.17 = (f32[192,768]{1,0:T(8,128)S(1)}, f32[192,768]{1,0:T(8,128)S(1)}, u32[]{:S(2)}, u32[]{:S(2)}) collective-permute-start(f32[192,768]{1,0:T(8,128)S(1)} %bitcast.17), channel_id=1, source_target_pairs={{0,1},{1,0},{2,3},{3,2},{4,5},{5,4},{6,7},{7,6},{8,9},{9,8},{10,11... | collective-permute-start | bytes 1769480 | tf_op jit(solution)/shard_map/ppermute | solution.py:213
  60.9 2.4 %collective-permute-start.18 = (f32[128,768]{1,0:T(8,128)S(1)}, f32[128,768]{1,0:T(8,128)S(1)}, u32[]{:S(2)}, u32[]{:S(2)}) collective-permute-start(f32[128,768]{1,0:T(8,128)S(1)} %bitcast.15), channel_id=1, source_target_pairs={{0,1},{1,0},{2,3},{3,2},{4,5},{5,4},{6,7},{7,6},{8,9},{9,8},{10,11... | collective-permute-start | bytes 1179656 | tf_op jit(solution)/shard_map/ppermute | solution.py:213

commit v6 on v4

--- a/solution.py
+++ b/solution.py
@@ -109,17 +109,20 @@
     stats_ref[...] = packed.T[0:8, :]
 
 
-def spread_kernel(e_ref, r_ref, u_ref):
-    width = u_ref.shape[1]
-    eh, em = split2(e_ref[...])
-    rh, rm = r_ref[0:width, :], r_ref[width:, :]
-    u_ref[...] = (dot_nt(em, rh) + dot_nt(eh, rm)) + dot_nt(eh, rh)
-
-
-def positive_kernel(hits_ref, r_ref, after_ref, p_ref):
-    width = p_ref.shape[1]
-    hits = hits_ref[...]
-    p_ref[...] = dot_nt(hits, r_ref[width:, :]) + dot_nt(hits, r_ref[0:width, :])
+def spread_kernel(e_ref, hits_ref, r_ref, u_ref, p_ref):
+    rows, width = u_ref.shape
+    low = split2(e_ref[...])[1]
+    both = dot_nt(jnp.concatenate([low, hits_ref[...]], axis=0), r_ref[0:width, :])
+    u_ref[...] = both[0:rows]
+    p_ref[...] = both[rows:]
+
+
+def positive_kernel(e_ref, hits_ref, r_ref, u_part_ref, p_part_ref, after_ref, u_ref, p_ref):
+    rows, width = p_ref.shape
+    high = e_ref[...].astype(BF16)
+    both = dot_nt(jnp.concatenate([high, hits_ref[...]], axis=0), r_ref[width:, :])
+    u_ref[...] = (u_part_ref[...] + both[0:rows]) + dot_nt(high, r_ref[0:width, :])
+    p_ref[...] = p_part_ref[...] + both[rows:]
 
 
 def turn_kernel(q_ref, qt_ref):
@@ -385,7 +388,7 @@
         12 * work,
         24,
     )(*[pltpu.with_memory_space_constraint(x, pltpu.HBM) for x in (queries, codes_t, codebook, positive)])
-    u = call(spread_kernel, [((rows, width), F32)], [VMEM] * 2, (), 6 * work)(e, r)[0]
+    u, p = call(spread_kernel, [((rows, width), F32)] * 2, [VMEM] * 3, (), 4 * work)(e, hits, r)
     qt = call(turn_kernel, [((width, 2 * rows), BF16)], [VMEM], (), work)(q)[0]
     joined, got, bits, after = stats, swap(stats, "corpus", 1), 2, qt
     while bits < corpus:
@@ -393,7 +396,7 @@
         got = swap(joined, "corpus", bits)
         after = u
         bits *= 2
-    p = call(positive_kernel, [((rows, width), F32)], [VMEM] * 3, (), 4 * work)(hits, r, joined)[0]
+    u, p = call(positive_kernel, [((rows, width), F32)] * 2, [VMEM] * 6, (), 6 * work)(e, hits, r, u, p, joined)
     half = rows // 2
     keep, send, loss, scale = call(
         terms_kernel,

time: 64.6 us -> 64.6 us (level)
  no operation moved by 1% of the time
where the time goes in v6:
time: 64.6 us; the launch traced here: 64.5 us
  starting transfers between devices  25.8 us (40%)
  Pallas kernels  20.9 us (32%)
  waiting for transfers between devices  16.8 us (26%)
  between operations  0.94 us (1%)
    ppermute x14, starting transfers between devices, swap(): lax.ppermute(x, axis, [(i, i ^ bits) for i in range(lax.axis_size(axis))])  15.6 us
    ppermute x14, waiting for transfers between devices, swap(): lax.ppermute(x, axis, [(i, i ^ bits) for i in range(lax.axis_size(axis))])  10.7 us
    ppermute x5, starting transfers between devices, chip_swap(): lax.ppermute(x, 'corpus', [(i, i ^ 2 << bit_at(step, i % 2, count)) for i...  10.2 us
    pallas_call x1, Pallas kernels, local(): call(score_kernel, [((rows, width), F32), ((subs, docs), I32), ((rows, do...  7.86 us
    ppermute x5, waiting for transfers between devices, chip_swap(): lax.ppermute(x, 'corpus', [(i, i ^ 2 << bit_at(step, i % 2, count)) for i...  6.18 us
    pallas_call x1, Pallas kernels, local(): call(book_kernel, [((part_rows, width), F32)] + [((part_rows, width // 2)...  4.01 us
    pallas_call x1, Pallas kernels, local(): call(doc_kernel, [((width, docs), F32)], [VMEM] * 4, [pltpu.VMEM((2 * row...  2.43 us
    pallas_call x1, Pallas kernels, local(): call(positive_kernel, [((rows, width), F32)] * 2, [VMEM] * 6, (), 6 * work)  2.04 us
  transfers between devices with their start and end apart: 19, of which 12 were waited for; matrix products, arithmetic and copies ran while one was open for 0% of the time, Pallas kernels for 18%

profile of v6, /device:TPU:0, one launch (start us, length us, event | category | flops | bytes accessed | tf_op | source)
XLA Modules:
  0.0 64.5 jit_solution(14758795197189081277)
XLA Ops:
  0.6 7.9 %score_kernel.1 = (f32[384,768]{1,0:T(8,128)S(1)}, s32[96,1024]{1,0:T(8,128)S(1)}, f32[384,1024]{1,0:T(8,128)S(1)}, bf16[384,1024]{1,0:T(8,128)(2,1)S(1)}, bf16[...) custom-call(f32[384,768]{1,0:T(8,128)} %q_hbm.1, s32[96,1024]{1,0:T(8,128)} %bitcast.26, f32[256,768]{1,0:T(8,128)} %book_hbm.1, ...), custom_call_target="tpu_custom_call" | custom-call | flops 3623878656 | bytes 131072 | tf_op jit(solution)/shard_map/score_kernel/pallas_call | solution.py:375
  8.5 0.5 collective-permute-start
  9.0 0.4 turn_kernel.1.after_ref.qt_ref
  9.4 0.5 collective-permute-done.b_ref
  9.9 3.0 %collective-permute-start.1 = (f32[8,384]{1,0:T(8,128)S(1)}, f32[8,384]{1,0:T(8,128)S(1)}, u32[]{:S(2)}, u32[]{:S(2)}) collective-permute-start(f32[8,384]{1,0:T(8,128)S(1)} %join_kernel.2.a_ref), channel_id=1, source_target_pairs={{0,2},{1,3},{2,0},{3,1},{4,6},{5,7},{6,4},{7,5},{8,10},{9,11},{10,... | collective-permute-start | bytes 36872 | tf_op jit(solution)/shard_map/ppermute | solution.py:216
  12.9 1.4 %spread_kernel.1 = (f32[384,768]{1,0:T(8,128)S(1)}, f32[384,768]{1,0:T(8,128)S(1)}) custom-call(f32[384,1024]{1,0:T(8,128)S(1)} %get-tuple-element.37.e_ref, bf16[384,1024]{1,0:T(8,128)(2,1)S(1)} %get-tuple-element.38.hits_ref, bf16[1536,1024]{1,0:T(8,128)(2,1)S(1)} %get-tuple-element.39.r_ref), custom_call_target="tpu_custom_call" | custom-call | flops 1207959552 | bytes 131072 | tf_op jit(solution)/shard_map/spread_kernel/pallas_call | solution.py:391
  14.3 0.2 collective-permute-done.1.b_ref
  14.6 3.1 %collective-permute-start.2 = (f32[8,384]{1,0:T(8,128)S(1)}, f32[8,384]{1,0:T(8,128)S(1)}, u32[]{:S(2)}, u32[]{:S(2)}) collective-permute-start(f32[8,384]{1,0:T(8,128)S(1)} %join_kernel.3.after_ref.a_ref), channel_id=1, source_target_pairs={{0,4},{1,5},{2,6},{3,7},{4,0},{5,1},{6,2},{7,3},{8,12},{9,13},{10,... | collective-permute-start | bytes 36872 | tf_op jit(solution)/shard_map/ppermute | solution.py:216
  17.6 2.0 %positive_kernel.1 = (f32[384,768]{1,0:T(8,128)S(1)}, f32[384,768]{1,0:T(8,128)S(1)}) custom-call(f32[384,1024]{1,0:T(8,128)S(1)} %get-tuple-element.37.e_ref, bf16[384,1024]{1,0:T(8,128)(2,1)S(1)} %get-tuple-element.38.hits_ref, bf16[1536,1024]{1,0:T(8,128)(2,1)S(1)} %get-tuple-element.39.r_ref, f32[384,768]{1,0:T(8,128)S(1)} %get-tuple-element.40.after_ref.u_part_ref, ...), custom_call_target="tpu_custom_call" | custom-call | flops 1811939328 | bytes 131072 | tf_op jit(solution)/shard_map/positive_kernel/pallas_call | solution.py:399
  19.7 0.0 collective-permute-done.2.b_ref
  19.7 0.4 terms_kernel.1
  20.1 0.1 collective-permute-start.3
  20.2 2.4 %doc_kernel.1.refs_0_.dg_ref = f32[768,1024]{1,0:T(8,128)S(1)} custom-call(f32[384,1024]{1,0:T(8,128)S(1)} %get-tuple-element.37.e_ref, bf16[384,1024]{1,0:T(8,128)(2,1)S(1)} %get-tuple-element.38.hits_ref, f32[1,384]{1,0:T(1,128)S(1)} %get-tuple-element.47.scale_ref, bf16[768,768]{1,0:T(8,128)(2,1)S(1)} %turn_kernel.1.after_ref.qt_ref), custom_call_target="tpu_custom_call" | custom-call | flops 1811939328 | bytes 131072 | tf_op jit(solution)/shard_map/doc_kernel/pallas_call | solution.py:410
  22.6 0.0 collective-permute-done.3
  22.6 0.1 query_halve.1
  22.7 1.6 %collective-permute-start.4 = (f32[96,768]{1,0:T(8,128)S(1)}, f32[96,768]{1,0:T(8,128)S(1)}, u32[]{:S(2)}, u32[]{:S(2)}) collective-permute-start(f32[96,768]{1,0:T(8,128)S(1)} %get-tuple-element.49), channel_id=1, source_target_pairs={{0,2},{1,5},{2,0},{3,7},{4,6},{5,1},{6,4},{7,3},{8,10},{9,13},{10,... | collective-permute-start | bytes 884744 | tf_op jit(solution)/shard_map/ppermute | solution.py:269
  24.4 4.0 %book_kernel.1 = (f32[128,768]{1,0:T(8,128)S(1)}, f32[128,384]{1,0:T(8,128)S(1)}, f32[128,384]{1,0:T(8,128)S(1)}) custom-call(f32[768,1024]{1,0:T(8,128)S(1)} %doc_kernel.1.refs_0_.dg_ref, s32[96,1024]{1,0:T(8,128)S(1)} %get-tuple-element.50.codes_ref, f32[96,768]{1,0:T(8,128)S(1)} %get-tuple-element.48.after_ref.whole_ref), custom_call_target="tpu_custom_call" | custom-call | flops 2415919104 | bytes 131072 | tf_op jit(solution)/shard_map/book_kernel/pallas_call | solution.py:414
  28.4 1.2 %collective-permute-start.5 = (f32[128,384]{1,0:T(8,128)S(1)}, f32[128,384]{1,0:T(8,128)S(1)}, u32[]{:S(2)}, u32[]{:S(2)}) collective-permute-start(f32[128,384]{1,0:T(8,128)S(1)} %get-tuple-element.52), channel_id=1, source_target_pairs={{0,1},{1,0},{2,3},{3,2},{4,5},{5,4},{6,7},{7,6},{8,9},{9,8},{10,11... | collective-permute-start | bytes 589832 | tf_op jit(solution)/shard_map/ppermute | solution.py:216
  29.6 0.1 collective-permute-start.6
  29.7 1.0 %collective-permute-done.5 = f32[128,384]{1,0:T(8,128)S(1)} collective-permute-done((f32[128,384]{1,0:T(8,128)S(1)}, f32[128,384]{1,0:T(8,128)S(1)}, u32[]{:S(2)}, u32[]{:S(2)}) %collective-permute-start.5) | collective-permute-done | bytes 196640 | tf_op jit(solution)/shard_map/ppermute | solution.py:216
  30.7 0.4 collective-permute-done.6
  31.1 1.6 %collective-permute-start.8 = (f32[32,768]{1,0:T(8,128)S(1)}, f32[32,768]{1,0:T(8,128)S(1)}, u32[]{:S(2)}, u32[]{:S(2)}) collective-permute-start(f32[32,768]{1,0:T(8,128)S(1)} %get-tuple-element.57), channel_id=1, source_target_pairs={{0,8},{8,0},{16,24},{24,16},{1,9},{9,1},{17,25},{25,17},{2,10},{10... | collective-permute-start | bytes 294920 | tf_op jit(solution)/shard_map/ppermute | solution.py:216
  32.7 1.5 %collective-permute-start.9 = (f32[32,768]{1,0:T(8,128)S(1)}, f32[32,768]{1,0:T(8,128)S(1)}, u32[]{:S(2)}, u32[]{:S(2)}) collective-permute-start(f32[32,768]{1,0:T(8,128)S(1)} %get-tuple-element.58), channel_id=1, source_target_pairs={{0,16},{8,24},{16,0},{24,8},{1,17},{9,25},{17,1},{25,9},{2,18},{10... | collective-permute-start | bytes 294920 | tf_op jit(solution)/shard_map/ppermute | solution.py:216
  34.2 0.5 collective-permute-start.10
  34.7 0.0 collective-permute-done.4.refs_0_
  34.7 1.7 %collective-permute-start.7 = (f32[96,768]{1,0:T(8,128)S(1)}, f32[96,768]{1,0:T(8,128)S(1)}, u32[]{:S(2)}, u32[]{:S(2)}) collective-permute-start(f32[96,768]{1,0:T(8,128)S(1)} %get-tuple-element.56), channel_id=1, source_target_pairs={{0,4},{1,3},{2,6},{3,1},{4,0},{5,7},{6,2},{7,5},{8,12},{9,11},{10,... | collective-permute-start | bytes 884744 | tf_op jit(solution)/shard_map/ppermute | solution.py:269
  36.4 0.0 collective-permute-done.8.refs_0_
  36.4 2.1 %collective-permute-done.9.refs_1_ = f32[32,768]{1,0:T(8,128)S(1)} collective-permute-done((f32[32,768]{1,0:T(8,128)S(1)}, f32[32,768]{1,0:T(8,128)S(1)}, u32[]{:S(2)}, u32[]{:S(2)}) %collective-permute-start.9) | collective-permute-done | bytes 98336 | tf_op jit(solution)/shard_map/ppermute | solution.py:216
  38.5 1.2 %collective-permute-done.10.refs_2_ = f32[32,768]{1,0:T(8,128)S(1)} collective-permute-done((f32[32,768]{1,0:T(8,128)S(1)}, f32[32,768]{1,0:T(8,128)S(1)}, u32[]{:S(2)}, u32[]{:S(2)}) %collective-permute-start.10) | collective-permute-done | bytes 98336 | tf_op jit(solution)/shard_map/ppermute | solution.py:216
  39.7 1.7 %collective-permute-start.11 = (f32[32,768]{1,0:T(8,128)S(1)}, f32[32,768]{1,0:T(8,128)S(1)}, u32[]{:S(2)}, u32[]{:S(2)}) collective-permute-start(f32[32,768]{1,0:T(8,128)S(1)} %book_sum.1.whole_ref), channel_id=1, source_target_pairs={{0,2},{1,5},{2,0},{3,7},{4,6},{5,1},{6,4},{7,3},{8,10},{9,13},{10,... | collective-permute-start | bytes 294920 | tf_op jit(solution)/shard_map/ppermute | solution.py:269
  41.4 3.0 %collective-permute-done.11.refs_0_ = f32[32,768]{1,0:T(8,128)S(1)} collective-permute-done((f32[32,768]{1,0:T(8,128)S(1)}, f32[32,768]{1,0:T(8,128)S(1)}, u32[]{:S(2)}, u32[]{:S(2)}) %collective-permute-start.11) | collective-permute-done | bytes 98336 | tf_op jit(solution)/shard_map/ppermute | solution.py:269
  44.4 2.5 %collective-permute-start.12 = (f32[32,768]{1,0:T(8,128)S(1)}, f32[32,768]{1,0:T(8,128)S(1)}, u32[]{:S(2)}, u32[]{:S(2)}) collective-permute-start(f32[32,768]{1,0:T(8,128)S(1)} %book_join.2.whole_ref), channel_id=1, source_target_pairs={{0,4},{1,3},{2,6},{3,1},{4,0},{5,7},{6,2},{7,5},{8,12},{9,11},{10,... | collective-permute-start | bytes 294920 | tf_op jit(solution)/shard_map/ppermute | solution.py:269
  47.0 3.1 %collective-permute-done.12.refs_0_ = f32[32,768]{1,0:T(8,128)S(1)} collective-permute-done((f32[32,768]{1,0:T(8,128)S(1)}, f32[32,768]{1,0:T(8,128)S(1)}, u32[]{:S(2)}, u32[]{:S(2)}) %collective-permute-start.12) | collective-permute-done | bytes 98336 | tf_op jit(solution)/shard_map/ppermute | solution.py:269
  50.1 0.0 collective-permute-done.7.refs_0_
  50.2 2.6 %collective-permute-start.13 = (f32[96,768]{1,0:T(8,128)S(1)}, f32[96,768]{1,0:T(8,128)S(1)}, u32[]{:S(2)}, u32[]{:S(2)}) collective-permute-start(f32[96,768]{1,0:T(8,128)S(1)} %get-tuple-element.61), channel_id=1, source_target_pairs={{0,2},{1,5},{2,0},{3,7},{4,6},{5,1},{6,4},{7,3},{8,10},{9,13},{10,... | collective-permute-start | bytes 884744 | tf_op jit(solution)/shard_map/ppermute | solution.py:269
  52.8 2.2 %collective-permute-start.16 = (f32[32,768]{1,0:T(8,128)S(1)}, f32[32,768]{1,0:T(8,128)S(1)}, u32[]{:S(2)}, u32[]{:S(2)}) collective-permute-start(f32[32,768]{1,0:T(8,128)S(1)} %book_join.3.refs_1_.refs_0_), channel_id=1, source_target_pairs={{0,24},{8,16},{16,8},{24,0},{1,25},{9,17},{17,9},{25,1},{2,26},{10... | collective-permute-start | bytes 294920 | tf_op jit(solution)/shard_map/ppermute | solution.py:216
  55.1 0.9 %collective-permute-start.15 = (f32[32,768]{1,0:T(8,128)S(1)}, f32[32,768]{1,0:T(8,128)S(1)}, u32[]{:S(2)}, u32[]{:S(2)}) collective-permute-start(f32[32,768]{1,0:T(8,128)S(1)} %book_join.3.refs_1_.refs_0_), channel_id=1, source_target_pairs={{0,16},{8,24},{16,0},{24,8},{1,17},{9,25},{17,1},{25,9},{2,18},{10... | collective-permute-start | bytes 294920 | tf_op jit(solution)/shard_map/ppermute | solution.py:216
  56.0 0.4 collective-permute-start.14
  56.3 2.9 %collective-permute-done.16.refs_3_ = f32[32,768]{1,0:T(8,128)S(1)} collective-permute-done((f32[32,768]{1,0:T(8,128)S(1)}, f32[32,768]{1,0:T(8,128)S(1)}, u32[]{:S(2)}, u32[]{:S(2)}) %collective-permute-start.16) | collective-permute-done | bytes 98336 | tf_op jit(solution)/shard_map/ppermute | solution.py:216
  59.2 0.8 %collective-permute-done.15.refs_2_ = f32[32,768]{1,0:T(8,128)S(1)} collective-permute-done((f32[32,768]{1,0:T(8,128)S(1)}, f32[32,768]{1,0:T(8,128)S(1)}, u32[]{:S(2)}, u32[]{:S(2)}) %collective-permute-start.15) | collective-permute-done | bytes 98336 | tf_op jit(solution)/shard_map/ppermute | solution.py:216
  60.1 0.5 collective-permute-done.14.refs_1_
  60.6 0.0 collective-permute-done.13.refs_0_
  60.6 0.1 query_put.1
  60.7 0.2 collective-permute-start.17
  60.9 0.4 collective-permute-start.18
  61.3 1.0 %finish_own.1 = (f32[384]{0:T(512)}, f32[2,192,768]{2,1,0:T(8,128)}, f32[2,128,768]{2,1,0:T(8,128)}) custom-call(f32[1,384]{1,0:T(1,128)S(1)} %get-tuple-element.44.refs_0_, f32[192,768]{1,0:T(8,128)S(1)} %bitcast.16, f32[128,768]{1,0:T(8,128)S(1)} %bitcast.14), custom_call_target="tpu_custom_call" | custom-call | tf_op jit(solution)/shard_map/finish_own/pallas_call | solution.py:354
  62.3 1.1 %collective-permute-done.18.refs_3_ = f32[128,768]{1,0:T(8,128)S(1)} collective-permute-done((f32[128,768]{1,0:T(8,128)S(1)}, f32[128,768]{1,0:T(8,128)S(1)}, u32[]{:S(2)}, u32[]{:S(2)}) %collective-permute-start.18) | collective-permute-done | bytes 393248 | tf_op jit(solution)/shard_map/ppermute | solution.py:216
  63.3 0.0 collective-permute-done.17.refs_2_
  63.3 1.0 %finish_got.1 = (f32[2,192,768]{2,1,0:T(8,128)}, f32[2,128,768]{2,1,0:T(8,128)}) custom-call(f32[2,192,768]{2,1,0:T(8,128)} %get-tuple-element.62.refs_0_, f32[2,128,768]{2,1,0:T(8,128)} %get-tuple-element.63.refs_1_, f32[192,768]{1,0:T(8,128)S(1)} %collective-permute-done.17.refs_2_, ...), custom_call_target="tpu_custom_call", output_to_operand_aliasing={{0}: (0, {}), {1}: (1, {})} | custom-call | tf_op jit(solution)/shard_map/finish_got/pallas_call | solution.py:359
  (9 shorter events, 0.2 us)
Async XLA Ops:
  8.5 1.4 %collective-permute-start = (f32[8,384]{1,0:T(8,128)S(1)}, f32[8,384]{1,0:T(8,128)S(1)}, u32[]{:S(2)}, u32[]{:S(2)}) collective-permute-start(f32[8,384]{1,0:T(8,128)S(1)} %get-tuple-element.35.a_ref.first_ref), channel_id=1, source_target_pairs={{0,1},{1,0},{2,3},{3,2},{4,5},{5,4},{6,7},{7,6},{8,9},{9,8},{10,11... | collective-permute-start | bytes 36872 | tf_op jit(solution)/shard_map/ppermute | solution.py:216
  9.9 4.7 %collective-permute-start.1 = (f32[8,384]{1,0:T(8,128)S(1)}, f32[8,384]{1,0:T(8,128)S(1)}, u32[]{:S(2)}, u32[]{:S(2)}) collective-permute-start(f32[8,384]{1,0:T(8,128)S(1)} %join_kernel.2.a_ref), channel_id=1, source_target_pairs={{0,2},{1,3},{2,0},{3,1},{4,6},{5,7},{6,4},{7,5},{8,10},{9,11},{10,... | collective-permute-start | bytes 36872 | tf_op jit(solution)/shard_map/ppermute | solution.py:216
  14.6 5.2 %collective-permute-start.2 = (f32[8,384]{1,0:T(8,128)S(1)}, f32[8,384]{1,0:T(8,128)S(1)}, u32[]{:S(2)}, u32[]{:S(2)}) collective-permute-start(f32[8,384]{1,0:T(8,128)S(1)} %join_kernel.3.after_ref.a_ref), channel_id=1, source_target_pairs={{0,4},{1,5},{2,6},{3,7},{4,0},{5,1},{6,2},{7,3},{8,12},{9,13},{10,... | collective-permute-start | bytes 36872 | tf_op jit(solution)/shard_map/ppermute | solution.py:216
  20.1 2.5 %collective-permute-start.3 = (f32[192,768]{1,0:T(8,128)S(1)}, f32[192,768]{1,0:T(8,128)S(1)}, u32[]{:S(2)}, u32[]{:S(2)}) collective-permute-start(f32[192,768]{1,0:T(8,128)S(1)} %get-tuple-element.46), channel_id=1, source_target_pairs={{0,1},{1,0},{2,3},{3,2},{4,5},{5,4},{6,7},{7,6},{8,9},{9,8},{10,11... | collective-permute-start | bytes 1769480 | tf_op jit(solution)/shard_map/ppermute | solution.py:216
  22.7 11.9 %collective-permute-start.4 = (f32[96,768]{1,0:T(8,128)S(1)}, f32[96,768]{1,0:T(8,128)S(1)}, u32[]{:S(2)}, u32[]{:S(2)}) collective-permute-start(f32[96,768]{1,0:T(8,128)S(1)} %get-tuple-element.49), channel_id=1, source_target_pairs={{0,2},{1,5},{2,0},{3,7},{4,6},{5,1},{6,4},{7,3},{8,10},{9,13},{10,... | collective-permute-start | bytes 884744 | tf_op jit(solution)/shard_map/ppermute | solution.py:269
  28.4 2.3 %collective-permute-start.5 = (f32[128,384]{1,0:T(8,128)S(1)}, f32[128,384]{1,0:T(8,128)S(1)}, u32[]{:S(2)}, u32[]{:S(2)}) collective-permute-start(f32[128,384]{1,0:T(8,128)S(1)} %get-tuple-element.52), channel_id=1, source_target_pairs={{0,1},{1,0},{2,3},{3,2},{4,5},{5,4},{6,7},{7,6},{8,9},{9,8},{10,11... | collective-permute-start | bytes 589832 | tf_op jit(solution)/shard_map/ppermute | solution.py:216
  29.6 1.4 %collective-permute-start.6 = (f32[128,384]{1,0:T(8,128)S(1)}, f32[128,384]{1,0:T(8,128)S(1)}, u32[]{:S(2)}, u32[]{:S(2)}) collective-permute-start(f32[128,384]{1,0:T(8,128)S(1)} %get-tuple-element.53), channel_id=1, source_target_pairs={{0,1},{1,0},{2,3},{3,2},{4,5},{5,4},{6,7},{7,6},{8,9},{9,8},{10,11... | collective-permute-start | bytes 589832 | tf_op jit(solution)/shard_map/ppermute | solution.py:216
  31.1 5.3 %collective-permute-start.8 = (f32[32,768]{1,0:T(8,128)S(1)}, f32[32,768]{1,0:T(8,128)S(1)}, u32[]{:S(2)}, u32[]{:S(2)}) collective-permute-start(f32[32,768]{1,0:T(8,128)S(1)} %get-tuple-element.57), channel_id=1, source_target_pairs={{0,8},{8,0},{16,24},{24,16},{1,9},{9,1},{17,25},{25,17},{2,10},{10... | collective-permute-start | bytes 294920 | tf_op jit(solution)/shard_map/ppermute | solution.py:216
  32.7 5.9 %collective-permute-start.9 = (f32[32,768]{1,0:T(8,128)S(1)}, f32[32,768]{1,0:T(8,128)S(1)}, u32[]{:S(2)}, u32[]{:S(2)}) collective-permute-start(f32[32,768]{1,0:T(8,128)S(1)} %get-tuple-element.58), channel_id=1, source_target_pairs={{0,16},{8,24},{16,0},{24,8},{1,17},{9,25},{17,1},{25,9},{2,18},{10... | collective-permute-start | bytes 294920 | tf_op jit(solution)/shard_map/ppermute | solution.py:216
  34.2 5.5 %collective-permute-start.10 = (f32[32,768]{1,0:T(8,128)S(1)}, f32[32,768]{1,0:T(8,128)S(1)}, u32[]{:S(2)}, u32[]{:S(2)}) collective-permute-start(f32[32,768]{1,0:T(8,128)S(1)} %get-tuple-element.59), channel_id=1, source_target_pairs={{0,24},{8,16},{16,8},{24,0},{1,25},{9,17},{17,9},{25,1},{2,26},{10... | collective-permute-start | bytes 294920 | tf_op jit(solution)/shard_map/ppermute | solution.py:216
  34.7 15.4 %collective-permute-start.7 = (f32[96,768]{1,0:T(8,128)S(1)}, f32[96,768]{1,0:T(8,128)S(1)}, u32[]{:S(2)}, u32[]{:S(2)}) collective-permute-start(f32[96,768]{1,0:T(8,128)S(1)} %get-tuple-element.56), channel_id=1, source_target_pairs={{0,4},{1,3},{2,6},{3,1},{4,0},{5,7},{6,2},{7,5},{8,12},{9,11},{10,... | collective-permute-start | bytes 884744 | tf_op jit(solution)/shard_map/ppermute | solution.py:269
  39.7 4.7 %collective-permute-start.11 = (f32[32,768]{1,0:T(8,128)S(1)}, f32[32,768]{1,0:T(8,128)S(1)}, u32[]{:S(2)}, u32[]{:S(2)}) collective-permute-start(f32[32,768]{1,0:T(8,128)S(1)} %book_sum.1.whole_ref), channel_id=1, source_target_pairs={{0,2},{1,5},{2,0},{3,7},{4,6},{5,1},{6,4},{7,3},{8,10},{9,13},{10,... | collective-permute-start | bytes 294920 | tf_op jit(solution)/shard_map/ppermute | solution.py:269
  44.4 5.7 %collective-permute-start.12 = (f32[32,768]{1,0:T(8,128)S(1)}, f32[32,768]{1,0:T(8,128)S(1)}, u32[]{:S(2)}, u32[]{:S(2)}) collective-permute-start(f32[32,768]{1,0:T(8,128)S(1)} %book_join.2.whole_ref), channel_id=1, source_target_pairs={{0,4},{1,3},{2,6},{3,1},{4,0},{5,7},{6,2},{7,5},{8,12},{9,11},{10,... | collective-permute-start | bytes 294920 | tf_op jit(solution)/shard_map/ppermute | solution.py:269
  50.2 10.4 %collective-permute-start.13 = (f32[96,768]{1,0:T(8,128)S(1)}, f32[96,768]{1,0:T(8,128)S(1)}, u32[]{:S(2)}, u32[]{:S(2)}) collective-permute-start(f32[96,768]{1,0:T(8,128)S(1)} %get-tuple-element.61), channel_id=1, source_target_pairs={{0,2},{1,5},{2,0},{3,7},{4,6},{5,1},{6,4},{7,3},{8,10},{9,13},{10,... | collective-permute-start | bytes 884744 | tf_op jit(solution)/shard_map/ppermute | solution.py:269
  52.8 6.4 %collective-permute-start.16 = (f32[32,768]{1,0:T(8,128)S(1)}, f32[32,768]{1,0:T(8,128)S(1)}, u32[]{:S(2)}, u32[]{:S(2)}) collective-permute-start(f32[32,768]{1,0:T(8,128)S(1)} %book_join.3.refs_1_.refs_0_), channel_id=1, source_target_pairs={{0,24},{8,16},{16,8},{24,0},{1,25},{9,17},{17,9},{25,1},{2,26},{10... | collective-permute-start | bytes 294920 | tf_op jit(solution)/shard_map/ppermute | solution.py:216
  55.1 5.0 %collective-permute-start.15 = (f32[32,768]{1,0:T(8,128)S(1)}, f32[32,768]{1,0:T(8,128)S(1)}, u32[]{:S(2)}, u32[]{:S(2)}) collective-permute-start(f32[32,768]{1,0:T(8,128)S(1)} %book_join.3.refs_1_.refs_0_), channel_id=1, source_target_pairs={{0,16},{8,24},{16,0},{24,8},{1,17},{9,25},{17,1},{25,9},{2,18},{10... | collective-permute-start | bytes 294920 | tf_op jit(solution)/shard_map/ppermute | solution.py:216
  56.0 4.6 %collective-permute-start.14 = (f32[32,768]{1,0:T(8,128)S(1)}, f32[32,768]{1,0:T(8,128)S(1)}, u32[]{:S(2)}, u32[]{:S(2)}) collective-permute-start(f32[32,768]{1,0:T(8,128)S(1)} %book_join.3.refs_1_.refs_0_), channel_id=1, source_target_pairs={{0,8},{8,0},{16,24},{24,16},{1,9},{9,1},{17,25},{25,17},{2,10},{10... | collective-permute-start | bytes 294920 | tf_op jit(solution)/shard_map/ppermute | solution.py:216
  60.7 2.6 %collective-permute-start.17 = (f32[192,768]{1,0:T(8,128)S(1)}, f32[192,768]{1,0:T(8,128)S(1)}, u32[]{:S(2)}, u32[]{:S(2)}) collective-permute-start(f32[192,768]{1,0:T(8,128)S(1)} %bitcast.15), channel_id=1, source_target_pairs={{0,1},{1,0},{2,3},{3,2},{4,5},{5,4},{6,7},{7,6},{8,9},{9,8},{10,11... | collective-permute-start | bytes 1769480 | tf_op jit(solution)/shard_map/ppermute | solution.py:216
  60.9 2.4 %collective-permute-start.18 = (f32[128,768]{1,0:T(8,128)S(1)}, f32[128,768]{1,0:T(8,128)S(1)}, u32[]{:S(2)}, u32[]{:S(2)}) collective-permute-start(f32[128,768]{1,0:T(8,128)S(1)} %bitcast.13), channel_id=1, source_target_pairs={{0,1},{1,0},{2,3},{3,2},{4,5},{5,4},{6,7},{7,6},{8,9},{9,8},{10,11... | collective-permute-start | bytes 1179656 | tf_op jit(solution)/shard_map/ppermute | solution.py:216
